TPU v7x, 32 devices: a whole 2x2x4 slice. The times are simulated.
32 devices in a mesh: dp: 8 (over y, x, core), blk: 4 (over z).
Axes of the slice: x: 2, y: 2, z: 4, core: 2. Of those that a mesh axis runs over, the one named last changes fastest.
Arguments:
- inputs: float32 [24576, 768], P(('dp', 'blk')), may hold values from -6 to 6
- positions: int32 [24576], P(('dp', 'blk')), may hold values from 0 to 1535
- segments: int32 [24576], P('dp'), may hold values from 0 to 24575, as said below
- gain_attn: float32 [768], replicated, may hold values from 0.1 to 1.9
- w_qkv: bfloat16 [768, 2304], replicated, may hold values from -0.21875 to 0.21875
- w_out: bfloat16 [768, 768], replicated, may hold values from -0.875 to 0.875
- gain_mlp: float32 [768], replicated, may hold values from 0.1 to 1.9
- w_up: bfloat16 [768, 3072], replicated, may hold values from -0.21875 to 0.21875
- b_up: float32 [3072], replicated, may hold values from -3 to 3
- w_down: bfloat16 [3072, 768], replicated, may hold values from -0.109375 to 0.109375
- cotangent: float32 [24576, 768], P(('dp', 'blk')), may hold values from -6 to 6
Outputs:
- outputs: float32 [24576, 768], P(('dp', 'blk'))
- input_grad: float32 [24576, 768], P(('dp', 'blk'))
- grad_gain_attn: float32 [768], replicated
- grad_qkv: float32 [768, 2304], replicated
- grad_out: float32 [768, 768], replicated
- grad_gain_mlp: float32 [768], replicated
- grad_up: float32 [768, 3072], replicated
- grad_bias_up: float32 [3072], replicated
- grad_down: float32 [3072, 768], replicated
Inputs may be any that keep to these rules, and one draw needn't show every extreme that they name: `segments`: ids never fall along the rows of one index of dp, and rows of different indices of dp have different ids; one clip of each index of dp covers rows of all its 4 devices along blk.
All inputs are finite; a program needn't handle non-finite values.
Results may differ from a plain program's by a relative error of at most 0.0095.
Values may be sent and summed in bfloat16 or wider, within the bound.
A program may use at most 256 MiB of HBM per device.

v0:
```python
import math

import jax
import jax.numpy as jnp
from jax import lax
from jax.sharding import PartitionSpec as P

HEADS = 12
HEAD = 64


eps_norm = 1e-06
mask_fill = -1000000000.0


def position_table(positions, model_width):
    half_width = model_width // 2
    freqs = jnp.exp(jnp.arange(half_width, dtype=jnp.float32) * (-math.log(10000.0) / half_width))
    angles = positions.astype(jnp.float32)[:, None] * freqs[None, :]
    return jnp.concatenate([jnp.sin(angles), jnp.cos(angles)], axis=1)


def normalize(values):
    center = values - jnp.mean(values, axis=-1, keepdims=True)
    inverse = lax.rsqrt(jnp.mean(center * center, axis=-1, keepdims=True) + eps_norm)
    return (center * inverse, inverse)


def norm_back(grad_norm, normed, inverse):
    first = jnp.mean(grad_norm, axis=-1, keepdims=True)
    second = jnp.mean(grad_norm * normed, axis=-1, keepdims=True)
    return inverse * (grad_norm - first - normed * second)


def left_dot(left, right):
    return lax.dot_general(
        left, right, (((0,), (0,)), ((), ())), preferred_element_type=jnp.float32
    )


def right_dot(left, right):
    return lax.dot_general(
        left, right, (((1,), (1,)), ((), ())), preferred_element_type=jnp.float32
    )


def head_columns(matrix, column, pair_width):
    piece = lax.dynamic_slice_in_dim(matrix, column, pair_width, 1)
    return piece.reshape(matrix.shape[0], 2, pair_width // 2)


def on_device(
    inputs, positions, segments, gain_attn, w_qkv, w_out, gain_mlp, w_up, b_up, w_down, cotangent
):
    row_count, model_width = inputs.shape
    pair_width = 2 * HEAD
    pair_count = HEADS // 2
    score_scale = HEAD ** (-0.5)
    place = lax.axis_index("blk")
    seg_query = lax.dynamic_slice_in_dim(segments, place * row_count, row_count)
    same_clip = (seg_query[:, None] == segments[None, :])[None]
    hidden = inputs + position_table(positions, model_width)
    normed_attn, inverse_attn = normalize(hidden)
    a_low = (normed_attn * gain_attn).astype(jnp.bfloat16)
    qkv = jnp.dot(a_low, w_qkv, preferred_element_type=jnp.float32).astype(jnp.bfloat16)
    queries = qkv[:, :model_width]
    kv_all = lax.all_gather(qkv[:, model_width:], "blk", axis=0, tiled=True)
    keys = kv_all[:, :model_width]
    values = kv_all[:, model_width:]
    group_rows = kv_all.shape[0]

    def pair_scores(query_pair, key_pair):
        scores = (
            jnp.einsum("qhd,khd->hqk", query_pair, key_pair, preferred_element_type=jnp.float32)
            * score_scale
        )
        return jnp.where(same_clip, scores, mask_fill)

    def forward_pair(index, carry):
        attended, log_totals = carry
        column = index * pair_width
        scores = pair_scores(
            head_columns(queries, column, pair_width), head_columns(keys, column, pair_width)
        )
        row_top = jnp.max(scores, axis=-1, keepdims=True)
        expd = jnp.exp(scores - row_top)
        row_total = jnp.sum(expd, axis=-1, keepdims=True)
        probs_low = (expd / row_total).astype(jnp.bfloat16)
        result = jnp.einsum(
            "hqk,khd->qhd",
            probs_low,
            head_columns(values, column, pair_width),
            preferred_element_type=jnp.float32,
        ).reshape(row_count, pair_width)
        attended = lax.dynamic_update_slice_in_dim(attended, result, column, 1)
        log_pair = (row_top + jnp.log(row_total))[:, :, 0].T
        log_totals = lax.dynamic_update_slice_in_dim(log_totals, log_pair, 2 * index, 1)
        return (attended, log_totals)

    attended, log_totals = lax.fori_loop(
        0,
        pair_count,
        forward_pair,
        (
            jnp.zeros((row_count, model_width), jnp.float32),
            jnp.zeros((row_count, HEADS), jnp.float32),
        ),
    )
    attn_low = attended.astype(jnp.bfloat16)
    resid = hidden + jnp.dot(attn_low, w_out, preferred_element_type=jnp.float32)
    normed_mlp, inverse_mlp = normalize(resid)
    b_low = (normed_mlp * gain_mlp).astype(jnp.bfloat16)
    pre_act = jnp.dot(b_low, w_up, preferred_element_type=jnp.float32) + b_up
    cumulative = 0.5 * (1.0 + lax.erf(pre_act * 0.7071067811865476))
    density = jnp.exp(-0.5 * pre_act * pre_act) * 0.3989422804014327
    z_low = (pre_act * cumulative).astype(jnp.bfloat16)
    outputs = resid + jnp.dot(z_low, w_down, preferred_element_type=jnp.float32)
    dy_low = cotangent.astype(jnp.bfloat16)
    grad_down = left_dot(z_low, dy_low)
    d_gelu = right_dot(dy_low, w_down)
    d_pre = (d_gelu * (cumulative + pre_act * density)).astype(jnp.bfloat16)
    grad_up = left_dot(b_low, d_pre)
    grad_bias_up = jnp.sum(d_pre.astype(jnp.float32), axis=0)
    d_normed = right_dot(d_pre, w_up)
    grad_gain_mlp = jnp.sum(d_normed * normed_mlp, axis=0)
    d_resid = cotangent + norm_back(d_normed * gain_mlp, normed_mlp, inverse_mlp)
    dr_low = d_resid.astype(jnp.bfloat16)
    grad_out = left_dot(attn_low, dr_low)
    d_attn = right_dot(dr_low, w_out).astype(jnp.bfloat16)

    def backward_pair(index, carry):
        d_query, d_kv = carry
        column = index * pair_width
        query_pair = head_columns(queries, column, pair_width)
        key_pair = head_columns(keys, column, pair_width)
        value_pair = head_columns(values, column, pair_width)
        grad_pair = head_columns(d_attn, column, pair_width)
        scores = pair_scores(query_pair, key_pair)
        log_pair = lax.dynamic_slice_in_dim(log_totals, 2 * index, 2, 1).T[:, :, None]
        probs = jnp.exp(scores - log_pair)
        d_probs = jnp.einsum(
            "qhd,khd->hqk", grad_pair, value_pair, preferred_element_type=jnp.float32
        )
        row_dot = jnp.sum(probs * d_probs, axis=-1, keepdims=True)
        d_scores = (probs * (d_probs - row_dot)).astype(jnp.bfloat16)
        probs_low = probs.astype(jnp.bfloat16)
        grad_q = (
            jnp.einsum("hqk,khd->qhd", d_scores, key_pair, preferred_element_type=jnp.float32)
            * score_scale
        )
        grad_k = (
            jnp.einsum("hqk,qhd->khd", d_scores, query_pair, preferred_element_type=jnp.float32)
            * score_scale
        )
        grad_v = jnp.einsum(
            "hqk,qhd->khd", probs_low, grad_pair, preferred_element_type=jnp.float32
        )
        d_query = lax.dynamic_update_slice_in_dim(
            d_query, grad_q.reshape(row_count, pair_width), column, 1
        )
        d_kv = lax.dynamic_update_slice_in_dim(
            d_kv, grad_k.reshape(group_rows, pair_width), column, 1
        )
        d_kv = lax.dynamic_update_slice_in_dim(
            d_kv, grad_v.reshape(group_rows, pair_width), model_width + column, 1
        )
        return (d_query, d_kv)

    d_query, d_kv = lax.fori_loop(
        0,
        pair_count,
        backward_pair,
        (
            jnp.zeros((row_count, model_width), jnp.float32),
            jnp.zeros((group_rows, 2 * model_width), jnp.float32),
        ),
    )
    d_kv_mine = lax.psum_scatter(d_kv, "blk", scatter_dimension=0, tiled=True)
    d_qkv = jnp.concatenate([d_query, d_kv_mine], axis=1).astype(jnp.bfloat16)
    grad_qkv = left_dot(a_low, d_qkv)
    d_normed_attn = right_dot(d_qkv, w_qkv)
    grad_gain_attn = jnp.sum(d_normed_attn * normed_attn, axis=0)
    input_grad = d_resid + norm_back(d_normed_attn * gain_attn, normed_attn, inverse_attn)
    small_terms = jnp.concatenate([grad_gain_attn, grad_gain_mlp, grad_bias_up])
    flat_qkv = grad_qkv.reshape(-1)
    flat_out = grad_out.reshape(-1)
    flat_up = grad_up.reshape(-1)
    flat_down = grad_down.reshape(-1)
    shares = (
        lax.psum_scatter(flat_qkv, ("dp", "blk"), scatter_dimension=0, tiled=True),
        lax.psum_scatter(flat_out, ("dp", "blk"), scatter_dimension=0, tiled=True),
        lax.psum_scatter(flat_up, ("dp", "blk"), scatter_dimension=0, tiled=True),
        lax.psum_scatter(flat_down, ("dp", "blk"), scatter_dimension=0, tiled=True),
        lax.psum_scatter(small_terms, ("dp", "blk"), scatter_dimension=0, tiled=True),
    )
    summed = (
        lax.all_gather(shares[0], ("dp", "blk"), axis=0, tiled=True),
        lax.all_gather(shares[1], ("dp", "blk"), axis=0, tiled=True),
        lax.all_gather(shares[2], ("dp", "blk"), axis=0, tiled=True),
        lax.all_gather(shares[3], ("dp", "blk"), axis=0, tiled=True),
        lax.all_gather(shares[4], ("dp", "blk"), axis=0, tiled=True),
    )
    sum_qkv, sum_out, sum_up, sum_down, sum_small = summed
    ff_width = w_up.shape[1]
    return (
        outputs,
        input_grad,
        sum_small[:model_width],
        sum_qkv.reshape(model_width, 3 * model_width),
        sum_out.reshape(model_width, model_width),
        sum_small[model_width : 2 * model_width],
        sum_up.reshape(model_width, ff_width),
        sum_small[2 * model_width :],
        sum_down.reshape(ff_width, model_width),
    )


def solution(mesh):
    placed = (
        P(("dp", "blk"), None),
        P(("dp", "blk")),
        P("dp"),
        P(),
        P(),
        P(),
        P(),
        P(),
        P(),
        P(),
        P(("dp", "blk"), None),
    )
    return jax.shard_map(
        on_device,
        mesh=mesh,
        in_specs=placed,
        out_specs=(
            P(("dp", "blk"), None),
            P(("dp", "blk"), None),
            P(),
            P(),
            P(),
            P(),
            P(),
            P(),
            P(),
        ),
        check_vma=False,
    )
```

profile of v0, /device:TPU:0, one launch (start us, length us, event | category | flops | bytes accessed | tf_op | source)
XLA Modules:
  0.0 2007.4 jit_solution(3378582563268198554)
XLA Ops:
  31.7 160.4 %all-gather.6.cloned.1.call-done = bf16[3072,1536]{1,0:T(8,128)(2,1)} async-done(((bf16[768,1536]{1,0:T(8,128)(2,1)}), bf16[3072,1536]{1,0:T(8,128)(2,1)}) %all-gather.6.cloned.1.call-update) | async-done | bytes 9437200 | tf_op jit(solution)/shard_map/all_gather | solution.py:67
  215.3 223.6 %while.34 = (s32[]{:T(128)}, bf16[768,768]{0,1:T(8,128)(2,1)}, f32[768,12]{0,1:T(8,128)}, bf16[3072,768]{0,1:T(8,128)(2,1)}, bf16[768,768]{0,1:T(8,128)(2,1)}, /...) while((s32[]{:T(128)}, bf16[768,768]{0,1:T(8,128)(2,1)}, ...), condition=%wide.region_5.6_spmd.clone, body=%wide.region_2.5_spmd.clone.sunk | while | flops 1266940416 | bytes 147545408 | solution.py:100
  482.1 438.9 %while.35 = (s32[]{:T(128)}, bf16[768,768]{0,1:T(8,128)(2,1)}, f32[3072,1536]{0,1:T(8,128)}, bf16[3072,768]{0,1:T(8,128)(2,1)}, bf16[768,768]{0,1:T(8,128)(2,1)}...) while((s32[]{:T(128)}, bf16[768,768]{0,1:T(8,128)(2,1)}, ...), condition=%wide.region_12.13_spmd.clone, body=%wide.region_10.0_spmd.clone.sunk | while | flops 3093625344 | bytes 196077136 | solution.py:169
  501.3 17.1 multiply_reduce_fusion.10
  518.4 14.2 multiply_convert_fusion.9
  574.4 17.1 multiply_reduce_fusion.10
  591.5 14.2 multiply_convert_fusion.9
  647.5 17.1 multiply_reduce_fusion.10
  664.6 14.2 multiply_convert_fusion.9
  720.6 17.1 multiply_reduce_fusion.10
  737.7 14.2 multiply_convert_fusion.9
  793.7 17.1 multiply_reduce_fusion.10
  810.8 14.2 multiply_convert_fusion.9
  866.8 17.1 multiply_reduce_fusion.10
  883.9 14.2 multiply_convert_fusion.9
  961.1 272.1 %reduce-scatter.2.cloned.1.call-done = f32[768,1536]{0,1:T(8,128)} async-done(((f32[3072,1536]{0,1:T(8,128)}), f32[768,1536]{0,1:T(8,128)}) %reduce-scatter.2.cloned.1.call-update) | async-done | bytes 4718608 | tf_op jit(solution)/shard_map/reduce_scatter | solution.py:178
  1251.9 433.4 %all-reduce.9.cloned.1.call-done = (f32[1769472]{0:T(1024)}, f32[589824]{0:T(1024)}, f32[2359296]{0:T(1024)}, f32[2359296]{0:T(1024)}) async-done(((f32[1769472]{0:T(1024)}, f32[589824]{0:T(1024)}, f32[2359296]{0:T(1024)}, f32[2359296]{0:T(1024)}), (f32[1769472]{0:T(1024)}, f32[589824]{0:T(1024)}, f32[2359296]{0:T(1024)}, f32[2359296]{0:T(1024)})) %all-reduce.9.cloned.1.call-update) | async-done | bytes 28311568
  1718.4 41.0 %all-reduce.1 = f32[4608]{0:T(1024)} all-reduce(f32[4608]{0:T(1024)} %pad_maximum_fusion.3), channel_id=3, replica_groups=mesh['dp'=8,'blk'=4] {'dp','blk'}, use_global_device_ids=true, to_apply=%region_19.20.clone | all-reduce | flops 4608 | bytes 36864
  1761.5 41.0 %all-reduce = f32[4608]{0:T(1024)} all-reduce(f32[4608]{0:T(1024)} %dynamic-slice_dynamic-update-slice_fusion), channel_id=1, replica_groups=mesh['dp'=8,'blk'=4] {'dp','blk'}, use_global_device_ids=true, to_apply=%add | all-reduce | flops 4608 | bytes 36864
  1808.6 13.1 all-gather.8.cloned.1.call-done
  1829.9 75.6 %all-gather.12.cloned.1.call-done = f32[2359296]{0:T(1024)} async-done(((f32[73728]{0:T(1024)}), f32[2359296]{0:T(1024)}) %all-gather.12.cloned.1.call-update) | async-done | bytes 9437200 | tf_op jit(solution)/shard_map/all_gather | solution.py:199
  1905.4 10.9 reshape.245
  1916.3 72.6 %all-gather.14.cloned.1.call-done = f32[2359296]{0:T(1024)} async-done(((f32[73728]{0:T(1024)}), f32[2359296]{0:T(1024)}) %all-gather.14.cloned.1.call-update) | async-done | bytes 9437200 | tf_op jit(solution)/shard_map/all_gather | solution.py:200
  1988.9 11.3 reshape.247
  (374 shorter events, 672.7 us)
Async XLA Ops:
  7.2 185.0 %all-gather.6.cloned.1.call-start = ((), (), s32[]{:S(2)}) async-start(), calls=%async_computation.1 | async-start | bytes 11796480 | tf_op jit(solution)/shard_map/all_gather | solution.py:67
  22.6 1210.6 %reduce-scatter.2.cloned.1.call-start = ((), (), s32[]{:S(2)}) async-start(), calls=%async_computation.2 | async-start | bytes 23592960 | tf_op jit(solution)/shard_map/reduce_scatter | solution.py:178
  442.6 26.0 %copy-start.8 = (f32[768,768]{0,1:T(8,128)}, f32[768,768]{0,1:T(8,128)S(1)}, u32[]{:S(2)}) copy-start(f32[768,768]{0,1:T(8,128)S(1)} %get-tuple-element.520) | copy-start | bytes 7077892
  442.7 26.0 %copy-start.24 = (f32[768]{0:T(1024)}, f32[768]{0:T(1024)S(1)}, u32[]{:S(2)}) copy-start(f32[768]{0:T(1024)S(1)} %broadcast_multiply_fusion.4) | copy-start | bytes 9220
  443.4 25.2 %copy-start.26 = (f32[768]{0:T(1024)}, f32[768]{0:T(1024)S(1)}, u32[]{:S(2)}) copy-start(f32[768]{0:T(1024)S(1)} %add_rsqrt_fusion) | copy-start | bytes 9220
  501.3 17.1 copy-start.1
  518.4 14.2 copy-start.5
  574.4 17.1 copy-start.1
  591.5 14.2 copy-start.5
  647.5 17.1 copy-start.1
  664.6 14.2 copy-start.5
  720.6 17.1 copy-start.1
  737.7 14.2 copy-start.5
  793.7 17.1 copy-start.1
  810.8 14.2 copy-start.5
  866.8 17.1 copy-start.1
  921.0 764.2 %all-reduce.9.cloned.1.call-start = ((), (), s32[]{:S(2)}) async-start(), calls=%async_computation.7 | async-start | bytes 56623104
  961.1 276.3 %copy-start.31 = (f32[768]{0:T(1024)S(1)}, f32[768]{0:T(1024)}, u32[]{:S(2)}) copy-start(f32[768]{0:T(1024)} %copy-done.30) | copy-start | bytes 9220
  961.1 276.3 %copy-start.33 = (f32[768]{0:T(1024)S(1)}, f32[768]{0:T(1024)}, u32[]{:S(2)}) copy-start(f32[768]{0:T(1024)} %copy-done.32) | copy-start | bytes 9220
  961.1 276.3 %copy-start.36 = (f32[768]{0:T(1024)S(1)}, f32[768]{0:T(1024)}, u32[]{:S(2)}) copy-start(f32[768]{0:T(1024)} %param.18) | copy-start | bytes 9220
  1251.9 553.3 %all-gather.10.cloned.1.call-start = ((), (), s32[]{:S(2)}) async-start(), calls=%async_computation.4 | async-start | bytes 2433024 | tf_op jit(solution)/shard_map/all_gather | solution.py:198
  1686.8 134.8 %all-gather.8.cloned.1.call-start = ((), (), s32[]{:S(2)}) async-start(), calls=%async_computation.3 | async-start | bytes 7299072 | tf_op jit(solution)/shard_map/all_gather | solution.py:197
  1688.5 216.9 %all-gather.12.cloned.1.call-start = ((), (), s32[]{:S(2)}) async-start(), calls=%async_computation.5 | async-start | bytes 9732096 | tf_op jit(solution)/shard_map/all_gather | solution.py:199
  1690.3 298.6 %all-gather.14.cloned.1.call-start = ((), (), s32[]{:S(2)}) async-start(), calls=%async_computation.6 | async-start | bytes 9732096 | tf_op jit(solution)/shard_map/all_gather | solution.py:200
  (70 other events, 356.9 us)
Sparse Core Ops, SparseCore 0:
  22.7 169.4 all-gather.5
  921.2 311.9 reduce-scatter.1
  1252.0 433.2 all-reduce.8
  1688.5 57.4 all-gather.9
  1749.3 72.3 all-gather.7
  1824.9 80.4 all-gather.11
  1908.2 80.6 all-gather.13
where the time goes:
time: 2020 us; the launch traced here: 2010 us
  waiting for transfers between devices  1030 us (51%)
  matrix products  425 us (21%)
  local copies, waits for them, and re-layouts  272 us (13%)
  other arithmetic  185 us (9%)
  blocking collectives  82 us (4%)
    unnamed x8, waiting for transfers between devices  433 us
    reduce_scatter x1, waiting for transfers between devices, on_device(): d_kv_mine = lax.psum_scatter(d_kv, 'blk', scatter_dimension=0, tiled=True)  272 us
    all_gather x1, waiting for transfers between devices, on_device(): kv_all = lax.all_gather(qkv[:, model_width:], 'blk', axis=0, tiled=True)  160 us
    dot_general x6, matrix products, backward_pair(): jnp.einsum('qhd,khd->hqk', grad_pair, value_pair, preferred_element_type=...  103 us
    dot_general x12, matrix products, pair_scores(): jnp.einsum('qhd,khd->hqk', query_pair, key_pair, preferred_element_type=j...  86.4 us
    convert_element_type x6, other arithmetic, backward_pair(): d_scores = (probs * (d_probs - row_dot)).astype(jnp.bfloat16)  85 us
    unnamed x2, blocking collectives  82 us
    all_gather x1, waiting for transfers between devices, on_device(): lax.all_gather(shares[2], ('dp', 'blk'), axis=0, tiled=True)  75.6 us
  transfers between devices with their start and end apart: 7, of which 6 were waited for; matrix products, arithmetic and copies ran while one was open for 5% of the time, Pallas kernels for 0%

commit v1 on v0

v1 whole, which is shorter than its diff:
```python
import functools
import math

import jax
import jax.numpy as jnp
from jax import lax
from jax.experimental import pallas as pl
from jax.experimental.pallas import tpu as pltpu
from jax.sharding import PartitionSpec as P

HEADS = 12
HEAD = 64
PAIR = 2 * HEAD
SCALE = HEAD**-0.5
LOG2E = 1.4426950408889634
MASKED = -1.0e9
QUERY_BLOCK = 384
EPS_NORM = 1e-06
LOW = jnp.bfloat16
WIDE = jnp.float32

NN = (((1,), (0,)), ((), ()))
NT = (((1,), (1,)), ((), ()))
TN = (((0,), (0,)), ((), ()))


def dot(left, right, dims):
    return lax.dot_general(left, right, dims, preferred_element_type=WIDE)


def position_table(positions, model_width):
    half_width = model_width // 2
    freqs = jnp.exp(jnp.arange(half_width, dtype=WIDE) * (-math.log(10000.0) / half_width))
    angles = positions.astype(WIDE)[:, None] * freqs[None, :]
    return jnp.concatenate([jnp.sin(angles), jnp.cos(angles)], axis=1)


def normalize(values):
    center = values - jnp.mean(values, axis=-1, keepdims=True)
    inverse = lax.rsqrt(jnp.mean(center * center, axis=-1, keepdims=True) + EPS_NORM)
    return center * inverse, inverse


def norm_back(grad_norm, normed, inverse):
    first = jnp.mean(grad_norm, axis=-1, keepdims=True)
    second = jnp.mean(grad_norm * normed, axis=-1, keepdims=True)
    return inverse * (grad_norm - first - normed * second)


def in_head(values, head):
    lanes = lax.broadcasted_iota(jnp.int32, values.shape, 1)
    return (lanes < HEAD) == (head == 0)


def only_head(values, head, other=None):
    other = jnp.zeros_like(values) if other is None else other
    return jnp.where(in_head(values, head), values, other)


def split_scaled(query):
    scaled = query.astype(WIDE) * (SCALE * LOG2E)
    high = scaled.astype(LOW)
    return high, (scaled - high.astype(WIDE)).astype(LOW)


def extra_columns(own, key_keep, query_keep, rows):
    if own:
        zeros = jnp.zeros((rows, PAIR), LOW)
        return zeros, zeros
    lanes = lax.broadcasted_iota(jnp.int32, (rows, PAIR), 1) % HEAD
    key_fill = jnp.where(key_keep == 0, MASKED, 0.0)
    query_fill = jnp.where(query_keep == 0, MASKED, 0.0)
    one, zero = jnp.ones((rows, PAIR), WIDE), jnp.zeros((rows, PAIR), WIDE)
    key_extra = jnp.where(lanes == 0, key_fill, jnp.where(lanes == 1, one, zero))
    query_extra = jnp.where(lanes == 0, one, jnp.where(lanes == 1, query_fill, zero))
    return key_extra.astype(LOW), query_extra.astype(LOW)


def score_sides(key, query, key_extra, query_extra):
    high, low = split_scaled(query)
    key_side = [
        jnp.concatenate([only_head(key, head, key_extra), only_head(key, head)], axis=1)
        for head in range(2)
    ]
    query_side = [
        jnp.concatenate([only_head(high, head, query_extra), only_head(low, head)], axis=1)
        for head in range(2)
    ]
    return key_side, query_side


def work_items(rows):
    return [(start, head) for start in range(0, rows, QUERY_BLOCK) for head in range(2)]


def forward_kernel(own, last, *refs):
    a_ref, w_ref, q_ref, key_mark, query_mark = refs[:5]
    refs = refs[5:]
    if not own:
        acc_in, top_in, total_in = refs[:3]
        refs = refs[3:]
    kv_ref, acc_ref, top_ref, total_ref = refs[:4]
    refs = refs[4:]
    if last:
        attn_ref = refs[0]
    rows = q_ref.shape[0]
    kv = dot(a_ref[...], w_ref[...], NN).astype(LOW)
    kv_ref[...] = kv
    key, value = kv[:, :PAIR], kv[:, PAIR:]
    value_t = value.T
    ones = jnp.ones((16, rows), LOW)
    value_rows = [
        jnp.concatenate([value_t[head * HEAD : (head + 1) * HEAD], ones], axis=0) for head in range(2)
    ]
    marks = (None, None) if own else (key_mark[...], query_mark[...])
    key_extra, query_extra = extra_columns(own, *marks, rows)
    key_side, query_side = score_sides(key, q_ref[...], key_extra, query_extra)

    def scores(start, head):
        stop = start + QUERY_BLOCK
        result = dot(key_side[head], query_side[head][start:stop], NT)
        if own:
            result = jnp.where(key_mark[...] == query_mark[:, start:stop], result, MASKED)
        return result

    def weights(start, head, result):
        stop = start + QUERY_BLOCK
        top = jnp.max(result, axis=0, keepdims=True)
        if not own:
            top = jnp.maximum(top, top_in[head : head + 1, start:stop])
        return jnp.exp2(result - top).astype(LOW), top

    def attend(start, head, expd, top):
        stop = start + QUERY_BLOCK
        lanes, row = slice(head * HEAD, (head + 1) * HEAD), slice(head, head + 1)
        result = dot(value_rows[head], expd, NN)
        acc, total = result[:HEAD], result[HEAD : HEAD + 1]
        if not own:
            shrink = jnp.exp2(top_in[row, start:stop] - top)
            acc = acc_in[lanes, start:stop] * shrink + acc
            total = total_in[row, start:stop] * shrink + total
        if last:
            acc = acc * (1.0 / total)
            top = top + jnp.log(total) * LOG2E
        acc_ref[lanes, start:stop] = acc
        top_ref[row, start:stop] = top
        total_ref[row, start:stop] = total

    items = work_items(rows)
    result = scores(*items[0])
    before = None
    for index, item in enumerate(items):
        following = scores(*items[index + 1]) if index + 1 < len(items) else None
        done = weights(*item, result)
        if before is not None:
            attend(*before)
        before = (*item, *done)
        result = following
    attend(*before)
    if last:
        attn_ref[...] = acc_ref[...].T.astype(LOW)


def forward_call(own, last, a_shard, w_kv, query, key_mark, query_mark, state):
    rows, width = query.shape
    pairs = width // PAIR
    whole = lambda shape: pl.BlockSpec(shape, lambda pair: (0,) * len(shape))
    columns = pl.BlockSpec((rows, PAIR), lambda pair: (0, pair))
    across = pl.BlockSpec((PAIR, rows), lambda pair: (pair, 0))
    line = pl.BlockSpec((None, 2, rows), lambda pair: (pair, 0, 0))
    state_specs = [across, line, line]
    state_shapes = [
        jax.ShapeDtypeStruct((width, rows), WIDE),
        jax.ShapeDtypeStruct((pairs, 2, rows), WIDE),
        jax.ShapeDtypeStruct((pairs, 2, rows), WIDE),
    ]
    in_specs = [
        whole((rows, width)),
        pl.BlockSpec((width, 2 * PAIR), lambda pair: (0, pair)),
        columns,
        whole(key_mark.shape),
        whole(query_mark.shape),
    ]
    operands = [a_shard, w_kv, query, key_mark, query_mark]
    if not own:
        in_specs += state_specs
        operands += list(state)
    out_specs = [pl.BlockSpec((rows, 2 * PAIR), lambda pair: (0, pair)), *state_specs]
    out_shape = [jax.ShapeDtypeStruct((rows, 2 * width), LOW), *state_shapes]
    if last:
        out_specs.append(columns)
        out_shape.append(jax.ShapeDtypeStruct((rows, width), LOW))
    return pl.pallas_call(
        functools.partial(forward_kernel, own, last),
        grid=(pairs,),
        in_specs=in_specs,
        out_specs=out_specs,
        out_shape=out_shape,
        name="attend_own" if own else "attend_shard",
        cost_estimate=pl.CostEstimate(
            flops=14 * rows * rows * width, bytes_accessed=24 * rows * width, transcendentals=0
        ),
        compiler_params=pltpu.CompilerParams(vmem_limit_bytes=48 * 2**20),
    )(*operands)


def backward_kernel(own, first, *refs):
    kv_ref, q_ref, da_ref, lse_ref, attn_ref, key_mark, query_mark = refs[:7]
    refs = refs[7:]
    if not first:
        dq_in = refs[0]
        refs = refs[1:]
    dkv_ref, dq_ref, dk_sum, dv_sum = refs
    rows = q_ref.shape[0]
    key, value = kv_ref[:, :PAIR], kv_ref[:, PAIR:]
    query, grad = q_ref[...], da_ref[...]
    key_t, query_t, grad_t = key.T, query.T, grad.T
    marks = (None, None) if own else (key_mark[...], query_mark[...])
    key_extra, query_extra = extra_columns(own, *marks, rows)
    key_side, query_side = score_sides(key, query, key_extra, query_extra)
    grad_side = [only_head(grad, head) for head in range(2)]
    product = grad_t.astype(WIDE) * attn_ref[...]
    row_dots = [
        jnp.sum(product[head * HEAD : (head + 1) * HEAD], axis=0, keepdims=True) for head in range(2)
    ]
    dq_all = []
    for start, head in work_items(rows):
        stop = start + QUERY_BLOCK
        lanes, row = slice(head * HEAD, (head + 1) * HEAD), slice(head, head + 1)
        score = dot(key_side[head], query_side[head][start:stop], NT)
        if own:
            score = jnp.where(key_mark[...] == query_mark[:, start:stop], score, MASKED)
        probs = jnp.exp2(score - lse_ref[row, start:stop])
        d_probs = dot(value, grad_side[head][start:stop], NT)
        d_scores = (probs * (d_probs - row_dots[head][:, start:stop])).astype(LOW)
        probs = probs.astype(LOW)
        dv = dot(grad_t[lanes, start:stop], probs, NT)
        dk = dot(query_t[lanes, start:stop], d_scores, NT)
        dq = dot(key_t[lanes], d_scores, NN)
        if start == 0:
            dv_sum[lanes], dk_sum[lanes] = dv, dk
        else:
            dv_sum[lanes] += dv
            dk_sum[lanes] += dk
        if not first:
            dq = dq + dq_in[lanes, start:stop]
        if own:
            dq_all.append((start, head, dq))
        else:
            dq_ref[lanes, start:stop] = dq
    if own:
        for start in range(0, rows, QUERY_BLOCK):
            both = jnp.concatenate([dq for at, head, dq in dq_all if at == start], axis=0)
            dq_ref[start : start + QUERY_BLOCK] = (both * SCALE).T.astype(LOW)
    dkv_ref[:, :PAIR] = (dk_sum[...] * SCALE).T.astype(LOW)
    dkv_ref[:, PAIR:] = dv_sum[...].T.astype(LOW)


def backward_call(own, first, kv, query, d_attn, lse, attended, key_mark, query_mark, dq):
    rows, width = query.shape
    pairs = width // PAIR
    whole = lambda shape: pl.BlockSpec(shape, lambda pair: (0,) * len(shape))
    columns = pl.BlockSpec((rows, PAIR), lambda pair: (0, pair))
    across = pl.BlockSpec((PAIR, rows), lambda pair: (pair, 0))
    line = pl.BlockSpec((None, 2, rows), lambda pair: (pair, 0, 0))
    double = pl.BlockSpec((rows, 2 * PAIR), lambda pair: (0, pair))
    in_specs = [double, columns, columns, line, across, whole(key_mark.shape), whole(query_mark.shape)]
    operands = [kv, query, d_attn, lse, attended, key_mark, query_mark]
    if not first:
        in_specs.append(across)
        operands.append(dq)
    dq_shape = jax.ShapeDtypeStruct((rows, width), LOW) if own else jax.ShapeDtypeStruct((width, rows), WIDE)
    return pl.pallas_call(
        functools.partial(backward_kernel, own, first),
        grid=(pairs,),
        in_specs=in_specs,
        out_specs=[double, columns if own else across],
        out_shape=[jax.ShapeDtypeStruct((rows, 2 * width), LOW), dq_shape],
        scratch_shapes=[pltpu.VMEM((PAIR, rows), WIDE), pltpu.VMEM((PAIR, rows), WIDE)],
        name="back_own" if own else "back_shard",
        cost_estimate=pl.CostEstimate(
            flops=26 * rows * rows * width, bytes_accessed=24 * rows * width, transcendentals=0
        ),
        compiler_params=pltpu.CompilerParams(vmem_limit_bytes=48 * 2**20),
    )(*operands)


def on_device(
    inputs, positions, segments, gain_attn, w_qkv, w_out, gain_mlp, w_up, b_up, w_down, cotangent
):
    rows, width = inputs.shape
    pairs = width // PAIR
    place = lax.axis_index("blk")
    w_query = w_qkv[:, :width]
    w_kv = (
        w_qkv[:, width:].reshape(width, 2, pairs, PAIR).swapaxes(1, 2).reshape(width, 2 * width)
    )

    def send(value, pairs_of_places):
        return lax.ppermute(value, "blk", pairs_of_places)

    hidden = inputs + position_table(positions, width)
    normed_attn, inverse_attn = normalize(hidden)
    a_low = (normed_attn * gain_attn).astype(LOW)

    near = [(0, 1), (1, 0), (2, 3), (3, 2)]
    middle = [(1, 2), (2, 1)]
    outward = [(1, 0), (2, 3)]
    inward = [(0, 1), (3, 2)]
    table = jnp.array([[0, 1, 2, 3], [1, 0, 2, 3], [2, 3, 1, 0], [3, 2, 1, 0]], jnp.int32)
    shard_1 = send(a_low, near)
    shard_2_middle = send(a_low, middle)
    shard_2 = shard_2_middle + send(shard_2_middle, outward)
    shard_3_middle = send(shard_1, middle)
    shard_3 = shard_3_middle + send(shard_3_middle, outward)
    shards = [a_low, shard_1, shard_2, shard_3]

    seg_query = lax.dynamic_slice_in_dim(segments, place * rows, rows)
    marks = [(seg_query[:, None], seg_query[None, :])]
    for index in range(1, 4):
        other = lax.dynamic_index_in_dim(table[:, index], place, keepdims=False)
        seg_key = lax.dynamic_slice_in_dim(segments, other * rows, rows)
        later_first = jnp.where(other > place, seg_key[0], seg_query[0])
        earlier_last = jnp.where(other > place, seg_query[-1], seg_key[-1])
        clip = jnp.where(later_first == earlier_last, later_first, -1)
        marks.append(
            ((seg_key == clip).astype(jnp.int32)[:, None], (seg_query == clip).astype(jnp.int32)[:, None])
        )

    query = dot(a_low, w_query, NN).astype(LOW)
    kvs, state = [], None
    for index in range(4):
        kv, *state = forward_call(
            index == 0, index == 3, shards[index], w_kv, query, *marks[index], state
        )
        kvs.append(kv)
    attended, lse, _, attn_low = state

    resid = hidden + dot(attn_low, w_out, NN)
    normed_mlp, inverse_mlp = normalize(resid)
    b_low = (normed_mlp * gain_mlp).astype(LOW)
    pre_act = dot(b_low, w_up, NN) + b_up
    cumulative = 0.5 * (1.0 + lax.erf(pre_act * 0.7071067811865476))
    density = jnp.exp(-0.5 * pre_act * pre_act) * 0.3989422804014327
    z_low = (pre_act * cumulative).astype(LOW)
    outputs = resid + dot(z_low, w_down, NN)
    dy_low = cotangent.astype(LOW)
    grad_down = dot(z_low, dy_low, TN)
    d_gelu = dot(dy_low, w_down, NT)
    d_pre = (d_gelu * (cumulative + pre_act * density)).astype(LOW)
    grad_up = dot(b_low, d_pre, TN)
    grad_bias_up = jnp.sum(d_pre.astype(WIDE), axis=0)
    d_normed = dot(d_pre, w_up, NT)
    grad_gain_mlp = jnp.sum(d_normed * normed_mlp, axis=0)
    d_resid = cotangent + norm_back(d_normed * gain_mlp, normed_mlp, inverse_mlp)
    dr_low = d_resid.astype(LOW)
    grad_out = dot(attn_low, dr_low, TN)
    d_attn = dot(dr_low, w_out, NT).astype(LOW)

    everywhere = ("dp", "blk")
    sum_down, sum_up, sum_out = lax.psum(
        (grad_down.astype(LOW), grad_up.astype(LOW), grad_out.astype(LOW)), everywhere
    )

    dq = None
    parts, grad_kv = [None] * 4, 0.0
    for index in (3, 2, 1, 0):
        dkv, dq = backward_call(
            index == 0, index == 3, kvs[index], query, d_attn, lse, attended, *marks[index], dq
        )
        parts[index] = dot(dkv, w_kv, NT)
        grad_kv = grad_kv + dot(shards[index], dkv, TN)
    far = send(parts[3].astype(LOW), inward)
    mid_3 = send((parts[3] + far.astype(WIDE)).astype(LOW), middle)
    mid_2 = send(parts[2].astype(LOW), inward)
    last_1 = send((parts[2] + mid_2.astype(WIDE)).astype(LOW), middle)
    last_2 = send((parts[1] + mid_3.astype(WIDE)).astype(LOW), outward)
    last_3 = send(parts[1].astype(LOW), inward)
    d_normed_attn = (
        parts[0]
        + dot(dq, w_query, NT)
        + last_1.astype(WIDE)
        + last_2.astype(WIDE)
        + last_3.astype(WIDE)
    )
    grad_query = dot(a_low, dq, TN)
    grad_gain_attn = jnp.sum(d_normed_attn * normed_attn, axis=0)
    input_grad = d_resid + norm_back(d_normed_attn * gain_attn, normed_attn, inverse_attn)
    grad_kv = (
        grad_kv.astype(LOW).reshape(width, pairs, 2, PAIR).swapaxes(1, 2).reshape(width, 2 * width)
    )
    grad_qkv = jnp.concatenate([grad_query.astype(LOW), grad_kv], axis=1)
    small = jnp.concatenate([grad_gain_attn, grad_gain_mlp, grad_bias_up])
    sum_qkv, sum_small = lax.psum((grad_qkv, small), everywhere)
    return (
        outputs,
        input_grad,
        sum_small[:width],
        sum_qkv.astype(WIDE),
        sum_out.astype(WIDE),
        sum_small[width : 2 * width],
        sum_up.astype(WIDE),
        sum_small[2 * width :],
        sum_down.astype(WIDE),
    )


def solution(mesh):
    rows = P(("dp", "blk"), None)
    placed = (rows, P(("dp", "blk")), P("dp"), P(), P(), P(), P(), P(), P(), P(), rows)
    return jax.shard_map(
        on_device,
        mesh=mesh,
        in_specs=placed,
        out_specs=(rows, rows, P(), P(), P(), P(), P(), P(), P()),
        check_vma=False,
    )
```

time: 2020 us -> 670 us (0.33)
  waiting for transfers between devices: 1030 us -> 232 us
  matrix products: 425 us -> 75.5 us
  local copies, waits for them, and re-layouts: 272 us -> 57.5 us
  Pallas kernels: 0 us -> 159 us
  other arithmetic: 185 us -> 39 us
  blocking collectives: 82 us -> 43 us
  starting transfers between devices: 0.54 us -> 26.8 us
    unnamed x8 -> x1, waiting for transfers between devices: 433 us -> 0.02 us
    dot_general x54 -> x20, matrix products: 425 us -> 75.5 us  [dot(): return lax.dot_general(left, right, dims, preferred_element_type=WIDE)]
    all_gather x5 -> x0, waiting for transfers between devices: 322 us -> none  [the longest x1 160 us: on_device(): kv_all = lax.all_gather(qkv[:, model_width:], 'blk', axis=0, tiled=True)]
    reduce_scatter x1 -> x0, waiting for transfers between devices: 272 us -> none  [on_device(): d_kv_mine = lax.psum_scatter(d_kv, 'blk', scatter_dimension=0, tiled=True)]
    pallas_call x0 -> x8, Pallas kernels: none -> 159 us  [the longest x4 93.8 us: backward_call(): pl.pallas_call(functools.partial(backward_kernel, own, first), grid=(pair...]
    ppermute x0 -> x11, waiting for transfers between devices: none -> 132 us  [send(): return lax.ppermute(value, 'blk', pairs_of_places)]
    psum x0 -> x1, waiting for transfers between devices: none -> 100 us  [on_device(): sum_qkv, sum_small = lax.psum((grad_qkv, small), everywhere)]
    unnamed x2 -> x0, blocking collectives: 82 us -> none
  transfers between devices with their start and end apart: 7 -> 12, of which waited for: 6 -> 5; matrix products, arithmetic and copies ran while one was open for 5% -> 10% of each run, Pallas kernels for 0% -> 7%
where the time goes in v1:
time: 670 us; the launch traced here: 660 us
  waiting for transfers between devices  232 us (35%)
  Pallas kernels  159 us (24%)
  matrix products  75.5 us (11%)
  local copies, waits for them, and re-layouts  57.5 us (9%)
  blocking collectives  43 us (6%)
  other arithmetic  39 us (6%)
  between operations  27.1 us (4%)
  starting transfers between devices  26.8 us (4%)
    ppermute x11, waiting for transfers between devices, send(): return lax.ppermute(value, 'blk', pairs_of_places)  132 us
    psum x1, waiting for transfers between devices, on_device(): sum_qkv, sum_small = lax.psum((grad_qkv, small), everywhere)  100 us
    pallas_call x4, Pallas kernels, backward_call(): pl.pallas_call(functools.partial(backward_kernel, own, first), grid=(pair...  93.8 us
    dot_general x20, matrix products, dot(): return lax.dot_general(left, right, dims, preferred_element_type=WIDE)  75.5 us
    pallas_call x4, Pallas kernels, forward_call(): pl.pallas_call(functools.partial(forward_kernel, own, last), grid=(pairs,...  65 us
    psum x1, blocking collectives, on_device(): sum_qkv, sum_small = lax.psum((grad_qkv, small), everywhere)  43 us
    ppermute x11, starting transfers between devices, send(): return lax.ppermute(value, 'blk', pairs_of_places)  26.8 us
    unnamed x128, local copies, waits for them, and re-layouts  19.6 us
  transfers between devices with their start and end apart: 12, of which 5 were waited for; matrix products, arithmetic and copies ran while one was open for 10% of the time, Pallas kernels for 7%

profile of v1, /device:TPU:0, one launch (start us, length us, event | category | flops | bytes accessed | tf_op | source)
XLA Modules:
  0.0 659.7 jit_solution(8612015776496577297)
XLA Ops:
  36.6 6.9 %collective-permute-done.refs_0_ = bf16[768,768]{1,0:T(8,128)(2,1)S(1)} collective-permute-done((bf16[768,768]{1,0:T(8,128)(2,1)S(1)}, bf16[768,768]{1,0:T(8,128)(2,1)S(1)}, u32[]{:S(2)}, u32[]{:S(2)}) %collective-permute-start) | collective-permute-done | bytes 1179680 | tf_op jit(solution)/shard_map/ppermute | solution.py:300
  59.2 6.8 %copy.30 = bf16[768,6,2,128]{3,2,1,0:T(2,128)(2,1)} copy(bf16[768,6,2,128]{0,3,1,2:T(8,128)(2,1)} %bitcast.50) | data formatting | bytes 4718592 | tf_op jit(solution)/shard_map/transpose | solution.py:296
  66.0 6.3 reshape.86.refs_1_
  76.2 16.0 %attend_own.1 = (bf16[768,1536]{1,0:T(8,128)(2,1)S(1)}, f32[768,768]{1,0:T(8,128)}, f32[6,2,768]{2,1,0:T(2,128)S(1)}, f32[6,2,768]{2,1,0:T(2,128)S(1)}) custom-call(bf16[768,768]{1,0:T(8,128)(2,1)S(1)} %multiply_convert_fusion.2.refs_0_, bf16[768,1536]{1,0:T(8,128)(2,1)} %reshape.86.refs_1_, bf16[768,768]{1,0:T(8,128)(2,1)S(1)} %convolution_convert_fusion.5.refs_2_.refs_1_, ...), custom_call_target="tpu_custom_call" | custom-call | flops 6341787648 | bytes 14155776 | tf_op jit(solution)/shard_map/attend_own/pallas_call | solution.py:193
  95.1 16.1 %attend_shard.3 = (bf16[768,1536]{1,0:T(8,128)(2,1)S(1)}, f32[768,768]{1,0:T(8,128)}, f32[6,2,768]{2,1,0:T(2,128)S(1)}, f32[6,2,768]{2,1,0:T(2,128)S(1)}) custom-call(bf16[768,768]{1,0:T(8,128)(2,1)S(1)} %collective-permute-done.refs_0_, bf16[768,1536]{1,0:T(8,128)(2,1)} %reshape.86.refs_1_, bf16[768,768]{1,0:T(8,128)(2,1)S(1)} %convolution_convert_fusion.5.refs_2_.refs_1_, ...), custom_call_target="tpu_custom_call" | custom-call | flops 6341787648 | bytes 14155776 | tf_op jit(solution)/shard_map/attend_shard/pallas_call | solution.py:193
  114.3 16.1 %attend_shard.4 = (bf16[768,1536]{1,0:T(8,128)(2,1)S(1)}, f32[768,768]{1,0:T(8,128)}, f32[6,2,768]{2,1,0:T(2,128)S(1)}, f32[6,2,768]{2,1,0:T(2,128)S(1)}) custom-call(bf16[768,768]{1,0:T(8,128)(2,1)S(1)} %add.118.refs_0_, bf16[768,1536]{1,0:T(8,128)(2,1)} %reshape.86.refs_1_, bf16[768,768]{1,0:T(8,128)(2,1)S(1)} %convolution_convert_fusion.5.refs_2_.refs_1_, ...), custom_call_target="tpu_custom_call" | custom-call | flops 6341787648 | bytes 14155776 | tf_op jit(solution)/shard_map/attend_shard/pallas_call | solution.py:193
  132.9 16.8 %attend_shard.5 = (bf16[768,1536]{1,0:T(8,128)(2,1)}, f32[768,768]{1,0:T(8,128)}, f32[6,2,768]{2,1,0:T(2,128)S(1)}, f32[6,2,768]{2,1,0:T(2,128)}, bf16[768,768]{1,0:T(8,128)(2,1)S(1)}) custom-call(bf16[768,768]{1,0:T(8,128)(2,1)S(1)} %add.114.refs_0_, bf16[768,1536]{1,0:T(8,128)(2,1)} %reshape.86.refs_1_, ...), custom_call_target="tpu_custom_call" | custom-call | flops 6341787648 | bytes 14155776 | tf_op jit(solution)/shard_map/attend_shard/pallas_call | solution.py:193
  152.6 7.6 %multiply_convert_fusion = (bf16[768,3072]{1,0:T(8,128)(2,1)}, f32[768,3072]{1,0:T(8,128)}) fusion(f32[3072]{0:T(1024)S(1)} %copy-done.53, bf16[768,3072]{1,0:T(8,128)(2,1)S(1)} %bitcast.52, f32[768,768]{1,0:T(8,128)S(1)} %get-tuple-element.101, f32[768]{0:T(1024)S(1)} %copy-done.51, f32[768]{0:T(1024)S(1)} %add_rsqrt_fusion, ...), kind=kOutput, calls=%fused_computation.8 | convolution fusion | flops 3640393728 | bytes 21255168 | tf_op jit(solution)/shard_map/dot_general | solution.py:28
  160.3 12.2 %convert_reduce_fusion = (f32[3072]{0:T(1024)}, bf16[768,3072]{1,0:T(8,128)(2,1)}) fusion(f32[768,3072]{1,0:T(8,128)} %get-tuple-element.104, f32[3072]{0:T(1024)S(1)} %copy-done.53, bf16[3072,768]{1,0:T(8,128)(2,1)} %param.21, f32[768,768]{1,0:T(8,128)S(1)} %copy-done.40), kind=kOutput, calls=%fused_computation.7 | convolution fusion | flops 3655136256 | bytes 21258240 | tf_op jit(solution)/shard_map/dot_general | solution.py:28
  172.4 8.4 %multiply_reduce_fusion = (f32[768]{0:T(1024)}, f32[768]{0:T(1024)S(1)}, f32[768]{0:T(1024)S(1)}, f32[768,768]{1,0:T(8,128)S(1)}) fusion(f32[768,768]{1,0:T(8,128)S(1)} %get-tuple-element.101, f32[768]{0:T(1024)S(1)} %add_rsqrt_fusion, f32[768]{0:T(1024)S(1)} %broadcast_multiply_fusion.4, f32[768]{0:T(1024)S(1)} %copy-done.51, ...), kind=kOutput, calls=%fused_computation.15 | convolution fusion | flops 3628594944 | bytes 14174208 | tf_op jit(solution)/shard_map/dot_general | solution.py:28
  180.9 6.2 convolution_convert_fusion.1
  197.2 23.1 %back_shard.3 = (bf16[768,1536]{1,0:T(8,128)(2,1)S(1)}, f32[768,768]{1,0:T(8,128)}) custom-call(bf16[768,1536]{1,0:T(8,128)(2,1)} %get-tuple-element.48.refs_0_, bf16[768,768]{1,0:T(8,128)(2,1)S(1)} %copy-done.23, bf16[768,768]{1,0:T(8,128)(2,1)S(1)} %convolution_convert_fusion.4.refs_2_, f32[6,2,768]{2,1,0:T(2,128)S(1)} %get-tuple-element.44.refs_3_, ...), custom_call_target="tpu_custom_call" | custom-call | flops 11777605632 | bytes 14155776 | tf_op jit(solution)/shard_map/back_shard/pallas_call | solution.py:273
  220.4 23.9 %back_shard.4 = (bf16[768,1536]{1,0:T(8,128)(2,1)S(1)}, f32[768,768]{1,0:T(8,128)}) custom-call(bf16[768,1536]{1,0:T(8,128)(2,1)} %copy-done.26, bf16[768,768]{1,0:T(8,128)(2,1)S(1)} %copy-done.24, bf16[768,768]{1,0:T(8,128)(2,1)S(1)} %convolution_convert_fusion.4.refs_2_, f32[6,2,768]{2,1,0:T(2,128)S(1)} %get-tuple-element.44.refs_3_, ...), custom_call_target="tpu_custom_call" | custom-call | flops 11777605632 | bytes 14155776 | tf_op jit(solution)/shard_map/back_shard/pallas_call | solution.py:273
  245.1 23.1 %back_shard.5 = (bf16[768,1536]{1,0:T(8,128)(2,1)S(1)}, f32[768,768]{1,0:T(8,128)}) custom-call(bf16[768,1536]{1,0:T(8,128)(2,1)} %copy-done.25, bf16[768,768]{1,0:T(8,128)(2,1)S(1)} %copy-done.24, bf16[768,768]{1,0:T(8,128)(2,1)S(1)} %convolution_convert_fusion.4.refs_2_, f32[6,2,768]{2,1,0:T(2,128)S(1)} %copy-done.29, ...), custom_call_target="tpu_custom_call" | custom-call | flops 11777605632 | bytes 14155776 | tf_op jit(solution)/shard_map/back_shard/pallas_call | solution.py:273
  270.3 23.7 %back_own.1 = (bf16[768,1536]{1,0:T(8,128)(2,1)}, bf16[768,768]{1,0:T(8,128)(2,1)S(1)}) custom-call(bf16[768,1536]{1,0:T(8,128)(2,1)} %copy-done.27, bf16[768,768]{1,0:T(8,128)(2,1)S(1)} %copy-done.24, bf16[768,768]{1,0:T(8,128)(2,1)S(1)} %copy-done.19, f32[6,2,768]{2,1,0:T(2,128)S(1)} %copy-done.30, f32[768,768]{1,0:T(8,128)} %get-tuple-element.45.refs_4_, ...), custom_call_target="tpu_custom_call" | custom-call | flops 11777605632 | bytes 14155776 | tf_op jit(solution)/shard_map/back_own/pallas_call | solution.py:273
  307.3 6.0 copy.50
  329.9 48.1 %collective-permute-done.7 = bf16[768,768]{1,0:T(8,128)(2,1)S(1)} collective-permute-done((bf16[768,768]{1,0:T(8,128)(2,1)S(1)}, bf16[768,768]{1,0:T(8,128)(2,1)S(1)}, u32[]{:S(2)}, u32[]{:S(2)}) %collective-permute-start.7) | collective-permute-done | bytes 1179680 | tf_op jit(solution)/shard_map/ppermute | solution.py:300
  381.6 46.1 %collective-permute-done.5 = bf16[768,768]{1,0:T(8,128)(2,1)S(1)} collective-permute-done((bf16[768,768]{1,0:T(8,128)(2,1)S(1)}, bf16[768,768]{1,0:T(8,128)(2,1)S(1)}, u32[]{:S(2)}, u32[]{:S(2)}) %collective-permute-start.5) | collective-permute-done | bytes 1179680 | tf_op jit(solution)/shard_map/ppermute | solution.py:300
  432.8 7.3 %collective-permute-start.10 = (bf16[768,768]{1,0:T(8,128)(2,1)S(1)}, bf16[768,768]{1,0:T(8,128)(2,1)S(1)}, u32[]{:S(2)}, u32[]{:S(2)}) collective-permute-start(bf16[768,768]{1,0:T(8,128)(2,1)S(1)} %get-tuple-element.80), channel_id=1, source_target_pairs={{0,1},{3,2},{4,5},{7,6},{8,9},{11,10},{12,13},{15,14},{16,17},{19,... | collective-permute-start | bytes 3538952 | tf_op jit(solution)/shard_map/ppermute | solution.py:300
  447.8 30.7 %collective-permute-done.9 = bf16[768,768]{1,0:T(8,128)(2,1)S(1)} collective-permute-done((bf16[768,768]{1,0:T(8,128)(2,1)S(1)}, bf16[768,768]{1,0:T(8,128)(2,1)S(1)}, u32[]{:S(2)}, u32[]{:S(2)}) %collective-permute-start.9) | collective-permute-done | bytes 1179680 | tf_op jit(solution)/shard_map/ppermute | solution.py:300
  481.7 43.0 %psum.35 = f32[4608]{0:T(1024)S(1)} all-reduce(f32[4608]{0:T(1024)S(1)} %pad_maximum_fusion.1), channel_id=1, replica_groups=mesh['dp'=8,'blk'=4] {'dp','blk'}, use_global_device_ids=true, to_apply=%region_11.12 | all-reduce | flops 4608 | bytes 36864 | tf_op jit(solution)/shard_map/psum | solution.py:394
  530.3 100.3 %all-reduce.3.cloned.1.call-done = (bf16[768,2304]{0,1:T(8,128)(2,1)}, bf16[768,768]{1,0:T(8,128)(2,1)}, bf16[768,3072]{1,0:T(8,128)(2,1)}, bf16[3072,768]{1,0:T(8,128)(2,1)}) async-done(((bf16[768,2304]{0,1:T(8,128)(2,1)}, bf16[768,768]{1,0:T(8,128)(2,1)}, bf16[768,3072]{1,0:T(8,128)(2,1)}, bf16[3072,768]{1,0:T(8,128)(2,1)}), (bf16[768,2304]{0,1:T(8,128)(2,1)}, bf16[768,768]{1,0:T(8,128)(2,1)}, ...) | async-done | bytes 14155792 | tf_op jit(solution)/shard_map/psum | solution.py:394
  638.1 7.4 %convert_element_type.127 = f32[768,3072]{1,0:T(8,128)} convert(bf16[768,3072]{1,0:T(8,128)(2,1)} %get-tuple-element.74) | non-fusion elementwise | flops 2359296 | bytes 14155776 | tf_op jit(solution)/shard_map/convert_element_type | solution.py:402
  645.4 6.9 %convert_element_type.129 = f32[3072,768]{1,0:T(8,128)} convert(bf16[3072,768]{1,0:T(8,128)(2,1)} %get-tuple-element.75) | non-fusion elementwise | flops 2359296 | bytes 14155776 | tf_op jit(solution)/shard_map/convert_element_type | solution.py:404
  (215 shorter events, 123.8 us)
Async XLA Ops:
  7.2 142.6 %copy-start = (bf16[768,768]{1,0:T(8,128)(2,1)S(1)}, bf16[768,768]{1,0:T(8,128)(2,1)}, u32[]{:S(2)}) copy-start(bf16[768,768]{1,0:T(8,128)(2,1)} %param.17) | copy-start | bytes 3538948
  7.2 623.4 %all-reduce.3.cloned.1.call-start = ((), (), s32[]{:S(2)}) async-start(), calls=%async_computation | async-start | bytes 28311552 | tf_op jit(solution)/shard_map/psum | solution.py:394
  14.4 29.1 %collective-permute-start = (bf16[768,768]{1,0:T(8,128)(2,1)S(1)}, bf16[768,768]{1,0:T(8,128)(2,1)S(1)}, u32[]{:S(2)}, u32[]{:S(2)}) collective-permute-start(bf16[768,768]{1,0:T(8,128)(2,1)S(1)} %multiply_convert_fusion.2.refs_0_), channel_id=1, source_target_pairs={{0,1},{1,0},{2,3},{3,2},{4,5},{5,4},{6,7},{7,6},{8,9},{9,8},{10,11... | collective-permute-start | bytes 3538952 | tf_op jit(solution)/shard_map/ppermute | solution.py:300
  17.4 57.3 %collective-permute-start.3 = (bf16[768,768]{1,0:T(8,128)(2,1)S(1)}, bf16[768,768]{1,0:T(8,128)(2,1)}, u32[]{:S(2)}, u32[]{:S(2)}) collective-permute-start(bf16[768,768]{1,0:T(8,128)(2,1)S(1)} %multiply_convert_fusion.2.refs_0_), channel_id=1, source_target_pairs={{1,2},{2,1},{5,6},{6,5},{9,10},{10,9},{13,14},{14,13},{17,18},{18,... | collective-permute-start | bytes 3538952 | tf_op jit(solution)/shard_map/ppermute | solution.py:300
  43.4 50.2 %collective-permute-start.1 = (bf16[768,768]{1,0:T(8,128)(2,1)S(1)}, bf16[768,768]{1,0:T(8,128)(2,1)}, u32[]{:S(2)}, u32[]{:S(2)}) collective-permute-start(bf16[768,768]{1,0:T(8,128)(2,1)S(1)} %collective-permute-done.refs_0_), channel_id=1, source_target_pairs={{1,2},{2,1},{5,6},{6,5},{9,10},{10,9},{13,14},{14,13},{17,18},{18,... | collective-permute-start | bytes 3538952 | tf_op jit(solution)/shard_map/ppermute | solution.py:300
  74.7 58.2 %copy-start.22 = (bf16[768,768]{1,0:T(8,128)(2,1)}, bf16[768,768]{1,0:T(8,128)(2,1)S(1)}, u32[]{:S(2)}) copy-start(bf16[768,768]{1,0:T(8,128)(2,1)S(1)} %convolution_convert_fusion.5.refs_2_.refs_1_) | copy-start | bytes 3538948
  74.7 37.9 %collective-permute-start.4 = (bf16[768,768]{1,0:T(8,128)(2,1)}, bf16[768,768]{1,0:T(8,128)(2,1)S(1)}, u32[]{:S(2)}, u32[]{:S(2)}) collective-permute-start(bf16[768,768]{1,0:T(8,128)(2,1)} %collective-permute-done.3), channel_id=1, source_target_pairs={{1,0},{2,3},{5,4},{6,7},{9,8},{10,11},{13,12},{14,15},{17,16},{18,... | collective-permute-start | bytes 3538952 | tf_op jit(solution)/shard_map/ppermute | solution.py:300
  93.6 36.8 %collective-permute-start.2 = (bf16[768,768]{1,0:T(8,128)(2,1)}, bf16[768,768]{1,0:T(8,128)(2,1)S(1)}, u32[]{:S(2)}, u32[]{:S(2)}) collective-permute-start(bf16[768,768]{1,0:T(8,128)(2,1)} %collective-permute-done.1), channel_id=1, source_target_pairs={{1,0},{2,3},{5,4},{6,7},{9,8},{10,11},{13,12},{14,15},{17,16},{18,... | collective-permute-start | bytes 3538952 | tf_op jit(solution)/shard_map/ppermute | solution.py:300
  149.8 70.6 %copy-start.28 = (f32[6,2,768]{2,1,0:T(2,128)}, f32[6,2,768]{2,1,0:T(2,128)S(1)}, u32[]{:S(2)}) copy-start(f32[6,2,768]{2,1,0:T(2,128)S(1)} %get-tuple-element.44.refs_3_) | copy-start | bytes 110596
  151.0 36.0 %copy-start.34 = (f32[768,768]{1,0:T(8,128)}, f32[768,768]{1,0:T(8,128)S(1)}, u32[]{:S(2)}) copy-start(f32[768,768]{1,0:T(8,128)S(1)} %get-tuple-element.101) | copy-start | bytes 7077892
  191.4 52.9 %copy-start.18 = (bf16[768,768]{1,0:T(8,128)(2,1)}, bf16[768,768]{1,0:T(8,128)(2,1)S(1)}, u32[]{:S(2)}) copy-start(bf16[768,768]{1,0:T(8,128)(2,1)S(1)} %convolution_convert_fusion.4.refs_2_) | copy-start | bytes 3538948
  220.3 82.0 %copy-start.2 = (bf16[768,1536]{1,0:T(8,128)(2,1)}, bf16[768,1536]{1,0:T(8,128)(2,1)S(1)}, u32[]{:S(2)}) copy-start(bf16[768,1536]{1,0:T(8,128)(2,1)S(1)} %get-tuple-element.56) | copy-start | bytes 7077892
  320.7 57.2 %collective-permute-start.7 = (bf16[768,768]{1,0:T(8,128)(2,1)S(1)}, bf16[768,768]{1,0:T(8,128)(2,1)S(1)}, u32[]{:S(2)}, u32[]{:S(2)}) collective-permute-start(bf16[768,768]{1,0:T(8,128)(2,1)S(1)} %get-tuple-element.105), channel_id=1, source_target_pairs={{0,1},{3,2},{4,5},{7,6},{8,9},{11,10},{12,13},{15,14},{16,17},{19,... | collective-permute-start | bytes 3538952 | tf_op jit(solution)/shard_map/ppermute | solution.py:300
  328.5 99.3 %collective-permute-start.5 = (bf16[768,768]{1,0:T(8,128)(2,1)S(1)}, bf16[768,768]{1,0:T(8,128)(2,1)S(1)}, u32[]{:S(2)}, u32[]{:S(2)}) collective-permute-start(bf16[768,768]{1,0:T(8,128)(2,1)S(1)} %get-tuple-element.107), channel_id=1, source_target_pairs={{0,1},{3,2},{4,5},{7,6},{8,9},{11,10},{12,13},{15,14},{16,17},{19,... | collective-permute-start | bytes 3538952 | tf_op jit(solution)/shard_map/ppermute | solution.py:300
  378.2 50.7 %collective-permute-start.8 = (bf16[768,768]{1,0:T(8,128)(2,1)S(1)}, bf16[768,768]{1,0:T(8,128)(2,1)S(1)}, u32[]{:S(2)}, u32[]{:S(2)}) collective-permute-start(bf16[768,768]{1,0:T(8,128)(2,1)S(1)} %add_convert_fusion.2), channel_id=1, source_target_pairs={{1,2},{2,1},{5,6},{6,5},{9,10},{10,9},{13,14},{14,13},{17,18},{18,... | collective-permute-start | bytes 3538952 | tf_op jit(solution)/shard_map/ppermute | solution.py:300
  379.6 62.9 %slice-start.2 = ((s8[4718592]{0:T(1024)(128)(4,1)}), s8[4194304]{0:T(1024)(128)(4,1)S(1)}, s32[]{:S(2)}) async-start(s8[4718592]{0:T(1024)(128)(4,1)} %bitcast.53), calls=%async_computation.3 | async-start | bytes 8388608
  428.1 19.8 %collective-permute-start.6 = (bf16[768,768]{1,0:T(8,128)(2,1)S(1)}, bf16[768,768]{1,0:T(8,128)(2,1)S(1)}, u32[]{:S(2)}, u32[]{:S(2)}) collective-permute-start(bf16[768,768]{1,0:T(8,128)(2,1)S(1)} %add_convert_fusion.3), channel_id=1, source_target_pairs={{1,2},{2,1},{5,6},{6,5},{9,10},{10,9},{13,14},{14,13},{17,18},{18,... | collective-permute-start | bytes 3538952 | tf_op jit(solution)/shard_map/ppermute | solution.py:300
  431.5 47.0 %collective-permute-start.9 = (bf16[768,768]{1,0:T(8,128)(2,1)S(1)}, bf16[768,768]{1,0:T(8,128)(2,1)S(1)}, u32[]{:S(2)}, u32[]{:S(2)}) collective-permute-start(bf16[768,768]{1,0:T(8,128)(2,1)S(1)} %get-tuple-element.79), channel_id=1, source_target_pairs={{1,0},{2,3},{5,4},{6,7},{9,8},{10,11},{13,12},{14,15},{17,16},{18,... | collective-permute-start | bytes 3538952 | tf_op jit(solution)/shard_map/ppermute | solution.py:300
  432.8 45.7 %collective-permute-start.10 = (bf16[768,768]{1,0:T(8,128)(2,1)S(1)}, bf16[768,768]{1,0:T(8,128)(2,1)S(1)}, u32[]{:S(2)}, u32[]{:S(2)}) collective-permute-start(bf16[768,768]{1,0:T(8,128)(2,1)S(1)} %get-tuple-element.80), channel_id=1, source_target_pairs={{0,1},{3,2},{4,5},{7,6},{8,9},{11,10},{12,13},{15,14},{16,17},{19,... | collective-permute-start | bytes 3538952 | tf_op jit(solution)/shard_map/ppermute | solution.py:300
  442.6 35.9 %copy-start.33 = (f32[768,768]{1,0:T(8,128)S(1)}, f32[768,768]{1,0:T(8,128)}, u32[]{:S(2)}) copy-start(f32[768,768]{1,0:T(8,128)} %copy-done.31) | copy-start | bytes 7077892
  442.6 35.9 %copy-start.45 = (f32[768]{0:T(1024)S(1)}, f32[768]{0:T(1024)}, u32[]{:S(2)}) copy-start(f32[768]{0:T(1024)} %copy-done.44) | copy-start | bytes 9220
  442.6 35.9 %copy-start.47 = (f32[768]{0:T(1024)S(1)}, f32[768]{0:T(1024)}, u32[]{:S(2)}) copy-start(f32[768]{0:T(1024)} %copy-done.46) | copy-start | bytes 9220
  442.6 35.9 %copy-start.49 = (f32[768]{0:T(1024)S(1)}, f32[768]{0:T(1024)}, u32[]{:S(2)}) copy-start(f32[768]{0:T(1024)} %param.15) | copy-start | bytes 9220
  447.8 33.9 %copy-start.52 = (f32[768]{0:T(1024)S(1)}, f32[768]{0:T(1024)}, u32[]{:S(2)}) copy-start(f32[768]{0:T(1024)} %get-tuple-element.68) | copy-start | bytes 9220
  (51 other events, 423.6 us)
Sparse Core Ops, SparseCore 0:
  315.4 315.1 all-reduce.2

commit v2 on v1

v2 whole, which is shorter than its diff:
```python
import functools
import math

import jax
import jax.numpy as jnp
from jax import lax
from jax.experimental import pallas as pl
from jax.experimental.pallas import tpu as pltpu
from jax.sharding import PartitionSpec as P

HEADS = 12
HEAD = 64
PAIR = 2 * HEAD
SCALE = HEAD**-0.5
LOG2E = 1.4426950408889634
MASKED = -1.0e9
QUERY_BLOCK = 384
EPS_NORM = 1e-06
LOW = jnp.bfloat16
WIDE = jnp.float32

NN = (((1,), (0,)), ((), ()))
NT = (((1,), (1,)), ((), ()))
TN = (((0,), (0,)), ((), ()))


def dot(left, right, dims):
    return lax.dot_general(left, right, dims, preferred_element_type=WIDE)


def position_table(positions, model_width):
    half_width = model_width // 2
    freqs = jnp.exp(jnp.arange(half_width, dtype=WIDE) * (-math.log(10000.0) / half_width))
    angles = positions.astype(WIDE)[:, None] * freqs[None, :]
    return jnp.concatenate([jnp.sin(angles), jnp.cos(angles)], axis=1)


def normalize(values):
    center = values - jnp.mean(values, axis=-1, keepdims=True)
    inverse = lax.rsqrt(jnp.mean(center * center, axis=-1, keepdims=True) + EPS_NORM)
    return center * inverse, inverse


def norm_back(grad_norm, normed, inverse):
    first = jnp.mean(grad_norm, axis=-1, keepdims=True)
    second = jnp.mean(grad_norm * normed, axis=-1, keepdims=True)
    return inverse * (grad_norm - first - normed * second)


def in_head(values, head):
    lanes = lax.broadcasted_iota(jnp.int32, values.shape, 1)
    return (lanes < HEAD) == (head == 0)


def only_head(values, head, other=None):
    other = jnp.zeros_like(values) if other is None else other
    return jnp.where(in_head(values, head), values, other)


def split_scaled(query):
    scaled = query.astype(WIDE) * (SCALE * LOG2E)
    high = scaled.astype(LOW)
    return high, (scaled - high.astype(WIDE)).astype(LOW)


def score_sides(key, query):
    high, low = split_scaled(query)
    key_side = jnp.concatenate([key, key], axis=1)
    query_side = [
        jnp.concatenate([only_head(high, head), only_head(low, head)], axis=1) for head in range(2)
    ]
    return key_side, query_side


def work_items(rows):
    return [(start, head) for start in range(0, rows, QUERY_BLOCK) for head in range(2)]


def whole(*shape):
    return pl.BlockSpec(shape, lambda pair: (0,) * len(shape))


def columns_of(rows, first=0):
    return pl.BlockSpec((rows, PAIR), lambda pair: (0, pair + first))


def forward_kernel(first, last, *refs):
    a_ref, wk_ref, wv_ref, q_ref, key_clip, query_clip = refs[:6]
    refs = refs[6:]
    if not first:
        acc_in, top_in, total_in = refs[:3]
        refs = refs[3:]
    k_ref, v_ref, acc_ref, top_ref, total_ref = refs[:5]
    attn_ref = refs[5] if last else None
    rows = q_ref.shape[0]
    kv = dot(a_ref[...], jnp.concatenate([wk_ref[...], wv_ref[...]], axis=1), NN).astype(LOW)
    key, value = kv[:, :PAIR], kv[:, PAIR:]
    k_ref[...] = key
    v_ref[...] = value
    value_t = value.T
    ones = jnp.ones((16, rows), LOW)
    value_rows = [
        jnp.concatenate([value_t[head * HEAD : (head + 1) * HEAD], ones], axis=0) for head in range(2)
    ]
    key_side, query_side = score_sides(key, q_ref[...])

    def scores(start, head):
        stop = start + QUERY_BLOCK
        result = dot(key_side, query_side[head][start:stop], NT)
        return jnp.where(key_clip[...] == query_clip[:, start:stop], result, MASKED)

    def weights(start, head, result):
        stop = start + QUERY_BLOCK
        top = jnp.max(result, axis=0, keepdims=True)
        if not first:
            top = jnp.maximum(top, top_in[head : head + 1, start:stop])
        return jnp.exp2(result - top).astype(LOW), top

    def attend(start, head, expd, top):
        stop = start + QUERY_BLOCK
        lanes, row = slice(head * HEAD, (head + 1) * HEAD), slice(head, head + 1)
        result = dot(value_rows[head], expd, NN)
        acc, total = result[:HEAD], result[HEAD : HEAD + 1]
        if not first:
            shrink = jnp.exp2(top_in[row, start:stop] - top)
            acc = acc_in[lanes, start:stop] * shrink + acc
            total = total_in[row, start:stop] * shrink + total
        if last:
            acc = acc * (1.0 / total)
            top = top + jnp.log(total) * LOG2E
        acc_ref[lanes, start:stop] = acc
        top_ref[row, start:stop] = top
        total_ref[row, start:stop] = total

    items = work_items(rows)
    result = scores(*items[0])
    before = None
    for index, item in enumerate(items):
        following = scores(*items[index + 1]) if index + 1 < len(items) else None
        done = weights(*item, result)
        if before is not None:
            attend(*before)
        before = (*item, *done)
        result = following
    attend(*before)
    if last:
        attn_ref[...] = acc_ref[...].T.astype(LOW)


def forward_call(first, last, a_shard, w_qkv, query, key_clip, query_clip, state):
    rows, width = query.shape
    pairs = width // PAIR
    across = pl.BlockSpec((PAIR, rows), lambda pair: (pair, 0))
    line = pl.BlockSpec((None, 2, rows), lambda pair: (pair, 0, 0))
    state_specs = [across, line, line]
    state_shapes = [
        jax.ShapeDtypeStruct((width, rows), WIDE),
        jax.ShapeDtypeStruct((pairs, 2, rows), WIDE),
        jax.ShapeDtypeStruct((pairs, 2, rows), WIDE),
    ]
    in_specs = [
        whole(rows, width),
        columns_of(width, pairs),
        columns_of(width, 2 * pairs),
        columns_of(rows),
        whole(rows, 1),
        whole(1, rows),
    ]
    operands = [a_shard, w_qkv, w_qkv, query, key_clip, query_clip]
    if not first:
        in_specs += state_specs
        operands += list(state)
    low_rows = jax.ShapeDtypeStruct((rows, width), LOW)
    out_specs = [columns_of(rows), columns_of(rows), *state_specs]
    out_shape = [low_rows, low_rows, *state_shapes]
    if last:
        out_specs.append(columns_of(rows))
        out_shape.append(low_rows)
    return pl.pallas_call(
        functools.partial(forward_kernel, first, last),
        grid=(pairs,),
        in_specs=in_specs,
        out_specs=out_specs,
        out_shape=out_shape,
        name="attend",
        cost_estimate=pl.CostEstimate(
            flops=20 * rows * rows * width, bytes_accessed=24 * rows * width, transcendentals=0
        ),
        compiler_params=pltpu.CompilerParams(vmem_limit_bytes=48 * 2**20),
    )(*operands)


def backward_pair(key, value, query, grad_t, lse, row_dots, key_clip, query_clip, add):
    rows = query.shape[0]
    grad = grad_t.T
    key_t, query_t = key.T, query.T
    key_side, query_side = score_sides(key, query)
    grad_side = [only_head(grad, head) for head in range(2)]
    for start, head in work_items(rows):
        stop = start + QUERY_BLOCK
        lanes, row = slice(head * HEAD, (head + 1) * HEAD), slice(head, head + 1)
        score = dot(key_side, query_side[head][start:stop], NT)
        score = jnp.where(key_clip == query_clip[:, start:stop], score, MASKED)
        probs = jnp.exp2(score - lse[row, start:stop])
        d_probs = dot(value, grad_side[head][start:stop], NT)
        d_scores = (probs * (d_probs - row_dots[row, start:stop])).astype(LOW)
        probs = probs.astype(LOW)
        dv = dot(grad_t[lanes, start:stop], probs, NT)
        dk = dot(query_t[lanes, start:stop], d_scores, NT)
        dq = dot(key_t[lanes], d_scores, NN)
        add(head, start, stop, dq, dk, dv)


def backward_kernel(first, last, *refs):
    k_ref, v_ref, q_ref, grad_ref, lse_ref, dots_ref, key_clip, query_clip, wk_ref, wv_ref = refs[:10]
    refs = refs[10:]
    if not first:
        dq_in = refs[0]
        refs = refs[1:]
    dk_ref, dv_ref, dq_ref, part_ref, dk_sum, dv_sum, dq_sum, dk_all, dv_all = refs
    pair = pl.program_id(0)
    rows = q_ref.shape[0]

    def add(head, start, stop, dq, dk, dv):
        lanes = slice(head * HEAD, (head + 1) * HEAD)
        if start == 0:
            dv_sum[lanes], dk_sum[lanes] = dv, dk
        else:
            dv_sum[lanes] += dv
            dk_sum[lanes] += dk
        if not first:
            dq = dq + dq_in[lanes, start:stop]
        if last:
            dq_sum[lanes, start:stop] = dq
        else:
            dq_ref[lanes, start:stop] = dq

    backward_pair(
        k_ref[...],
        v_ref[...],
        q_ref[...],
        grad_ref[...],
        lse_ref,
        dots_ref,
        key_clip[...],
        query_clip[...],
        add,
    )
    if last:
        dq_ref[...] = (dq_sum[...] * SCALE).T.astype(LOW)
    dk = (dk_sum[...] * SCALE).T.astype(LOW)
    dv = dv_sum[...].T.astype(LOW)
    dk_ref[...] = dk
    dv_ref[...] = dv
    dk_all[pair] = dk
    dv_all[pair] = dv

    @pl.when(pair == pl.num_programs(0) - 1)
    def _():
        pairs = dk_all.shape[0]
        dk_rows = jnp.concatenate([dk_all[index] for index in range(pairs)], axis=1)
        dv_rows = jnp.concatenate([dv_all[index] for index in range(pairs)], axis=1)
        part = dot(dk_rows, wk_ref[...], NT) + dot(dv_rows, wv_ref[...], NT)
        part_ref[...] = part.astype(part_ref.dtype)


def backward_call(first, last, key, value, query, grad_t, lse, row_dots, key_clip, query_clip, w_qkv, dq):
    rows, width = query.shape
    pairs = width // PAIR
    across = pl.BlockSpec((PAIR, rows), lambda pair: (pair, 0))
    line = pl.BlockSpec((None, 2, rows), lambda pair: (pair, 0, 0))
    columns = columns_of(rows)
    in_specs = [columns, columns, columns, across, line, line, whole(rows, 1), whole(1, rows)]
    in_specs += [
        pl.BlockSpec((width, width), lambda pair: (0, 1)),
        pl.BlockSpec((width, width), lambda pair: (0, 2)),
    ]
    operands = [key, value, query, grad_t, lse, row_dots, key_clip, query_clip, w_qkv, w_qkv]
    if not first:
        in_specs.append(across)
        operands.append(dq)
    low_rows = jax.ShapeDtypeStruct((rows, width), LOW)
    tall = pltpu.VMEM((PAIR, rows), WIDE)
    parts = pltpu.VMEM((pairs, rows, PAIR), LOW)
    return pl.pallas_call(
        functools.partial(backward_kernel, first, last),
        grid=(pairs,),
        in_specs=in_specs,
        out_specs=[columns, columns, columns if last else across, whole(rows, width)],
        out_shape=[
            low_rows,
            low_rows,
            low_rows if last else jax.ShapeDtypeStruct((width, rows), WIDE),
            jax.ShapeDtypeStruct((rows, width), WIDE if last else LOW),
        ],
        scratch_shapes=[tall, tall, tall, parts, parts],
        name="attend_back",
        cost_estimate=pl.CostEstimate(
            flops=40 * rows * rows * width, bytes_accessed=24 * rows * width, transcendentals=0
        ),
        compiler_params=pltpu.CompilerParams(vmem_limit_bytes=48 * 2**20),
    )(*operands)


MESH = pl.DeviceIdType.MESH
TURNS = ((0, 1, 2), (0, 2, 1))


def place_bits(turn):
    group, place = lax.axis_index("dp"), lax.axis_index("blk")
    steps = []
    for bit in TURNS[turn]:
        mine = group // (1 << bit) % 2
        steps.append((mine, (group + (1 - 2 * mine) * (1 << bit), place)))
    for bit in range(2):
        mine = place // (1 << bit) % 2
        steps.append((mine, (group, place + (1 - 2 * mine) * (1 << bit))))
    return steps


def remote(source, target, sems, index, device):
    return pltpu.make_async_remote_copy(
        src_ref=source,
        dst_ref=target,
        send_sem=sems[0].at[index],
        recv_sem=sems[1].at[index],
        device_id=device,
        device_id_type=MESH,
    )


def add_rows(total, start, term, rows, step):
    @pl.loop(0, rows // step)
    def _(index):
        here = pl.ds(pl.multiple_of(start + index * step, 16), step)
        there = pl.ds(pl.multiple_of(index * step, 16), step)
        total[here] = (total[here].astype(WIDE) + term[there].astype(WIDE)).astype(total.dtype)


class Sum:
    def __init__(self, turn, term, result, total, arrived, sems, local_sems):
        self.term, self.result, self.total, self.arrived = term, result, total, arrived
        self.sems, self.local_sems = sems, local_sems
        self.steps = place_bits(turn)
        self.count = len(self.steps)
        rows = total.shape[0]
        self.first = self.steps[0][0] * rows
        self.keep = [(0, rows)]
        for mine, _ in self.steps[1:]:
            start, size = self.keep[-1]
            self.keep.append((start + mine * (size // 2), size // 2))
        self.block = min(rows, self.keep[-1][1])
        self.pending = {}

    def _rows(self, ref, start, size):
        return ref.at[pl.ds(pl.multiple_of(start, 16), size)]

    def load(self):
        source = self._rows(self.term, self.first, self.total.shape[0])
        return pltpu.make_async_copy(source, self.total, self.local_sems.at[0])

    def store(self):
        start, size = self.keep[-1]
        source = self._rows(self.total, start, size)
        target = self._rows(self.result, self.first + start, size)
        return pltpu.make_async_copy(source, target, self.local_sems.at[1])

    def gather(self, step):
        mine, device = self.steps[step]
        start, size = self.keep[step]
        if step == 0:
            rows = self.total.shape[0]
            source = self._rows(self.term, (1 - mine) * rows, rows)
        else:
            upper, _ = self.keep[step - 1]
            source = self._rows(self.total, upper + (1 - mine) * size, size)
        return remote(source, self.arrived[step], self.sems, step, device)

    def start_sum(self, step):
        if step == 0:
            self.load().start()
        self.gather(step).start()

    def finish_sum(self, step):
        if step == 0:
            self.load().wait()
        self.gather(step).wait()
        start, size = self.keep[step]
        add_rows(self.total, start, self.arrived[step], size, self.block)

    def spread(self, step):
        start, size = self.keep[step]
        here = self._rows(self.result, self.first + start, size)
        return remote(here, here, self.sems, self.count + step, self.steps[step][1])

    def start_spread(self, step):
        if step == self.count - 1:
            self.store().start()
            self.store().wait()
        self.spread(step).start()

    def finish_spread(self, step):
        self.spread(step).wait()


def greet():
    group, place = lax.axis_index("dp"), lax.axis_index("blk")
    devices = [device for _, device in place_bits(0)]
    devices.append((group, 3 - place))
    barrier = pltpu.get_barrier_semaphore()
    for device in devices:
        pl.semaphore_signal(barrier, inc=1, device_id=device, device_id_type=MESH)
    pl.semaphore_wait(barrier, len(devices))


def arrivals(rows, lanes, steps=5):
    return [pltpu.VMEM((rows >> (step + 1), lanes), LOW) for step in range(steps)]


def sum_kernel(shapes, *refs):
    count = len(shapes)
    terms, small_in = refs[:count], refs[count]
    results, small_out = refs[count + 1 : 2 * count + 1], refs[2 * count + 1]
    refs = refs[2 * count + 2 :]
    totals = refs[:count]
    arrived = [refs[count + 5 * index : count + 5 * index + 5] for index in range(count)]
    small_arrived, sends, receives, locals_, small_sends, small_receives = refs[6 * count :]
    greet()
    sums = [
        Sum(
            index % 2,
            terms[index],
            results[index],
            totals[index],
            arrived[index],
            (sends.at[index], receives.at[index]),
            locals_.at[index],
        )
        for index in range(count)
    ]
    small_out[...] = small_in[...]
    small_steps = place_bits(0)

    def small(step):
        return remote(
            small_out, small_arrived.at[step], (small_sends, small_receives), step, small_steps[step][1]
        )

    for each in sums:
        each.start_sum(0)
    for step in range(5):
        small(step).start()
        for each in sums:
            each.finish_sum(step)
            if step < 4:
                each.start_sum(step + 1)
            else:
                each.start_spread(step)
        small(step).wait()
        small_out[...] += small_arrived[step]
    for step in reversed(range(5)):
        for each in sums:
            each.finish_spread(step)
            if step:
                each.start_spread(step - 1)


def sum_call(terms, small):
    shapes = [term.shape for term in terms]
    count = len(shapes)
    anywhere = pl.BlockSpec(memory_space=pl.ANY)
    inside = pl.BlockSpec(memory_space=pltpu.VMEM)
    scratch = [pltpu.VMEM((rows // 2, lanes), LOW) for rows, lanes in shapes]
    for rows, lanes in shapes:
        scratch += arrivals(rows, lanes)
    scratch += [
        pltpu.VMEM((5, *small.shape), WIDE),
        pltpu.SemaphoreType.DMA((count, 10)),
        pltpu.SemaphoreType.DMA((count, 10)),
        pltpu.SemaphoreType.DMA((count, 2)),
        pltpu.SemaphoreType.DMA((5,)),
        pltpu.SemaphoreType.DMA((5,)),
    ]
    return pl.pallas_call(
        functools.partial(sum_kernel, shapes),
        in_specs=[anywhere] * count + [inside],
        out_specs=[anywhere] * count + [inside],
        out_shape=[jax.ShapeDtypeStruct(shape, LOW) for shape in shapes]
        + [jax.ShapeDtypeStruct(small.shape, WIDE)],
        scratch_shapes=scratch,
        name="sum_gradients",
        compiler_params=pltpu.CompilerParams(
            collective_id=1, has_side_effects=True, vmem_limit_bytes=60 * 2**20
        ),
    )(*terms, small)


def on_device(
    groups, inputs, positions, segments, gain_attn, w_qkv, w_out, gain_mlp, w_up, b_up, w_down, cotangent
):
    rows, width = inputs.shape
    pairs = width // PAIR
    place = lax.axis_index("blk")
    w_query = w_qkv[:, :width]

    def send(value, pairs_of_places):
        return lax.ppermute(value, "blk", pairs_of_places)

    hidden = inputs + position_table(positions, width)
    normed_attn, inverse_attn = normalize(hidden)
    a_low = (normed_attn * gain_attn).astype(LOW)

    near = [(0, 1), (1, 0), (2, 3), (3, 2)]
    middle = [(1, 2), (2, 1)]
    outward = [(1, 0), (2, 3)]
    inward = [(0, 1), (3, 2)]
    table = jnp.array([[0, 1, 2, 3], [1, 0, 2, 3], [2, 3, 1, 0], [3, 2, 1, 0]], jnp.int32)
    shard_1 = send(a_low, near)
    shard_2_middle = send(a_low, middle)
    shard_2 = shard_2_middle + send(shard_2_middle, outward)
    shard_3_middle = send(shard_1, middle)
    shard_3 = shard_3_middle + send(shard_3_middle, outward)
    shards = [a_low, shard_1, shard_2, shard_3]

    def clips_of(index):
        other = lax.dynamic_index_in_dim(table[:, index], place, keepdims=False)
        return lax.dynamic_slice_in_dim(segments, other * rows, rows)

    clips = [clips_of(index)[:, None] for index in range(4)]
    query_clip = lax.dynamic_slice_in_dim(segments, place * rows, rows)[None, :]

    query = dot(a_low, w_query, NN).astype(LOW)
    keys, values, state = [], [], None
    for index in range(4):
        key, value, *state = forward_call(
            index == 0, index == 3, shards[index], w_qkv, query, clips[index], query_clip, state
        )
        keys.append(key)
        values.append(value)
    attended, lse, _, attn_low = state

    resid = hidden + dot(attn_low, w_out, NN)
    normed_mlp, inverse_mlp = normalize(resid)
    b_low = (normed_mlp * gain_mlp).astype(LOW)
    pre_act = dot(b_low, w_up, NN) + b_up
    cumulative = 0.5 * (1.0 + lax.erf(pre_act * 0.7071067811865476))
    density = jnp.exp(-0.5 * pre_act * pre_act) * 0.3989422804014327
    z_low = (pre_act * cumulative).astype(LOW)
    outputs = resid + dot(z_low, w_down, NN)
    dy_low = cotangent.astype(LOW)
    grad_down = dot(z_low, dy_low, TN).astype(LOW)
    d_gelu = dot(dy_low, w_down, NT)
    d_pre = (d_gelu * (cumulative + pre_act * density)).astype(LOW)
    grad_up_t = dot(d_pre, b_low, TN).astype(LOW)
    grad_bias_up = jnp.sum(d_pre.astype(WIDE), axis=0)
    d_normed = dot(d_pre, w_up, NT)
    grad_gain_mlp = jnp.sum(d_normed * normed_mlp, axis=0)
    d_resid = cotangent + norm_back(d_normed * gain_mlp, normed_mlp, inverse_mlp)
    dr_low = d_resid.astype(LOW)
    grad_out = dot(attn_low, dr_low, TN).astype(LOW)
    d_attn_t = dot(w_out, dr_low, NT).astype(LOW)
    row_dots = jnp.sum(
        (d_attn_t.astype(WIDE) * attended).reshape(pairs, 2, HEAD, rows), axis=2
    )

    everywhere = ("dp", "blk")

    def back(index, dq):
        return backward_call(
            index == 3,
            index == 0,
            keys[index],
            values[index],
            query,
            d_attn_t,
            lse,
            row_dots,
            clips[index],
            query_clip,
            w_qkv,
            dq,
        )

    dk_3, dv_3, dq, part_3 = back(3, None)
    far = send(part_3, inward)
    dk_2, dv_2, dq, part_2 = back(2, dq)
    far, part_2, dq = lax.optimization_barrier((far, part_2, dq))
    onward = (part_3.astype(WIDE) + far.astype(WIDE)).astype(LOW)
    mid_3 = send(onward, middle)
    mid_2 = send(part_2, inward)
    dq, onward = lax.optimization_barrier((dq, onward))
    dk_1, dv_1, dq, part_1 = back(1, dq)
    mid_3, mid_2, part_1, dq = lax.optimization_barrier((mid_3, mid_2, part_1, dq))
    onward_1 = (part_2.astype(WIDE) + mid_2.astype(WIDE)).astype(LOW)
    onward_2 = (part_1.astype(WIDE) + mid_3.astype(WIDE)).astype(LOW)
    last_1 = send(onward_1, middle)
    last_2 = send(onward_2, outward)
    last_3 = send(part_1, inward)
    dq, onward_1, onward_2 = lax.optimization_barrier((dq, onward_1, onward_2))
    dk_0, dv_0, dq, part_0 = back(0, dq)
    grad_query = dot(a_low, dq, TN).astype(LOW)
    d_keys, d_values = (dk_0, dk_1, dk_2, dk_3), (dv_0, dv_1, dv_2, dv_3)
    grad_key = sum(dot(shard, term, TN) for shard, term in zip(shards, d_keys)).astype(LOW)
    grad_value = sum(dot(shard, term, TN) for shard, term in zip(shards, d_values)).astype(LOW)
    d_normed_attn = (
        part_0
        + dot(dq, w_query, NT)
        + last_1.astype(WIDE)
        + last_2.astype(WIDE)
        + last_3.astype(WIDE)
    )
    grad_gain_attn = jnp.sum(d_normed_attn * normed_attn, axis=0)
    input_grad = d_resid + norm_back(d_normed_attn * gain_attn, normed_attn, inverse_attn)
    small = jnp.concatenate([grad_gain_attn, grad_gain_mlp, grad_bias_up])
    if groups == 8:
        stack = lambda matrix: matrix.reshape(width, pairs, PAIR).swapaxes(0, 1).reshape(-1, PAIR)
        unstack = lambda matrix: matrix.reshape(pairs, width, PAIR).swapaxes(0, 1).reshape(width, width)
        half = grad_down.shape[0] // 2
        terms = [grad_down[:half], grad_down[half:], grad_up_t[:half], grad_up_t[half:]]
        terms += [stack(matrix) for matrix in (grad_out, grad_query, grad_key, grad_value)]
        *sums, sum_small = sum_call(terms, jnp.pad(small.reshape(6, width), ((0, 2), (0, 0))))
        sum_down = jnp.concatenate(sums[:2], axis=0)
        sum_up_t = jnp.concatenate(sums[2:4], axis=0)
        sum_out, *sum_qkv = [unstack(matrix) for matrix in sums[4:]]
        sum_small = sum_small[:6].reshape(-1)
    else:
        sums = lax.psum(
            (grad_down, grad_up_t, grad_out, grad_query, grad_key, grad_value), everywhere
        )
        sum_small = lax.psum(small, everywhere)
        sum_down, sum_up_t, sum_out, *sum_qkv = sums
    return (
        outputs,
        input_grad,
        sum_small[:width],
        jnp.concatenate(sum_qkv, axis=1).astype(WIDE),
        sum_out.astype(WIDE),
        sum_small[width : 2 * width],
        sum_up_t.T.astype(WIDE),
        sum_small[2 * width :],
        sum_down.astype(WIDE),
    )


def solution(mesh):
    rows = P(("dp", "blk"), None)
    placed = (rows, P(("dp", "blk")), P("dp"), P(), P(), P(), P(), P(), P(), P(), rows)
    return jax.shard_map(
        functools.partial(on_device, mesh.shape["dp"]),
        mesh=mesh,
        in_specs=placed,
        out_specs=(rows, rows, P(), P(), P(), P(), P(), P(), P()),
        check_vma=False,
    )
```

time: 670 us -> 592 us (0.88)
  waiting for transfers between devices: 232 us -> 14.1 us
  Pallas kernels: 159 us -> 355 us
  blocking collectives: 43 us -> 0 us
  between operations: 27.1 us -> 9.57 us
    pallas_call x8 -> x9, Pallas kernels: 159 us -> 355 us  [the longest x1 180 us: sum_call(): pl.pallas_call(functools.partial(sum_kernel, shapes), in_specs=[anywhere]...]
    ppermute x11, waiting for transfers between devices: 132 us -> 14.1 us  [send(): return lax.ppermute(value, 'blk', pairs_of_places)]
    psum x1 -> x0, waiting for transfers between devices: 100 us -> none  [on_device(): sum_qkv, sum_small = lax.psum((grad_qkv, small), everywhere)]
    psum x1 -> x0, blocking collectives: 43 us -> none  [on_device(): sum_qkv, sum_small = lax.psum((grad_qkv, small), everywhere)]
    unnamed x128 -> x169, local copies, waits for them, and re-layouts: 19.6 us -> 34.3 us
    transpose x1 -> x0, local copies, waits for them, and re-layouts: 6.81 us -> none  [on_device(): w_qkv[:, width:].reshape(width, 2, pairs, PAIR).swapaxes(1, 2)]
    convert_element_type x4 -> x5, other arithmetic: 10.9 us -> 14.9 us  [the longest x1 6.15 us: on_device(): sum_up_t.T.astype(WIDE)]
    reshape x3 -> x8, local copies, waits for them, and re-layouts: 14.4 us -> 12.2 us  [the longest x4 7.7 us: on_device(): matrix.reshape(width, pairs, PAIR).swapaxes(0, 1).reshape(-1, PAIR)]
  transfers between devices with their start and end apart: 12 -> 11, of which waited for: 5 -> 1; matrix products, arithmetic and copies ran while one was open for 10% -> 8% of each run, Pallas kernels for 7% -> 22%
where the time goes in v2:
time: 592 us; the launch traced here: 583 us
  Pallas kernels  355 us (60%)
  matrix products  74 us (12%)
  local copies, waits for them, and re-layouts  58.5 us (10%)
  other arithmetic  43.8 us (7%)
  starting transfers between devices  28.1 us (5%)
  waiting for transfers between devices  14.1 us (2%)
  between operations  9.57 us (2%)
    pallas_call x1, Pallas kernels, sum_call(): pl.pallas_call(functools.partial(sum_kernel, shapes), in_specs=[anywhere]...  180 us
    pallas_call x4, Pallas kernels, backward_call(): pl.pallas_call(functools.partial(backward_kernel, first, last), grid=(pai...  106 us
    dot_general x20, matrix products, dot(): return lax.dot_general(left, right, dims, preferred_element_type=WIDE)  74 us
    pallas_call x4, Pallas kernels, forward_call(): pl.pallas_call(functools.partial(forward_kernel, first, last), grid=(pair...  68.8 us
    unnamed x169, local copies, waits for them, and re-layouts  34.3 us
    ppermute x11, starting transfers between devices, send(): return lax.ppermute(value, 'blk', pairs_of_places)  28.1 us
    ppermute x11, waiting for transfers between devices, send(): return lax.ppermute(value, 'blk', pairs_of_places)  14.1 us
  transfers between devices with their start and end apart: 11, of which 1 were waited for; matrix products, arithmetic and copies ran while one was open for 8% of the time, Pallas kernels for 22%

profile of v2, /device:TPU:0, one launch (start us, length us, event | category | flops | bytes accessed | tf_op | source)
XLA Modules:
  0.0 583.2 jit_solution(1873330547936380305)
XLA Ops:
  1.5 4.2 multiply_sine_fusion
  22.4 14.0 %collective-permute-done.refs_0_ = bf16[768,768]{1,0:T(8,128)(2,1)S(1)} collective-permute-done((bf16[768,768]{1,0:T(8,128)(2,1)S(1)}, bf16[768,768]{1,0:T(8,128)(2,1)S(1)}, u32[]{:S(2)}, u32[]{:S(2)}) %collective-permute-start) | collective-permute-done | bytes 1179680 | tf_op jit(solution)/shard_map/ppermute | solution.py:507
  41.3 16.5 %attend.4 = (bf16[768,768]{1,0:T(8,128)(2,1)S(1)}, bf16[768,768]{1,0:T(8,128)(2,1)S(1)}, f32[768,768]{1,0:T(8,128)}, f32[6,2,768]{2,1,0:T(2,128)S(1)}, f32[6,2,768]{2,1,0:T(2,128)S(1)}) custom-call(bf16[768,768]{1,0:T(8,128)(2,1)S(1)} %multiply_convert_fusion.2.refs_0_, bf16[768,2304]{1,0:T(8,128)(2,1)} %refs_9_.7, bf16[768,2304]{1,0:T(8,128)(2,1)} %refs_9_.7, ...), custom_call_target="tpu_custom_call" | custom-call | flops 9059696640 | bytes 14155776 | tf_op jit(solution)/shard_map/attend/pallas_call | solution.py:179
  60.9 17.0 %attend.5 = (bf16[768,768]{1,0:T(8,128)(2,1)S(1)}, bf16[768,768]{1,0:T(8,128)(2,1)S(1)}, f32[768,768]{1,0:T(8,128)}, f32[6,2,768]{2,1,0:T(2,128)S(1)}, f32[6,2,768]{2,1,0:T(2,128)S(1)}) custom-call(bf16[768,768]{1,0:T(8,128)(2,1)S(1)} %collective-permute-done.refs_0_, bf16[768,2304]{1,0:T(8,128)(2,1)} %refs_9_.7, bf16[768,2304]{1,0:T(8,128)(2,1)} %refs_9_.7, ...), custom_call_target="tpu_custom_call" | custom-call | flops 9059696640 | bytes 14155776 | tf_op jit(solution)/shard_map/attend/pallas_call | solution.py:179
  80.9 17.0 %attend.6 = (bf16[768,768]{1,0:T(8,128)(2,1)S(1)}, bf16[768,768]{1,0:T(8,128)(2,1)S(1)}, f32[768,768]{1,0:T(8,128)}, f32[6,2,768]{2,1,0:T(2,128)S(1)}, f32[6,2,768]{2,1,0:T(2,128)S(1)}) custom-call(bf16[768,768]{1,0:T(8,128)(2,1)S(1)} %add.123.refs_0_, bf16[768,2304]{1,0:T(8,128)(2,1)} %refs_9_.7, bf16[768,2304]{1,0:T(8,128)(2,1)} %refs_9_.7, ...), custom_call_target="tpu_custom_call" | custom-call | flops 9059696640 | bytes 14155776 | tf_op jit(solution)/shard_map/attend/pallas_call | solution.py:179
  99.3 18.2 %attend.7 = (bf16[768,768]{1,0:T(8,128)(2,1)S(1)}, bf16[768,768]{1,0:T(8,128)(2,1)S(1)}, f32[768,768]{1,0:T(8,128)}, f32[6,2,768]{2,1,0:T(2,128)S(1)}, f32[6,2,7...) custom-call(bf16[768,768]{1,0:T(8,128)(2,1)S(1)} %add.119.refs_0_, bf16[768,2304]{1,0:T(8,128)(2,1)} %refs_9_.7, ...), custom_call_target="tpu_custom_call" | custom-call | flops 9059696640 | bytes 14155776 | tf_op jit(solution)/shard_map/attend/pallas_call | solution.py:179
  121.7 7.6 %multiply_convert_fusion = (bf16[768,3072]{1,0:T(8,128)(2,1)}, f32[768,3072]{1,0:T(8,128)}) fusion(f32[3072]{0:T(1024)S(1)} %copy-done.75, bf16[768,3072]{1,0:T(8,128)(2,1)S(1)} %bitcast.92, f32[768,768]{1,0:T(8,128)S(1)} %get-tuple-element.158, f32[768]{0:T(1024)S(1)} %copy-done.74, f32[768]{0:T(1024)S(1)} %add_rsqrt_fusion, ...), kind=kOutput, calls=%fused_computation.9 | convolution fusion | flops 3640393728 | bytes 21255168 | tf_op jit(solution)/shard_map/dot_general | solution.py:28
  129.3 10.6 %convert_reduce_fusion = (f32[3072]{0:T(1024)}, bf16[768,3072]{1,0:T(8,128)(2,1)}) fusion(f32[768,3072]{1,0:T(8,128)} %get-tuple-element.160, f32[3072]{0:T(1024)S(1)} %copy-done.75, bf16[3072,768]{1,0:T(8,128)(2,1)S(1)} %bitcast.94, f32[768,768]{1,0:T(8,128)S(1)} %copy-done.55), kind=kOutput, calls=%fused_computation.8 | convolution fusion | flops 3655136256 | bytes 21258240 | tf_op jit(solution)/shard_map/dot_general | solution.py:28
  140.0 7.2 %multiply_reduce_fusion = (f32[768]{0:T(1024)S(1)}, f32[768]{0:T(1024)S(1)}, f32[768]{0:T(1024)S(1)}, f32[768,768]{1,0:T(8,128)S(1)}) fusion(f32[768,768]{1,0:T(8,128)S(1)} %get-tuple-element.158, f32[768]{0:T(1024)S(1)} %add_rsqrt_fusion, f32[768]{0:T(1024)S(1)} %broadcast_multiply_fusion.4, f32[768]{0:T(1024)S(1)} %copy-done.74, ...), kind=kOutput, calls=%fused_computation.16 | convolution fusion | flops 3628594944 | bytes 14174208 | tf_op jit(solution)/shard_map/dot_general | solution.py:28
  147.2 4.6 convolution_convert_fusion
  156.7 4.2 convolution_convert_fusion.1
  171.0 26.0 %attend_back.4 = (bf16[768,768]{1,0:T(8,128)(2,1)S(1)}, bf16[768,768]{1,0:T(8,128)(2,1)S(1)}, f32[768,768]{1,0:T(8,128)}, bf16[768,768]{1,0:T(8,128)(2,1)S(1)}) custom-call(bf16[768,768]{1,0:T(8,128)(2,1)S(1)} %copy-done.35, bf16[768,768]{1,0:T(8,128)(2,1)} %copy-done.36, bf16[768,768]{1,0:T(8,128)(2,1)} %copy-done.27, bf16[768,768]{1,0:T(8,128)(2,1)} %copy-done.64, ...), custom_call_target="tpu_custom_call" | custom-call | flops 18119393280 | bytes 14155776 | tf_op jit(solution)/shard_map/attend_back/pallas_call | solution.py:285
  199.1 10.6 %collective-permute-start.5 = (bf16[768,768]{1,0:T(8,128)(2,1)S(1)}, bf16[768,768]{1,0:T(8,128)(2,1)}, u32[]{:S(2)}, u32[]{:S(2)}) collective-permute-start(bf16[768,768]{1,0:T(8,128)(2,1)S(1)} %get-tuple-element.79), channel_id=1, source_target_pairs={{0,1},{3,2},{4,5},{7,6},{8,9},{11,10},{12,13},{15,14},{16,17},{19,... | collective-permute-start | bytes 3538952 | tf_op jit(solution)/shard_map/ppermute | solution.py:507
  210.5 26.2 %attend_back.5 = (bf16[768,768]{1,0:T(8,128)(2,1)S(1)}, bf16[768,768]{1,0:T(8,128)(2,1)S(1)}, f32[768,768]{1,0:T(8,128)}, bf16[768,768]{1,0:T(8,128)(2,1)S(1)}) custom-call(bf16[768,768]{1,0:T(8,128)(2,1)S(1)} %copy-done.32, bf16[768,768]{1,0:T(8,128)(2,1)} %copy-done.33, bf16[768,768]{1,0:T(8,128)(2,1)} %copy-done.27, bf16[768,768]{1,0:T(8,128)(2,1)} %copy-done.64, ...), custom_call_target="tpu_custom_call" | custom-call | flops 18119393280 | bytes 14155776 | tf_op jit(solution)/shard_map/attend_back/pallas_call | solution.py:285
  244.2 9.7 %convolution_add_fusion.1 = f32[768,768]{1,0:T(8,128)} fusion(f32[768,768]{1,0:T(8,128)} %copy-done.48, bf16[768,3072]{1,0:T(8,128)(2,1)} %get-tuple-element.159, bf16[3072,768]{1,0:T(8,128)(2,1)} %param.21), kind=kOutput, calls=%fused_computation.40 | convolution fusion | flops 3624468480 | bytes 14155776 | tf_op jit(solution)/shard_map/dot_general | solution.py:28
  259.5 26.3 %attend_back.6 = (bf16[768,768]{1,0:T(8,128)(2,1)S(1)}, bf16[768,768]{1,0:T(8,128)(2,1)S(1)}, f32[768,768]{1,0:T(8,128)}, bf16[768,768]{1,0:T(8,128)(2,1)S(1)}) custom-call(bf16[768,768]{1,0:T(8,128)(2,1)S(1)} %copy-done.29, bf16[768,768]{1,0:T(8,128)(2,1)} %copy-done.30, bf16[768,768]{1,0:T(8,128)(2,1)} %copy-done.27, bf16[768,768]{1,0:T(8,128)(2,1)} %copy-done.64, ...), custom_call_target="tpu_custom_call" | custom-call | flops 18119393280 | bytes 14155776 | tf_op jit(solution)/shard_map/attend_back/pallas_call | solution.py:285
  299.0 27.4 %attend_back.7 = (bf16[768,768]{1,0:T(8,128)(2,1)S(1)}, bf16[768,768]{1,0:T(8,128)(2,1)S(1)}, bf16[768,768]{1,0:T(8,128)(2,1)S(1)}, f32[768,768]{1,0:T(8,128)}) custom-call(bf16[768,768]{1,0:T(8,128)(2,1)S(1)} %copy-done.38, bf16[768,768]{1,0:T(8,128)(2,1)} %copy-done.39, bf16[768,768]{1,0:T(8,128)(2,1)} %copy-done.27, bf16[768,768]{1,0:T(8,128)(2,1)} %copy-done.64, ...), custom_call_target="tpu_custom_call" | custom-call | flops 18119393280 | bytes 14155776 | tf_op jit(solution)/shard_map/attend_back/pallas_call | solution.py:285
  348.2 4.2 multiply_reduce_fusion.1
  353.1 180.5 %sum_gradients.1 = (bf16[1536,768]{1,0:T(8,128)(2,1)}, bf16[1536,768]{1,0:T(8,128)(2,1)}, bf16[1536,768]{1,0:T(8,128)(2,1)}, bf16[1536,768]{1,0:T(8,128)(2,1)}, ...) custom-call(bf16[1536,768]{1,0:T(8,128)(2,1)} %get-tuple-element.149, ...), custom_call_target="tpu_custom_call" | custom-call | tf_op jit(solution)/shard_map/sum_gradients/pallas_call | solution.py:484
  546.3 4.4 maximum_convert_fusion.1
  550.7 8.1 %copy.54 = f32[768,2304]{1,0:T(8,128)} copy(f32[768,2304]{0,1:T(8,128)} %maximum_convert_fusion.1) | data formatting | bytes 14155776
  558.8 6.1 %convert_bitcast_fusion = f32[768,3072]{0,1:T(8,128)} fusion(bf16[1536,768]{1,0:T(8,128)(2,1)} %get-tuple-element.114, bf16[1536,768]{1,0:T(8,128)(2,1)S(1)} %copy-done.54), kind=kLoop, calls=%fused_computation.7 | loop fusion | flops 9437184 | bytes 14155776 | tf_op jit(solution)/shard_map/convert_element_type | solution.py:639
  565.0 9.7 %copy.56 = f32[768,3072]{1,0:T(8,128)} copy(f32[768,3072]{0,1:T(8,128)} %convert_bitcast_fusion) | data formatting | bytes 18874368
  574.7 6.3 %maximum_convert_fusion = f32[3072,768]{1,0:T(8,128)} fusion(bf16[1536,768]{1,0:T(8,128)(2,1)} %get-tuple-element.116, bf16[1536,768]{1,0:T(8,128)(2,1)S(1)} %copy-done.53), kind=kLoop, calls=%fused_computation.13 | loop fusion | flops 9437184 | bytes 14155776 | tf_op jit(solution)/shard_map/convert_element_type | solution.py:641
  (251 shorter events, 106.7 us)
Async XLA Ops:
  0.6 117.0 %copy-start = (bf16[768,768]{1,0:T(8,128)(2,1)S(1)}, bf16[768,768]{1,0:T(8,128)(2,1)}, u32[]{:S(2)}) copy-start(bf16[768,768]{1,0:T(8,128)(2,1)} %param.17) | copy-start | bytes 3538948
  6.5 30.7 %copy-start.71 = (s32[3072]{0:T(1024)S(1)}, s32[3072]{0:T(1024)}, u32[]{:S(2)}) copy-start(s32[3072]{0:T(1024)} %param.14) | copy-start | bytes 36868
  7.4 33.8 %copy-start.4 = (bf16[768,768]{1,0:T(8,128)(2,1)}, bf16[768,768]{1,0:T(8,128)(2,1)S(1)}, u32[]{:S(2)}) copy-start(bf16[768,768]{1,0:T(8,128)(2,1)S(1)} %multiply_convert_fusion.2.refs_0_) | copy-start | bytes 3538948
  7.4 29.0 %collective-permute-start = (bf16[768,768]{1,0:T(8,128)(2,1)S(1)}, bf16[768,768]{1,0:T(8,128)(2,1)S(1)}, u32[]{:S(2)}, u32[]{:S(2)}) collective-permute-start(bf16[768,768]{1,0:T(8,128)(2,1)S(1)} %multiply_convert_fusion.2.refs_0_), channel_id=1, source_target_pairs={{0,1},{1,0},{2,3},{3,2},{4,5},{5,4},{6,7},{7,6},{8,9},{9,8},{10,11... | collective-permute-start | bytes 3538952 | tf_op jit(solution)/shard_map/ppermute | solution.py:507
  10.5 29.5 %collective-permute-start.3 = (bf16[768,768]{1,0:T(8,128)(2,1)S(1)}, bf16[768,768]{1,0:T(8,128)(2,1)}, u32[]{:S(2)}, u32[]{:S(2)}) collective-permute-start(bf16[768,768]{1,0:T(8,128)(2,1)S(1)} %multiply_convert_fusion.2.refs_0_), channel_id=1, source_target_pairs={{1,2},{2,1},{5,6},{6,5},{9,10},{10,9},{13,14},{14,13},{17,18},{18,... | collective-permute-start | bytes 3538952 | tf_op jit(solution)/shard_map/ppermute | solution.py:507
  36.4 24.4 %copy-start.21 = (bf16[768,768]{1,0:T(8,128)(2,1)}, bf16[768,768]{1,0:T(8,128)(2,1)S(1)}, u32[]{:S(2)}) copy-start(bf16[768,768]{1,0:T(8,128)(2,1)S(1)} %collective-permute-done.refs_0_) | copy-start | bytes 3538948
  36.4 22.9 %collective-permute-start.1 = (bf16[768,768]{1,0:T(8,128)(2,1)S(1)}, bf16[768,768]{1,0:T(8,128)(2,1)S(1)}, u32[]{:S(2)}, u32[]{:S(2)}) collective-permute-start(bf16[768,768]{1,0:T(8,128)(2,1)S(1)} %collective-permute-done.refs_0_), channel_id=1, source_target_pairs={{1,2},{2,1},{5,6},{6,5},{9,10},{10,9},{13,14},{14,13},{17,18},{18,... | collective-permute-start | bytes 3538952 | tf_op jit(solution)/shard_map/ppermute | solution.py:507
  40.0 41.0 %copy-start.27 = (bf16[768,768]{1,0:T(8,128)(2,1)}, bf16[768,768]{1,0:T(8,128)(2,1)S(1)}, u32[]{:S(2)}) copy-start(bf16[768,768]{1,0:T(8,128)(2,1)S(1)} %convolution_convert_fusion.5.refs_3_.refs_2_) | copy-start | bytes 3538948
  40.0 39.0 %collective-permute-start.4 = (bf16[768,768]{1,0:T(8,128)(2,1)}, bf16[768,768]{1,0:T(8,128)(2,1)S(1)}, u32[]{:S(2)}, u32[]{:S(2)}) collective-permute-start(bf16[768,768]{1,0:T(8,128)(2,1)} %collective-permute-done.3), channel_id=1, source_target_pairs={{1,0},{2,3},{5,4},{6,7},{9,8},{10,11},{13,12},{14,15},{17,16},{18,... | collective-permute-start | bytes 3538952 | tf_op jit(solution)/shard_map/ppermute | solution.py:507
  59.2 40.1 %copy-start.16 = (s32[768,1]{1,0:T(8,128)}, s32[768,1]{1,0:T(8,128)S(1)}, u32[]{:S(2)}) copy-start(s32[768,1]{1,0:T(8,128)S(1)} %broadcast_in_dim.15.refs_4_.refs_6_) | copy-start | bytes 9220
  59.4 39.6 %collective-permute-start.2 = (bf16[768,768]{1,0:T(8,128)(2,1)S(1)}, bf16[768,768]{1,0:T(8,128)(2,1)S(1)}, u32[]{:S(2)}, u32[]{:S(2)}) collective-permute-start(bf16[768,768]{1,0:T(8,128)(2,1)S(1)} %collective-permute-done.1), channel_id=1, source_target_pairs={{1,0},{2,3},{5,4},{6,7},{9,8},{10,11},{13,12},{14,15},{17,16},{18,... | collective-permute-start | bytes 3538952 | tf_op jit(solution)/shard_map/ppermute | solution.py:507
  119.1 32.8 %copy-start.48 = (f32[768,768]{1,0:T(8,128)}, f32[768,768]{1,0:T(8,128)S(1)}, u32[]{:S(2)}) copy-start(f32[768,768]{1,0:T(8,128)S(1)} %get-tuple-element.158) | copy-start | bytes 7077892
  169.7 27.3 %copy-start.18 = (f32[6,2,768]{2,1,0:T(2,128)}, f32[6,2,768]{2,1,0:T(2,128)S(1)}, u32[]{:S(2)}) copy-start(f32[6,2,768]{2,1,0:T(2,128)S(1)} %reduce_sum.114.refs_5_) | copy-start | bytes 110596
  171.0 38.7 %copy-start.15 = (s32[768,1]{1,0:T(8,128)S(1)}, s32[768,1]{1,0:T(8,128)}, u32[]{:S(2)}) copy-start(s32[768,1]{1,0:T(8,128)} %copy-done.14) | copy-start | bytes 9220
  171.0 38.7 %copy-start.32 = (bf16[768,768]{1,0:T(8,128)(2,1)S(1)}, bf16[768,768]{1,0:T(8,128)(2,1)}, u32[]{:S(2)}) copy-start(bf16[768,768]{1,0:T(8,128)(2,1)} %copy-done.31) | copy-start | bytes 3538948
  171.0 38.7 %copy-start.42 = (f32[6,2,768]{2,1,0:T(2,128)S(1)}, f32[6,2,768]{2,1,0:T(2,128)}, u32[]{:S(2)}) copy-start(f32[6,2,768]{2,1,0:T(2,128)} %copy-done.40) | copy-start | bytes 110596
  199.1 54.8 %collective-permute-start.5 = (bf16[768,768]{1,0:T(8,128)(2,1)S(1)}, bf16[768,768]{1,0:T(8,128)(2,1)}, u32[]{:S(2)}, u32[]{:S(2)}) collective-permute-start(bf16[768,768]{1,0:T(8,128)(2,1)S(1)} %get-tuple-element.79), channel_id=1, source_target_pairs={{0,1},{3,2},{4,5},{7,6},{8,9},{11,10},{12,13},{15,14},{16,17},{19,... | collective-permute-start | bytes 3538952 | tf_op jit(solution)/shard_map/ppermute | solution.py:507
  255.5 35.3 %collective-permute-start.6 = (bf16[768,768]{1,0:T(8,128)(2,1)S(1)}, bf16[768,768]{1,0:T(8,128)(2,1)S(1)}, u32[]{:S(2)}, u32[]{:S(2)}) collective-permute-start(bf16[768,768]{1,0:T(8,128)(2,1)S(1)} %add_convert_fusion.4), channel_id=1, source_target_pairs={{1,2},{2,1},{5,6},{6,5},{9,10},{10,9},{13,14},{14,13},{17,18},{18,... | collective-permute-start | bytes 3538952 | tf_op jit(solution)/shard_map/ppermute | solution.py:507
  256.3 34.6 %collective-permute-start.7 = (bf16[768,768]{1,0:T(8,128)(2,1)S(1)}, bf16[768,768]{1,0:T(8,128)(2,1)S(1)}, u32[]{:S(2)}, u32[]{:S(2)}) collective-permute-start(bf16[768,768]{1,0:T(8,128)(2,1)S(1)} %get-tuple-element.86), channel_id=1, source_target_pairs={{0,1},{3,2},{4,5},{7,6},{8,9},{11,10},{12,13},{15,14},{16,17},{19,... | collective-permute-start | bytes 3538952 | tf_op jit(solution)/shard_map/ppermute | solution.py:507
  259.5 26.3 %copy-start.22 = (bf16[768,768]{1,0:T(8,128)(2,1)S(1)}, bf16[768,768]{1,0:T(8,128)(2,1)}, u32[]{:S(2)}) copy-start(bf16[768,768]{1,0:T(8,128)(2,1)} %copy-done.21) | copy-start | bytes 3538948
  292.2 55.9 %collective-permute-start.10 = (bf16[768,768]{1,0:T(8,128)(2,1)S(1)}, bf16[768,768]{1,0:T(8,128)(2,1)}, u32[]{:S(2)}, u32[]{:S(2)}) collective-permute-start(bf16[768,768]{1,0:T(8,128)(2,1)S(1)} %get-tuple-element.95), channel_id=1, source_target_pairs={{0,1},{3,2},{4,5},{7,6},{8,9},{11,10},{12,13},{15,14},{16,17},{19,... | collective-permute-start | bytes 3538952 | tf_op jit(solution)/shard_map/ppermute | solution.py:507
  296.0 52.0 %collective-permute-start.9 = (bf16[768,768]{1,0:T(8,128)(2,1)}, bf16[768,768]{1,0:T(8,128)(2,1)}, u32[]{:S(2)}, u32[]{:S(2)}) collective-permute-start(bf16[768,768]{1,0:T(8,128)(2,1)} %add_convert_fusion.2), channel_id=1, source_target_pairs={{1,0},{2,3},{5,4},{6,7},{9,8},{10,11},{13,12},{14,15},{17,16},{18,... | collective-permute-start | bytes 3538952 | tf_op jit(solution)/shard_map/ppermute | solution.py:507
  297.3 50.8 %collective-permute-start.8 = (bf16[768,768]{1,0:T(8,128)(2,1)}, bf16[768,768]{1,0:T(8,128)(2,1)}, u32[]{:S(2)}, u32[]{:S(2)}) collective-permute-start(bf16[768,768]{1,0:T(8,128)(2,1)} %add_convert_fusion.3), channel_id=1, source_target_pairs={{1,2},{2,1},{5,6},{6,5},{9,10},{10,9},{13,14},{14,13},{17,18},{18,... | collective-permute-start | bytes 3538952 | tf_op jit(solution)/shard_map/ppermute | solution.py:507
  299.0 29.5 %copy-start.5 = (bf16[768,768]{1,0:T(8,128)(2,1)S(1)}, bf16[768,768]{1,0:T(8,128)(2,1)}, u32[]{:S(2)}) copy-start(bf16[768,768]{1,0:T(8,128)(2,1)} %copy-done.4) | copy-start | bytes 3538948
  (70 other events, 364.3 us)

commit v3 on v2

--- a/solution.py
+++ b/solution.py
@@ -304,6 +304,8 @@
 
 MESH = pl.DeviceIdType.MESH
 TURNS = ((0, 1, 2), (0, 2, 1))
+STEPS = 5
+ADD_ROWS = 48
 
 
 def place_bits(turn):
@@ -329,78 +331,91 @@
     )
 
 
-def add_rows(total, start, term, rows, step):
-    @pl.loop(0, rows // step)
+def part_of(row, rows, column, columns):
+    row = row if isinstance(row, int) else pl.multiple_of(row, 16)
+    column = column if isinstance(column, int) else pl.multiple_of(column, PAIR)
+    return pl.ds(row, rows), pl.ds(column, columns)
+
+
+def add_block(total, term, row=0, column=0):
+    rows, columns = term.shape
+
+    @pl.loop(0, rows // ADD_ROWS)
     def _(index):
-        here = pl.ds(pl.multiple_of(start + index * step, 16), step)
-        there = pl.ds(pl.multiple_of(index * step, 16), step)
+        here = part_of(row + index * ADD_ROWS, ADD_ROWS, column, columns)
+        there = part_of(index * ADD_ROWS, ADD_ROWS, 0, columns)
         total[here] = (total[here].astype(WIDE) + term[there].astype(WIDE)).astype(total.dtype)
 
 
+def halves(shape, axes):
+    shapes = []
+    for axis in axes:
+        shape = (shape[0] // 2, shape[1]) if axis == "r" else (shape[0], shape[1] // 2)
+        shapes.append(shape)
+    return shapes
+
+
 class Sum:
-    def __init__(self, turn, term, result, total, arrived, sems, local_sems):
+    def __init__(self, turn, axes, corner, shape, term, result, total, arrived, sems, local_sems):
         self.term, self.result, self.total, self.arrived = term, result, total, arrived
         self.sems, self.local_sems = sems, local_sems
         self.steps = place_bits(turn)
-        self.count = len(self.steps)
-        rows = total.shape[0]
-        self.first = self.steps[0][0] * rows
-        self.keep = [(0, rows)]
-        for mine, _ in self.steps[1:]:
-            start, size = self.keep[-1]
-            self.keep.append((start + mine * (size // 2), size // 2))
-        self.block = min(rows, self.keep[-1][1])
-        self.pending = {}
-
-    def _rows(self, ref, start, size):
-        return ref.at[pl.ds(pl.multiple_of(start, 16), size)]
+        self.shapes = halves(shape, axes)
+        self.kept, self.left = [], []
+        row, column = corner
+        for axis, (rows, columns), (mine, _) in zip(axes, self.shapes, self.steps):
+            down, across = (rows, 0) if axis == "r" else (0, columns)
+            self.left.append((row + (1 - mine) * down, rows, column + (1 - mine) * across, columns))
+            row, column = row + mine * down, column + mine * across
+            self.kept.append((row, rows, column, columns))
+
+    def inside(self, place):
+        row, rows, column, columns = place
+        return part_of(row - self.kept[0][0], rows, column - self.kept[0][2], columns)
 
     def load(self):
-        source = self._rows(self.term, self.first, self.total.shape[0])
-        return pltpu.make_async_copy(source, self.total, self.local_sems.at[0])
+        return pltpu.make_async_copy(
+            self.term.at[part_of(*self.kept[0])], self.total, self.local_sems.at[0]
+        )
 
     def store(self):
-        start, size = self.keep[-1]
-        source = self._rows(self.total, start, size)
-        target = self._rows(self.result, self.first + start, size)
-        return pltpu.make_async_copy(source, target, self.local_sems.at[1])
+        return pltpu.make_async_copy(
+            self.total.at[self.inside(self.kept[-1])],
+            self.result.at[part_of(*self.kept[-1])],
+            self.local_sems.at[1],
+        )
 
     def gather(self, step):
-        mine, device = self.steps[step]
-        start, size = self.keep[step]
-        if step == 0:
-            rows = self.total.shape[0]
-            source = self._rows(self.term, (1 - mine) * rows, rows)
+        place = self.left[step]
+        source = self.term.at[part_of(*place)] if step == 0 else self.total.at[self.inside(place)]
+        return remote(source, self.arrived[step], self.sems, step, self.steps[step][1])
+
+    def spread(self, step):
+        here = self.result.at[part_of(*self.kept[step])]
+        return remote(here, here, self.sems, STEPS + step, self.steps[step][1])
+
+    def start(self):
+        self.load().start()
+        self.gather(0).start()
+
+    def turn(self, tick):
+        if tick < STEPS:
+            if tick == 0:
+                self.load().wait()
+            self.gather(tick).wait()
+            row, _, column, _ = self.kept[tick]
+            add_block(self.total, self.arrived[tick], row - self.kept[0][0], column - self.kept[0][2])
+            if tick + 1 < STEPS:
+                self.gather(tick + 1).start()
+            else:
+                self.store().start()
+                self.store().wait()
+                self.spread(STEPS - 1).start()
         else:
-            upper, _ = self.keep[step - 1]
-            source = self._rows(self.total, upper + (1 - mine) * size, size)
-        return remote(source, self.arrived[step], self.sems, step, device)
-
-    def start_sum(self, step):
-        if step == 0:
-            self.load().start()
-        self.gather(step).start()
-
-    def finish_sum(self, step):
-        if step == 0:
-            self.load().wait()
-        self.gather(step).wait()
-        start, size = self.keep[step]
-        add_rows(self.total, start, self.arrived[step], size, self.block)
-
-    def spread(self, step):
-        start, size = self.keep[step]
-        here = self._rows(self.result, self.first + start, size)
-        return remote(here, here, self.sems, self.count + step, self.steps[step][1])
-
-    def start_spread(self, step):
-        if step == self.count - 1:
-            self.store().start()
-            self.store().wait()
-        self.spread(step).start()
-
-    def finish_spread(self, step):
-        self.spread(step).wait()
+            step = 2 * STEPS - 1 - tick
+            self.spread(step).wait()
+            if step:
+                self.spread(step - 1).start()
 
 
 def greet():
@@ -413,32 +428,212 @@
     pl.semaphore_wait(barrier, len(devices))
 
 
-def arrivals(rows, lanes, steps=5):
-    return [pltpu.VMEM((rows >> (step + 1), lanes), LOW) for step in range(steps)]
-
-
-def sum_kernel(shapes, *refs):
-    count = len(shapes)
-    terms, small_in = refs[:count], refs[count]
-    results, small_out = refs[count + 1 : 2 * count + 1], refs[2 * count + 1]
-    refs = refs[2 * count + 2 :]
-    totals = refs[:count]
-    arrived = [refs[count + 5 * index : count + 5 * index + 5] for index in range(count)]
-    small_arrived, sends, receives, locals_, small_sends, small_receives = refs[6 * count :]
+PARTS = (
+    ("down", (0, 0), (1536, 768), "rrrrr", 0, (2, 6, 9, 12, 14, 16, 18, 20, 22, 23)),
+    ("down", (1536, 0), (1536, 768), "rrrrr", 1, (2, 6, 9, 12, 14, 16, 18, 20, 22, 23)),
+    ("up", (0, 0), (768, 1536), "rrrcc", 0, (3, 8, 11, 13, 15, 17, 19, 21, 24, 24)),
+    ("up", (0, 1536), (768, 1536), "rrrcc", 1, (3, 8, 11, 13, 15, 17, 19, 21, 24, 24)),
+    ("out", (0, 0), (768, 768), "rrrrc", 0, (4, 9, 11, 13, 15, 17, 19, 21, 23, 24)),
+    ("qkv", (0, 0), (768, 512), "rrrrc", 0, None),
+    ("qkv", (0, 512), (768, 512), "rrrrc", 1, None),
+    ("qkv", (0, 1024), (768, 512), "rrrrc", 0, None),
+    ("qkv", (0, 1536), (768, 768), "rrrrc", 1, None),
+)
+
+
+def gradient_kernel(*refs):
+    keys, values, shards = refs[:4], refs[4:8], refs[8:12]
+    q_ref, grad_ref, lse_ref, dots_ref, clips, query_clip, w_ref = refs[12:19]
+    down_in, up_in, out_in, small_in = refs[19:23]
+    down_out, up_out, out_out, qkv_out, small_out, input_out = refs[23:29]
+    refs = refs[29:]
+    kv_slot, a_slot, dq_sum, dk_sum, dv_sum, dk_all, dv_all, grad_k, grad_v, parts = refs[:10]
+    far, mid_2, mid_3, last_1, last_3, qkv_term, clip_slot, small_arrived = refs[10:18]
+    input_sum = dq_sum
+    kv_sems, a_sem, line_sends, line_receives, sends, receives, locals_ = refs[18:25]
+    small_sends, small_receives, out_sem, clip_sem = refs[25:29]
+    refs = refs[29:]
+    rows, width = q_ref.shape
+    pairs = width // PAIR
+    pieces = 4 * pairs
+    group, place = lax.axis_index("dp"), lax.axis_index("blk")
+    near = (group, place + 1 - 2 * (place % 2))
+    across = (group, 3 - place)
+    at_end = place % 3 == 0
+
+    arrays = {
+        "down": (down_in, down_out),
+        "up": (up_in, up_out),
+        "out": (out_in, out_out),
+        "qkv": (qkv_term, qkv_out),
+    }
+    sums = []
+    for index, (name, corner, shape, axes, turn, _) in enumerate(PARTS):
+        total, arrived = refs[0], refs[1:STEPS]
+        refs = refs[STEPS:]
+        if name == "down":
+            arrived = (qkv_term.at[:, pl.ds(index * width, width)], *arrived)
+        else:
+            arrived, refs = (refs[0], *arrived), refs[1:]
+        sums.append(
+            Sum(
+                turn,
+                axes,
+                corner,
+                shape,
+                *arrays[name],
+                total,
+                arrived,
+                (sends.at[index], receives.at[index]),
+                locals_.at[index],
+            )
+        )
+    early = [(each, part[5]) for each, part in zip(sums, PARTS) if part[5] is not None]
+    late = [each for each, part in zip(sums, PARTS) if part[5] is None]
+
+    line_sems = (line_sends, line_receives)
+    send_far = remote(parts.at[0], far, line_sems, 0, near)
+    send_mid_2 = remote(parts.at[1], mid_2, line_sems, 1, near)
+    send_mid_3 = remote(parts.at[0], mid_3, line_sems, 2, across)
+    send_last_1 = remote(parts.at[1], last_1, line_sems, 3, across)
+    send_last_2 = remote(parts.at[2], far, line_sems, 4, near)
+    send_last_3 = remote(parts.at[2], last_3, line_sems, 5, near)
+
+    def pair_columns(pair):
+        return pl.ds(pl.multiple_of(pair * PAIR, PAIR), PAIR)
+
+    def kv_copies(shard, pair, slot):
+        return [
+            pltpu.make_async_copy(
+                source[shard].at[:, pair_columns(pair)], kv_slot.at[slot, side], kv_sems.at[slot, side]
+            )
+            for side, source in enumerate((keys, values))
+        ]
+
+    def a_copy(shard):
+        return pltpu.make_async_copy(shards[shard], a_slot, a_sem)
+
+    def clip_copy(turn):
+        source = clips.at[pl.ds(pl.multiple_of(turn * rows, 8), rows)]
+        return pltpu.make_async_copy(source, clip_slot, clip_sem)
+
+    def of_pairs(stack):
+        return jnp.concatenate([stack[pair] for pair in range(pairs)], axis=1)
+
+    for copy in kv_copies(3, 0, 0):
+        copy.start()
     greet()
-    sums = [
-        Sum(
-            index % 2,
-            terms[index],
-            results[index],
-            totals[index],
-            arrived[index],
-            (sends.at[index], receives.at[index]),
-            locals_.at[index],
-        )
-        for index in range(count)
-    ]
+    for each, _ in early:
+        each.start()
+    dq_sum[...] = jnp.zeros_like(dq_sum)
+    grad_k[...] = jnp.zeros_like(grad_k)
+    grad_v[...] = jnp.zeros_like(grad_v)
     small_out[...] = small_in[...]
+
+    def weight_terms(d_query):
+        a_copy(0).wait()
+        d_key, d_value = of_pairs(dk_all), of_pairs(dv_all)
+        part = dot(d_key, w_ref[:, width : 2 * width], NT) + dot(d_value, w_ref[:, 2 * width :], NT)
+        if d_query is not None:
+            part = part + dot(d_query, w_ref[:, :width], NT)
+        small_out[:1] += jnp.sum(part * a_slot[...].astype(WIDE), axis=0, keepdims=True)
+        grad_k[...] += dot(a_slot[...], d_key, TN)
+        grad_v[...] += dot(a_slot[...], d_value, TN)
+        return part
+
+    @pl.loop(0, pieces)
+    def _(piece):
+        turn, pair, slot = piece // pairs, piece % pairs, piece % 2
+
+        def at(when, *actions, also=None):
+            @pl.when(piece == when if also is None else jnp.logical_and(piece == when, also))
+            def _():
+                for action in actions:
+                    action()
+
+        for shard in range(4):
+            following = piece + 1
+
+            @pl.when(jnp.logical_and(following // pairs == 3 - shard, following < pieces))
+            def _():
+                for copy in kv_copies(shard, following % pairs, following % 2):
+                    copy.start()
+
+            at((3 - shard) * pairs + 1, lambda: a_copy(shard).start())
+        for when in range(pieces):
+            ends = [
+                functools.partial(each.turn, tick)
+                for tick in range(2 * STEPS)
+                for each, ticks in early
+                if ticks[tick] == when
+            ]
+            if ends:
+                at(when, *ends)
+        at_middle = jnp.logical_not(at_end)
+        at(pairs, send_far.start, also=at_end)
+        at(2 * pairs, send_far.wait_send, send_mid_2.start, also=at_end)
+        at(
+            2 * pairs + 1,
+            send_far.wait_recv,
+            lambda: add_block(parts.at[0], far),
+            send_mid_3.start,
+            also=at_middle,
+        )
+        at(3 * pairs, send_mid_2.wait_send, send_last_3.start, also=at_end)
+        at(
+            3 * pairs + 2,
+            send_mid_2.wait_recv,
+            lambda: add_block(parts.at[1], mid_2),
+            send_last_1.start,
+            send_mid_3.wait,
+            lambda: add_block(parts.at[2], mid_3),
+            send_last_2.start,
+            also=at_middle,
+        )
+
+        @pl.when(pair == 0)
+        def _():
+            clip_copy(turn).start()
+            clip_copy(turn).wait()
+
+        for copy in kv_copies(0, pair, slot):
+            copy.wait()
+        columns = pair_columns(pair)
+
+        def add(head, start, stop, dq, dk, dv):
+            lanes = slice(head * HEAD, (head + 1) * HEAD)
+            if start == 0:
+                dv_sum[lanes], dk_sum[lanes] = dv, dk
+            else:
+                dv_sum[lanes] += dv
+                dk_sum[lanes] += dk
+            at_lanes = pl.ds(pl.multiple_of(pair * PAIR + head * HEAD, HEAD), HEAD)
+            dq_sum[at_lanes, start:stop] += dq
+
+        backward_pair(
+            kv_slot[slot, 0],
+            kv_slot[slot, 1],
+            q_ref[:, columns],
+            grad_ref[columns, :],
+            lse_ref.at[pair],
+            dots_ref.at[pair],
+            clip_slot[...],
+            query_clip[...],
+            add,
+        )
+        dk_all[pair] = (dk_sum[...] * SCALE).T.astype(LOW)
+        dv_all[pair] = dv_sum[...].T.astype(LOW)
+
+        @pl.when(jnp.logical_and(pair == pairs - 1, turn < 3))
+        def _():
+            parts[turn] = weight_terms(None).astype(LOW)
+
+    d_query = (dq_sum[...] * SCALE).T.astype(LOW)
+    input_sum[...] = weight_terms(d_query)
+    qkv_term[:, :width] = dot(a_slot[...], d_query, TN).astype(LOW)
+    qkv_term[:, width : 2 * width] = grad_k[...].astype(LOW)
+    qkv_term[:, 2 * width :] = grad_v[...].astype(LOW)
+
     small_steps = place_bits(0)
 
     def small(step):
@@ -446,53 +641,104 @@
             small_out, small_arrived.at[step], (small_sends, small_receives), step, small_steps[step][1]
         )
 
-    for each in sums:
-        each.start_sum(0)
-    for step in range(5):
-        small(step).start()
-        for each in sums:
-            each.finish_sum(step)
-            if step < 4:
-                each.start_sum(step + 1)
-            else:
-                each.start_spread(step)
-        small(step).wait()
-        small_out[...] += small_arrived[step]
-    for step in reversed(range(5)):
-        for each in sums:
-            each.finish_spread(step)
-            if step:
-                each.start_spread(step - 1)
-
-
-def sum_call(terms, small):
-    shapes = [term.shape for term in terms]
-    count = len(shapes)
+    for each in late:
+        each.start()
+    for each, ticks in early:
+        for tick in range(2 * STEPS):
+            if ticks[tick] == pieces:
+                each.turn(tick)
+
+    @pl.when(at_end)
+    def _():
+        send_last_3.wait_send()
+        send_last_2.wait_recv()
+        add_block(input_sum, far)
+
+    @pl.when(jnp.logical_not(at_end))
+    def _():
+        send_last_1.wait()
+        send_last_2.wait_send()
+        send_last_3.wait_recv()
+        add_block(input_sum, last_1)
+        add_block(input_sum, last_3)
+
+    store = pltpu.make_async_copy(input_sum, input_out, out_sem)
+    store.start()
+    for tick in range(2 * STEPS):
+        if tick < STEPS:
+            small(tick).start()
+        for each in late:
+            each.turn(tick)
+        if tick < STEPS:
+            small(tick).wait()
+            small_out[...] += small_arrived[tick]
+    store.wait()
+
+
+def gradient_call(
+    keys, values, shards, query, grad_t, lse, row_dots, clips, query_clip, w_qkv, grad_down, grad_up, grad_out, small
+):
+    rows, width = query.shape
+    pairs = width // PAIR
     anywhere = pl.BlockSpec(memory_space=pl.ANY)
     inside = pl.BlockSpec(memory_space=pltpu.VMEM)
-    scratch = [pltpu.VMEM((rows // 2, lanes), LOW) for rows, lanes in shapes]
-    for rows, lanes in shapes:
-        scratch += arrivals(rows, lanes)
+    square = (rows, width)
+    scratch = [
+        pltpu.VMEM((2, 2, rows, PAIR), LOW),
+        pltpu.VMEM(square, LOW),
+        pltpu.VMEM((width, rows), WIDE),
+        pltpu.VMEM((PAIR, rows), WIDE),
+        pltpu.VMEM((PAIR, rows), WIDE),
+        pltpu.VMEM((pairs, rows, PAIR), LOW),
+        pltpu.VMEM((pairs, rows, PAIR), LOW),
+        pltpu.VMEM((width, width), WIDE),
+        pltpu.VMEM((width, width), WIDE),
+        pltpu.VMEM((3, *square), LOW),
+    ]
+    scratch += [pltpu.VMEM(square, LOW)] * 5
     scratch += [
-        pltpu.VMEM((5, *small.shape), WIDE),
-        pltpu.SemaphoreType.DMA((count, 10)),
-        pltpu.SemaphoreType.DMA((count, 10)),
-        pltpu.SemaphoreType.DMA((count, 2)),
-        pltpu.SemaphoreType.DMA((5,)),
-        pltpu.SemaphoreType.DMA((5,)),
+        pltpu.VMEM((width, 3 * width), LOW),
+        pltpu.VMEM((rows, 1), clips.dtype),
+        pltpu.VMEM((STEPS, *small.shape), WIDE),
+        pltpu.SemaphoreType.DMA((2, 2)),
+        pltpu.SemaphoreType.DMA,
+        pltpu.SemaphoreType.DMA((6,)),
+        pltpu.SemaphoreType.DMA((6,)),
+        pltpu.SemaphoreType.DMA((len(PARTS), 2 * STEPS)),
+        pltpu.SemaphoreType.DMA((len(PARTS), 2 * STEPS)),
+        pltpu.SemaphoreType.DMA((len(PARTS), 2)),
+        pltpu.SemaphoreType.DMA((STEPS,)),
+        pltpu.SemaphoreType.DMA((STEPS,)),
+        pltpu.SemaphoreType.DMA,
+        pltpu.SemaphoreType.DMA,
     ]
+    for name, _, shape, axes, _, _ in PARTS:
+        shapes = halves(shape, axes)
+        scratch += [pltpu.VMEM(each, LOW) for each in (shapes[0], *shapes[1:])]
+        if name != "down":
+            scratch.append(pltpu.VMEM(shapes[0], LOW))
+    like = lambda array: jax.ShapeDtypeStruct(array.shape, array.dtype)
     return pl.pallas_call(
-        functools.partial(sum_kernel, shapes),
-        in_specs=[anywhere] * count + [inside],
-        out_specs=[anywhere] * count + [inside],
-        out_shape=[jax.ShapeDtypeStruct(shape, LOW) for shape in shapes]
-        + [jax.ShapeDtypeStruct(small.shape, WIDE)],
+        gradient_kernel,
+        in_specs=[anywhere] * 12 + [inside] * 4 + [anywhere] + [inside] * 2 + [anywhere] * 3 + [inside],
+        out_specs=[anywhere] * 4 + [inside, anywhere],
+        out_shape=[
+            like(grad_down),
+            like(grad_up),
+            like(grad_out),
+            jax.ShapeDtypeStruct((width, 3 * width), LOW),
+            like(small),
+            jax.ShapeDtypeStruct(square, WIDE),
+        ],
         scratch_shapes=scratch,
-        name="sum_gradients",
+        name="gradients",
         compiler_params=pltpu.CompilerParams(
-            collective_id=1, has_side_effects=True, vmem_limit_bytes=60 * 2**20
+            collective_id=1, has_side_effects=True, vmem_limit_bytes=62 * 2**20
         ),
-    )(*terms, small)
+    )(
+        *keys, *values, *shards, query, grad_t, lse, row_dots, clips, query_clip, w_qkv,
+        grad_down, grad_up, grad_out, small,
+    )
 
 
 def on_device(
@@ -551,7 +797,7 @@
     grad_down = dot(z_low, dy_low, TN).astype(LOW)
     d_gelu = dot(dy_low, w_down, NT)
     d_pre = (d_gelu * (cumulative + pre_act * density)).astype(LOW)
-    grad_up_t = dot(d_pre, b_low, TN).astype(LOW)
+    grad_up = dot(b_low, d_pre, TN).astype(LOW)
     grad_bias_up = jnp.sum(d_pre.astype(WIDE), axis=0)
     d_normed = dot(d_pre, w_up, NT)
     grad_gain_mlp = jnp.sum(d_normed * normed_mlp, axis=0)
@@ -562,6 +808,37 @@
     row_dots = jnp.sum(
         (d_attn_t.astype(WIDE) * attended).reshape(pairs, 2, HEAD, rows), axis=2
     )
+
+    if groups == 8 and rows == width:
+        small = jnp.concatenate([jnp.zeros_like(gain_attn), grad_gain_mlp, grad_bias_up])
+        sum_down, sum_up, sum_out, sum_qkv, sum_small, d_normed_attn = gradient_call(
+            keys,
+            values,
+            shards,
+            query,
+            d_attn_t,
+            lse,
+            row_dots,
+            jnp.concatenate(clips[::-1], axis=0),
+            query_clip,
+            w_qkv,
+            grad_down,
+            grad_up,
+            grad_out,
+            jnp.pad(small.reshape(6, width), ((0, 2), (0, 0))),
+        )
+        input_grad = d_resid + norm_back(d_normed_attn * gain_attn, normed_attn, inverse_attn)
+        return (
+            outputs,
+            input_grad,
+            sum_small[0] / gain_attn,
+            sum_qkv.astype(WIDE),
+            sum_out.astype(WIDE),
+            sum_small[1],
+            sum_up.astype(WIDE),
+            sum_small[2:6].reshape(-1),
+            sum_down.astype(WIDE),
+        )
 
     everywhere = ("dp", "blk")
 
@@ -612,23 +889,9 @@
     grad_gain_attn = jnp.sum(d_normed_attn * normed_attn, axis=0)
     input_grad = d_resid + norm_back(d_normed_attn * gain_attn, normed_attn, inverse_attn)
     small = jnp.concatenate([grad_gain_attn, grad_gain_mlp, grad_bias_up])
-    if groups == 8:
-        stack = lambda matrix: matrix.reshape(width, pairs, PAIR).swapaxes(0, 1).reshape(-1, PAIR)
-        unstack = lambda matrix: matrix.reshape(pairs, width, PAIR).swapaxes(0, 1).reshape(width, width)
-        half = grad_down.shape[0] // 2
-        terms = [grad_down[:half], grad_down[half:], grad_up_t[:half], grad_up_t[half:]]
-        terms += [stack(matrix) for matrix in (grad_out, grad_query, grad_key, grad_value)]
-        *sums, sum_small = sum_call(terms, jnp.pad(small.reshape(6, width), ((0, 2), (0, 0))))
-        sum_down = jnp.concatenate(sums[:2], axis=0)
-        sum_up_t = jnp.concatenate(sums[2:4], axis=0)
-        sum_out, *sum_qkv = [unstack(matrix) for matrix in sums[4:]]
-        sum_small = sum_small[:6].reshape(-1)
-    else:
-        sums = lax.psum(
-            (grad_down, grad_up_t, grad_out, grad_query, grad_key, grad_value), everywhere
-        )
-        sum_small = lax.psum(small, everywhere)
-        sum_down, sum_up_t, sum_out, *sum_qkv = sums
+    sums = lax.psum((grad_down, grad_up, grad_out, grad_query, grad_key, grad_value), everywhere)
+    sum_small = lax.psum(small, everywhere)
+    sum_down, sum_up, sum_out, *sum_qkv = sums
     return (
         outputs,
         input_grad,
@@ -636,7 +899,7 @@
         jnp.concatenate(sum_qkv, axis=1).astype(WIDE),
         sum_out.astype(WIDE),
         sum_small[width : 2 * width],
-        sum_up_t.T.astype(WIDE),
+        sum_up.astype(WIDE),
         sum_small[2 * width :],
         sum_down.astype(WIDE),
     )

time: 592 us -> 473 us (0.80)
  local copies, waits for them, and re-layouts: 58.5 us -> 20 us
  Pallas kernels: 355 us -> 322 us
  matrix products: 74 us -> 48.9 us
  starting transfers between devices: 28.1 us -> 9.44 us
    pallas_call x5 -> x1, Pallas kernels: 286 us -> 253 us  [gradient_call(): pl.pallas_call(gradient_kernel, in_specs=[anywhere] * 12 + [inside] * 4 +...]
    dot_general x20 -> x10, matrix products: 74 us -> 48.9 us  [dot(): return lax.dot_general(left, right, dims, preferred_element_type=WIDE)]
    unnamed x169 -> x80, local copies, waits for them, and re-layouts: 34.3 us -> 12.6 us
    ppermute x11 -> x5, starting transfers between devices: 28.1 us -> 9.44 us  [send(): return lax.ppermute(value, 'blk', pairs_of_places)]
    reshape x7 -> x1, local copies, waits for them, and re-layouts: 12.2 us -> 0.61 us  [on_device(): sum_small[2:6].reshape(-1)]
    slice x5 -> x2, local copies, waits for them, and re-layouts: 9.1 us -> 2.17 us  [the longest x1 1.43 us: on_device(): sum_small[1]]
    convert_element_type x5 -> x3, other arithmetic: 14.9 us -> 10.7 us  [the longest x1 5.05 us: on_device(): sum_up.astype(WIDE)]
    ppermute x11 -> x5, waiting for transfers between devices: 14.1 us -> 16.8 us  [send(): return lax.ppermute(value, 'blk', pairs_of_places)]
  transfers between devices with their start and end apart: 11 -> 5, of which waited for: 1 -> 3; matrix products, arithmetic and copies ran while one was open for 8% -> 2% of each run, Pallas kernels for 22% -> 11%
where the time goes in v3:
time: 473 us; the launch traced here: 465 us
  Pallas kernels  322 us (68%)
  matrix products  48.9 us (10%)
  other arithmetic  38.1 us (8%)
  local copies, waits for them, and re-layouts  20 us (4%)
  waiting for transfers between devices  16.8 us (4%)
  starting transfers between devices  9.44 us (2%)
  between operations  9.34 us (2%)
    pallas_call x1, Pallas kernels, gradient_call(): pl.pallas_call(gradient_kernel, in_specs=[anywhere] * 12 + [inside] * 4 +...  253 us
    pallas_call x4, Pallas kernels, forward_call(): pl.pallas_call(functools.partial(forward_kernel, first, last), grid=(pair...  69.5 us
    dot_general x10, matrix products, dot(): return lax.dot_general(left, right, dims, preferred_element_type=WIDE)  48.9 us
    ppermute x5, waiting for transfers between devices, send(): return lax.ppermute(value, 'blk', pairs_of_places)  16.8 us
    unnamed x80, local copies, waits for them, and re-layouts  12.6 us
  transfers between devices with their start and end apart: 5, of which 3 were waited for; matrix products, arithmetic and copies ran while one was open for 2% of the time, Pallas kernels for 11%

profile of v3, /device:TPU:0, one launch (start us, length us, event | category | flops | bytes accessed | tf_op | source)
XLA Modules:
  0.0 464.6 jit_solution(252864500537679041)
XLA Ops:
  1.5 4.2 multiply_sine_fusion
  7.4 3.0 collective-permute-start
  24.8 2.4 convolution_convert_fusion.4.refs_3_.refs_12_
  27.2 9.3 %collective-permute-done.refs_0_.refs_9_ = bf16[768,768]{1,0:T(8,128)(2,1)} collective-permute-done((bf16[768,768]{1,0:T(8,128)(2,1)S(1)}, bf16[768,768]{1,0:T(8,128)(2,1)}, u32[]{:S(2)}, u32[]{:S(2)}) %collective-permute-start) | collective-permute-done | bytes 1179680 | tf_op jit(solution)/shard_map/ppermute | solution.py:753
  38.2 16.5 %attend.4 = (bf16[768,768]{1,0:T(8,128)(2,1)S(1)}, bf16[768,768]{1,0:T(8,128)(2,1)S(1)}, f32[768,768]{1,0:T(8,128)}, f32[6,2,768]{2,1,0:T(2,128)S(1)}, f32[6,2,768]{2,1,0:T(2,128)S(1)}) custom-call(bf16[768,768]{1,0:T(8,128)(2,1)S(1)} %multiply_convert_fusion.2.refs_0_.refs_8_, bf16[768,2304]{1,0:T(8,128)(2,1)} %refs_18_.1, bf16[768,2304]{1,0:T(8,128)(2,1)} %refs_18_.1, ...), custom_call_target="tpu_custom_call" | custom-call | flops 9059696640 | bytes 14155776 | tf_op jit(solution)/shard_map/attend/pallas_call | solution.py:179
  63.8 17.4 %attend.5 = (bf16[768,768]{1,0:T(8,128)(2,1)S(1)}, bf16[768,768]{1,0:T(8,128)(2,1)S(1)}, f32[768,768]{1,0:T(8,128)}, f32[6,2,768]{2,1,0:T(2,128)S(1)}, f32[6,2,768]{2,1,0:T(2,128)S(1)}) custom-call(bf16[768,768]{1,0:T(8,128)(2,1)} %collective-permute-done.refs_0_.refs_9_, bf16[768,2304]{1,0:T(8,128)(2,1)} %refs_18_.1, bf16[768,2304]{1,0:T(8,128)(2,1)} %refs_18_.1, ...), custom_call_target="tpu_custom_call" | custom-call | flops 9059696640 | bytes 14155776 | tf_op jit(solution)/shard_map/attend/pallas_call | solution.py:179
  83.4 5.3 %collective-permute-done.4 = bf16[768,768]{1,0:T(8,128)(2,1)S(1)} collective-permute-done((bf16[768,768]{1,0:T(8,128)(2,1)}, bf16[768,768]{1,0:T(8,128)(2,1)S(1)}, u32[]{:S(2)}, u32[]{:S(2)}) %collective-permute-start.4) | collective-permute-done | bytes 1179680 | tf_op jit(solution)/shard_map/ppermute | solution.py:753
  90.3 17.4 %attend.6 = (bf16[768,768]{1,0:T(8,128)(2,1)S(1)}, bf16[768,768]{1,0:T(8,128)(2,1)S(1)}, f32[768,768]{1,0:T(8,128)}, f32[6,2,768]{2,1,0:T(2,128)S(1)}, f32[6,2,768]{2,1,0:T(2,128)S(1)}) custom-call(bf16[768,768]{1,0:T(8,128)(2,1)S(1)} %add.84.refs_0_.refs_10_, bf16[768,2304]{1,0:T(8,128)(2,1)} %refs_18_.1, bf16[768,2304]{1,0:T(8,128)(2,1)} %refs_18_.1, ...), custom_call_target="tpu_custom_call" | custom-call | flops 9059696640 | bytes 14155776 | tf_op jit(solution)/shard_map/attend/pallas_call | solution.py:179
  109.8 2.1 collective-permute-done.2
  113.5 18.2 %attend.7 = (bf16[768,768]{1,0:T(8,128)(2,1)S(1)}, bf16[768,768]{1,0:T(8,128)(2,1)S(1)}, f32[768,768]{1,0:T(8,128)}, f32[6,2,768]{2,1,0:T(2,128)S(1)}, f32[6,2,7...) custom-call(bf16[768,768]{1,0:T(8,128)(2,1)S(1)} %add.80.refs_0_.refs_11_, bf16[768,2304]{1,0:T(8,128)(2,1)} %refs_18_.1, ...), custom_call_target="tpu_custom_call" | custom-call | flops 9059696640 | bytes 14155776 | tf_op jit(solution)/shard_map/attend/pallas_call | solution.py:179
  134.9 7.2 %multiply_convert_fusion = (bf16[768,3072]{1,0:T(8,128)(2,1)S(1)}, f32[768,3072]{1,0:T(8,128)}) fusion(f32[3072]{0:T(1024)S(1)} %copy-done.32, bf16[768,3072]{1,0:T(8,128)(2,1)S(1)} %bitcast.26, f32[768,768]{1,0:T(8,128)S(1)} %get-tuple-element.78, f32[768]{0:T(1024)S(1)} %copy-done.31, f32[768]{0:T(1024)S(1)} %add_rsqrt_fusion, ...), kind=kOutput, calls=%fused_computation.8 | convolution fusion | flops 3640393728 | bytes 21255168 | tf_op jit(solution)/shard_map/dot_general | solution.py:28
  142.1 5.3 %convolution_add_fusion.1 = f32[768,768]{1,0:T(8,128)} fusion(f32[768,768]{1,0:T(8,128)S(1)} %get-tuple-element.78, bf16[768,3072]{1,0:T(8,128)(2,1)S(1)} %get-tuple-element.79, bf16[3072,768]{1,0:T(8,128)(2,1)S(1)} %bitcast.24), kind=kOutput, calls=%fused_computation.30 | convolution fusion | flops 3624468480 | bytes 14155776 | tf_op jit(solution)/shard_map/dot_general | solution.py:28
  147.4 5.7 %convolution_convert_fusion.1.refs_19_ = bf16[3072,768]{1,0:T(8,128)(2,1)} fusion(bf16[768,3072]{1,0:T(8,128)(2,1)S(1)} %get-tuple-element.79, f32[768,768]{1,0:T(8,128)S(1)} %copy-done.27), kind=kOutput, calls=%fused_computation.11 | convolution fusion | flops 3626827776 | bytes 11796480 | tf_op jit(solution)/shard_map/dot_general | solution.py:28
  153.1 10.0 %convert_reduce_fusion = (f32[3072]{0:T(1024)S(1)}, bf16[768,3072]{1,0:T(8,128)(2,1)}) fusion(f32[768,3072]{1,0:T(8,128)} %get-tuple-element.80, f32[3072]{0:T(1024)S(1)} %copy-done.32, bf16[3072,768]{1,0:T(8,128)(2,1)S(1)} %bitcast.24, f32[768,768]{1,0:T(8,128)S(1)} %copy-done.27), kind=kOutput, calls=%fused_computation.7 | convolution fusion | flops 3655136256 | bytes 21258240 | tf_op jit(solution)/shard_map/dot_general | solution.py:28
  163.0 6.7 %multiply_reduce_fusion.1 = (f32[768]{0:T(1024)S(1)}, f32[768]{0:T(1024)S(1)}, f32[768]{0:T(1024)S(1)}, f32[768,768]{1,0:T(8,128)S(1)}) fusion(f32[768,768]{1,0:T(8,128)S(1)} %get-tuple-element.78, f32[768]{0:T(1024)S(1)} %add_rsqrt_fusion, f32[768]{0:T(1024)S(1)} %broadcast_multiply_fusion.4, f32[768]{0:T(1024)S(1)} %copy-done.31, ...), kind=kOutput, calls=%fused_computation.15 | convolution fusion | flops 3628594944 | bytes 14174208 | tf_op jit(solution)/shard_map/dot_general | solution.py:28
  169.7 6.2 %convolution_convert_fusion.refs_20_ = bf16[768,3072]{1,0:T(8,128)(2,1)} fusion(bf16[768,3072]{1,0:T(8,128)(2,1)S(1)} %copy-done.33, f32[768,768]{1,0:T(8,128)S(1)} %get-tuple-element.78, f32[768]{0:T(1024)S(1)} %copy-done.31, f32[768]{0:T(1024)S(1)} %add_rsqrt_fusion, f32[768]{0:T(1024)S(1)} %broadcast_multiply_fusion.4), kind=kOutput, calls=%fused_computation.10 | convolution fusion | flops 3628597248 | bytes 11805696 | tf_op jit(solution)/shard_map/dot_general | solution.py:28
  177.1 2.2 convolution_convert_fusion.2.refs_21_
  179.3 2.2 fusion.6.refs_13_
  182.1 2.2 convert_multiply_fusion
  185.1 252.5 %gradients.1 = (bf16[3072,768]{1,0:T(8,128)(2,1)}, bf16[768,3072]{1,0:T(8,128)(2,1)}, bf16[768,768]{1,0:T(8,128)(2,1)}, bf16[768,2304]{1,0:T(8,128)(2,1)}, f32[8,768]{1,0:T(8,128)}, /*index=5*/f32[768,768]{1,0:T(8,128)}) custom-call(bf16[768,768]{1,0:T(8,128)(2,1)} %copy-done.6, bf16[768,768]{1,0:T(8,128)(2,1)} %copy-done.8, bf16[768,768]{1,0:T(8,128)(2,1)} %copy-done.10, ...), custom_call_target="tpu_custom_call" | custom-call | tf_op jit(solution)/shard_map/gradients/pallas_call | solution.py:721
  439.8 3.2 multiply_reduce_fusion.5
  446.3 4.1 convert_element_type.73
  450.9 5.0 %convert_element_type.75 = f32[768,3072]{1,0:T(8,128)} convert(bf16[768,3072]{1,0:T(8,128)(2,1)S(1)} %copy-done.24) | non-fusion elementwise | flops 2359296 | bytes 14155776 | tf_op jit(solution)/shard_map/convert_element_type | solution.py:838
  455.9 5.5 %convert_element_type.76 = f32[3072,768]{1,0:T(8,128)} convert(bf16[3072,768]{1,0:T(8,128)(2,1)S(1)} %bitcast.22) | non-fusion elementwise | flops 2359296 | bytes 14155776 | tf_op jit(solution)/shard_map/convert_element_type | solution.py:840
  (132 shorter events, 41.6 us)
Async XLA Ops:
  0.6 131.1 %copy-start = (bf16[768,768]{1,0:T(8,128)(2,1)S(1)}, bf16[768,768]{1,0:T(8,128)(2,1)}, u32[]{:S(2)}) copy-start(bf16[768,768]{1,0:T(8,128)(2,1)} %param.17) | copy-start | bytes 3538948
  0.7 5.0 %copy-start.26 = (f32[768,768]{1,0:T(8,128)S(1)}, f32[768,768]{1,0:T(8,128)}, u32[]{:S(2)}) copy-start(f32[768,768]{1,0:T(8,128)} %param.12) | copy-start | bytes 7077892
  6.4 15.9 %copy-start.30 = (s32[3072]{0:T(1024)S(1)}, s32[3072]{0:T(1024)}, u32[]{:S(2)}) copy-start(s32[3072]{0:T(1024)} %param.14) | copy-start | bytes 36868
  7.4 30.8 %copy-start.3 = (bf16[768,768]{1,0:T(8,128)(2,1)}, bf16[768,768]{1,0:T(8,128)(2,1)S(1)}, u32[]{:S(2)}) copy-start(bf16[768,768]{1,0:T(8,128)(2,1)S(1)} %multiply_convert_fusion.2.refs_0_.refs_8_) | copy-start | bytes 3538948
  7.4 29.1 %collective-permute-start = (bf16[768,768]{1,0:T(8,128)(2,1)S(1)}, bf16[768,768]{1,0:T(8,128)(2,1)}, u32[]{:S(2)}, u32[]{:S(2)}) collective-permute-start(bf16[768,768]{1,0:T(8,128)(2,1)S(1)} %multiply_convert_fusion.2.refs_0_.refs_8_), channel_id=1, source_target_pairs={{0,1},{1,0},{2,3},{3,2},{4,5},{5,4},{6,7},{7,6},{8,9},{9,8},{10,11... | collective-permute-start | bytes 3538952 | tf_op jit(solution)/shard_map/ppermute | solution.py:753
  10.5 46.4 %collective-permute-start.3 = (bf16[768,768]{1,0:T(8,128)(2,1)S(1)}, bf16[768,768]{1,0:T(8,128)(2,1)}, u32[]{:S(2)}, u32[]{:S(2)}) collective-permute-start(bf16[768,768]{1,0:T(8,128)(2,1)S(1)} %multiply_convert_fusion.2.refs_0_.refs_8_), channel_id=1, source_target_pairs={{1,2},{2,1},{5,6},{6,5},{9,10},{10,9},{13,14},{14,13},{17,18},{18,... | collective-permute-start | bytes 3538952 | tf_op jit(solution)/shard_map/ppermute | solution.py:753
  22.5 91.0 %copy-start.17 = (s32[1,768]{1,0:T(1,128)}, s32[1,768]{1,0:T(1,128)S(1)}, u32[]{:S(2)}) copy-start(s32[1,768]{1,0:T(1,128)S(1)} %broadcast_in_dim.13.refs_5_.refs_17_) | copy-start | bytes 9220
  24.8 13.4 %copy-start.15 = (s32[768,1]{1,0:T(8,128)S(1)}, s32[768,1]{1,0:T(8,128)}, u32[]{:S(2)}) copy-start(s32[768,1]{1,0:T(8,128)} %copy.35.refs_4_) | copy-start | bytes 9220
  27.2 27.5 %copy-start.4 = (bf16[768,768]{1,0:T(8,128)(2,1)}, bf16[768,768]{1,0:T(8,128)(2,1)S(1)}, u32[]{:S(2)}) copy-start(bf16[768,768]{1,0:T(8,128)(2,1)S(1)} %convolution_convert_fusion.4.refs_3_.refs_12_) | copy-start | bytes 3538948
  36.5 23.3 %collective-permute-start.1 = (bf16[768,768]{1,0:T(8,128)(2,1)}, bf16[768,768]{1,0:T(8,128)(2,1)}, u32[]{:S(2)}, u32[]{:S(2)}) collective-permute-start(bf16[768,768]{1,0:T(8,128)(2,1)} %collective-permute-done.refs_0_.refs_9_), channel_id=1, source_target_pairs={{1,2},{2,1},{5,6},{6,5},{9,10},{10,9},{13,14},{14,13},{17,18},{18,... | collective-permute-start | bytes 3538952 | tf_op jit(solution)/shard_map/ppermute | solution.py:753
  56.8 31.9 %collective-permute-start.4 = (bf16[768,768]{1,0:T(8,128)(2,1)}, bf16[768,768]{1,0:T(8,128)(2,1)S(1)}, u32[]{:S(2)}, u32[]{:S(2)}) collective-permute-start(bf16[768,768]{1,0:T(8,128)(2,1)} %collective-permute-done.3), channel_id=1, source_target_pairs={{1,0},{2,3},{5,4},{6,7},{9,8},{10,11},{13,12},{14,15},{17,16},{18,... | collective-permute-start | bytes 3538952 | tf_op jit(solution)/shard_map/ppermute | solution.py:753
  59.8 52.1 %collective-permute-start.2 = (bf16[768,768]{1,0:T(8,128)(2,1)}, bf16[768,768]{1,0:T(8,128)(2,1)S(1)}, u32[]{:S(2)}, u32[]{:S(2)}) collective-permute-start(bf16[768,768]{1,0:T(8,128)(2,1)} %collective-permute-done.1), channel_id=1, source_target_pairs={{1,0},{2,3},{5,4},{6,7},{9,8},{10,11},{13,12},{14,15},{17,16},{18,... | collective-permute-start | bytes 3538952 | tf_op jit(solution)/shard_map/ppermute | solution.py:753
  90.3 17.4 %copy-start.1 = (bf16[768,768]{1,0:T(8,128)(2,1)}, bf16[768,768]{1,0:T(8,128)(2,1)S(1)}, u32[]{:S(2)}) copy-start(bf16[768,768]{1,0:T(8,128)(2,1)S(1)} %add.84.refs_0_.refs_10_) | copy-start | bytes 3538948
  113.5 18.2 %copy-start.2 = (bf16[768,768]{1,0:T(8,128)(2,1)}, bf16[768,768]{1,0:T(8,128)(2,1)S(1)}, u32[]{:S(2)}) copy-start(bf16[768,768]{1,0:T(8,128)(2,1)S(1)} %add.80.refs_0_.refs_11_) | copy-start | bytes 3538948
  113.5 18.2 %copy-start.19 = (f32[768,768]{1,0:T(8,128)S(1)}, f32[768,768]{1,0:T(8,128)}, u32[]{:S(2)}) copy-start(f32[768,768]{1,0:T(8,128)} %copy-done.18) | copy-start | bytes 7077892
  133.2 8.9 %slice-start.2 = ((s8[4718592]{0:T(1024)(128)(4,1)}), s8[4194304]{0:T(1024)(128)(4,1)S(1)}, s32[]{:S(2)}) async-start(s8[4718592]{0:T(1024)(128)(4,1)} %bitcast.23), calls=%async_computation.2 | async-start | bytes 8388608
  134.9 7.2 %slice-start.3 = ((s8[4718592]{0:T(1024)(128)(4,1)}), s8[524288]{0:T(1024)(128)(4,1)S(1)}, s32[]{:S(2)}) async-start(s8[4718592]{0:T(1024)(128)(4,1)} %bitcast.23), calls=%async_computation.3 | async-start | bytes 1048576
  142.1 5.3 %copy-start.27 = (f32[768,768]{1,0:T(8,128)S(1)}, f32[768,768]{1,0:T(8,128)}, u32[]{:S(2)}) copy-start(f32[768,768]{1,0:T(8,128)} %param.22) | copy-start | bytes 7077892
  163.0 6.7 %copy-start.33 = (bf16[768,3072]{1,0:T(8,128)(2,1)S(1)}, bf16[768,3072]{1,0:T(8,128)(2,1)}, u32[]{:S(2)}) copy-start(bf16[768,3072]{1,0:T(8,128)(2,1)} %get-tuple-element.83) | copy-start | bytes 14155780
  446.3 9.6 %slice-start = ((s8[4718592]{0:T(1024)(128)(4,1)}), s8[4194304]{0:T(1024)(128)(4,1)S(1)}, s32[]{:S(2)}) async-start(s8[4718592]{0:T(1024)(128)(4,1)} %bitcast.21), calls=%async_computation | async-start | bytes 8388608
  450.9 5.1 %slice-start.1 = ((s8[4718592]{0:T(1024)(128)(4,1)}), s8[524288]{0:T(1024)(128)(4,1)S(1)}, s32[]{:S(2)}) async-start(s8[4718592]{0:T(1024)(128)(4,1)} %bitcast.21), calls=%async_computation.1 | async-start | bytes 1048576
  455.9 5.5 %copy-start.20 = (f32[768,768]{1,0:T(8,128)S(1)}, f32[768,768]{1,0:T(8,128)}, u32[]{:S(2)}) copy-start(f32[768,768]{1,0:T(8,128)} %copy-done.18) | copy-start | bytes 7077892
  455.9 5.5 %copy-start.22 = (f32[768,768]{1,0:T(8,128)S(1)}, f32[768,768]{1,0:T(8,128)}, u32[]{:S(2)}) copy-start(f32[768,768]{1,0:T(8,128)} %copy-done.21) | copy-start | bytes 7077892
  455.9 6.4 %copy-start.23 = (f32[768,768]{1,0:T(8,128)S(1)}, f32[768,768]{1,0:T(8,128)}, u32[]{:S(2)}) copy-start(f32[768,768]{1,0:T(8,128)} %get-tuple-element.55) | copy-start | bytes 7077892
  (21 other events, 38.4 us)

commit v4 on v3

--- a/solution.py
+++ b/solution.py
@@ -306,6 +306,7 @@
 TURNS = ((0, 1, 2), (0, 2, 1))
 STEPS = 5
 ADD_ROWS = 48
+FORWARD = 8
 
 
 def place_bits(turn):
@@ -429,11 +430,15 @@
 
 
 PARTS = (
-    ("down", (0, 0), (1536, 768), "rrrrr", 0, (2, 6, 9, 12, 14, 16, 18, 20, 22, 23)),
-    ("down", (1536, 0), (1536, 768), "rrrrr", 1, (2, 6, 9, 12, 14, 16, 18, 20, 22, 23)),
-    ("up", (0, 0), (768, 1536), "rrrcc", 0, (3, 8, 11, 13, 15, 17, 19, 21, 24, 24)),
-    ("up", (0, 1536), (768, 1536), "rrrcc", 1, (3, 8, 11, 13, 15, 17, 19, 21, 24, 24)),
-    ("out", (0, 0), (768, 768), "rrrrc", 0, (4, 9, 11, 13, 15, 17, 19, 21, 23, 24)),
+    ("down", (0, 0), (1536, 384), "rrrrr", 0, (1, 3, 7, 9, 10, 12, 14, 15, 17, 18)),
+    ("down", (0, 384), (1536, 384), "rrrrr", 1, (1, 3, 7, 8, 9, 11, 12, 14, 17, 18)),
+    ("down", (1536, 0), (1536, 384), "rrrrr", 1, (2, 5, 10, 11, 13, 15, 17, 18, 21, 22)),
+    ("down", (1536, 384), (1536, 384), "rrrrr", 0, (2, 5, 8, 9, 11, 12, 15, 18, 20, 21)),
+    ("up", (0, 0), (768, 768), "rrrrc", 0, (2, 6, 9, 10, 12, 14, 16, 18, 23, 24)),
+    ("up", (0, 768), (768, 768), "rrrrc", 1, (3, 6, 10, 12, 14, 17, 18, 21, 23, 24)),
+    ("up", (0, 1536), (768, 768), "rrrrc", 0, (3, 7, 10, 12, 13, 16, 18, 20, 24, 24)),
+    ("up", (0, 2304), (768, 768), "rrrrc", 1, (3, 7, 11, 13, 16, 18, 19, 23, 24, 24)),
+    ("out", (0, 0), (768, 768), "rrrrc", 0, (3, 9, 10, 12, 15, 17, 18, 22, 24, 24)),
     ("qkv", (0, 0), (768, 512), "rrrrc", 0, None),
     ("qkv", (0, 512), (768, 512), "rrrrc", 1, None),
     ("qkv", (0, 1024), (768, 512), "rrrrc", 0, None),
@@ -448,11 +453,11 @@
     down_out, up_out, out_out, qkv_out, small_out, input_out = refs[23:29]
     refs = refs[29:]
     kv_slot, a_slot, dq_sum, dk_sum, dv_sum, dk_all, dv_all, grad_k, grad_v, parts = refs[:10]
-    far, mid_2, mid_3, last_1, last_3, qkv_term, clip_slot, small_arrived = refs[10:18]
+    from_near, from_across, qkv_term, clip_slot, small_arrived = refs[10:15]
     input_sum = dq_sum
-    kv_sems, a_sem, line_sends, line_receives, sends, receives, locals_ = refs[18:25]
-    small_sends, small_receives, out_sem, clip_sem = refs[25:29]
-    refs = refs[29:]
+    kv_sems, a_sem, line_sends, line_receives, sends, receives, locals_ = refs[15:22]
+    small_sends, small_receives, out_sem, clip_sem = refs[22:26]
+    refs = refs[26:]
     rows, width = q_ref.shape
     pairs = width // PAIR
     pieces = 4 * pairs
@@ -472,7 +477,7 @@
         total, arrived = refs[0], refs[1:STEPS]
         refs = refs[STEPS:]
         if name == "down":
-            arrived = (qkv_term.at[:, pl.ds(index * width, width)], *arrived)
+            arrived = (qkv_term.at[:, pl.ds(index * shape[1], shape[1])], *arrived)
         else:
             arrived, refs = (refs[0], *arrived), refs[1:]
         sums.append(
@@ -491,13 +496,33 @@
     early = [(each, part[5]) for each, part in zip(sums, PARTS) if part[5] is not None]
     late = [each for each, part in zip(sums, PARTS) if part[5] is None]
 
-    line_sems = (line_sends, line_receives)
-    send_far = remote(parts.at[0], far, line_sems, 0, near)
-    send_mid_2 = remote(parts.at[1], mid_2, line_sems, 1, near)
-    send_mid_3 = remote(parts.at[0], mid_3, line_sems, 2, across)
-    send_last_1 = remote(parts.at[1], last_1, line_sems, 3, across)
-    send_last_2 = remote(parts.at[2], far, line_sems, 4, near)
-    send_last_3 = remote(parts.at[2], last_3, line_sems, 5, near)
+    chunk_rows = rows // pairs
+
+    def chunk_of(chunk):
+        return pl.ds(pl.multiple_of(chunk * chunk_rows, chunk_rows), chunk_rows)
+
+    def line_copy(channel, chunk, source, target, device):
+        return pltpu.make_async_remote_copy(
+            src_ref=parts.at[source, chunk_of(chunk)],
+            dst_ref=target.at[chunk_of(chunk)],
+            send_sem=line_sends.at[channel, chunk],
+            recv_sem=line_receives.at[channel, chunk],
+            device_id=device,
+            device_id_type=MESH,
+        )
+
+    def inward(source, chunk):
+        return line_copy(source, chunk, source, from_near.at[source], near)
+
+    def middle(source, chunk):
+        return line_copy(3 + source, chunk, source, from_across.at[source], across)
+
+    def outward(chunk):
+        return line_copy(5, chunk, 2, from_near.at[0], near)
+
+    def add_chunk(total, term, chunk):
+        here = chunk_of(chunk)
+        total[here] = (total[here].astype(WIDE) + term[here].astype(WIDE)).astype(total.dtype)
 
     def pair_columns(pair):
         return pl.ds(pl.multiple_of(pair * PAIR, PAIR), PAIR)
@@ -570,26 +595,23 @@
             if ends:
                 at(when, *ends)
         at_middle = jnp.logical_not(at_end)
-        at(pairs, send_far.start, also=at_end)
-        at(2 * pairs, send_far.wait_send, send_mid_2.start, also=at_end)
-        at(
-            2 * pairs + 1,
-            send_far.wait_recv,
-            lambda: add_block(parts.at[0], far),
-            send_mid_3.start,
-            also=at_middle,
-        )
-        at(3 * pairs, send_mid_2.wait_send, send_last_3.start, also=at_end)
-        at(
-            3 * pairs + 2,
-            send_mid_2.wait_recv,
-            lambda: add_block(parts.at[1], mid_2),
-            send_last_1.start,
-            send_mid_3.wait,
-            lambda: add_block(parts.at[2], mid_3),
-            send_last_2.start,
-            also=at_middle,
-        )
+
+        @pl.when(jnp.logical_and(turn > 0, at_end))
+        def _():
+            inward(turn - 1, pair).start()
+
+        @pl.when(jnp.logical_and(at_middle, jnp.logical_and(piece >= FORWARD, piece < FORWARD + 2 * pairs)))
+        def _():
+            source, chunk = (piece - FORWARD) // pairs, (piece - FORWARD) % pairs
+            inward(source, chunk).wait_recv()
+            add_chunk(parts.at[source], from_near.at[source], chunk)
+            middle(source, chunk).start()
+
+        @pl.when(jnp.logical_and(at_middle, turn == 3))
+        def _():
+            middle(0, pair).wait_recv()
+            add_chunk(parts.at[2], from_across.at[0], pair)
+            outward(pair).start()
 
         @pl.when(pair == 0)
         def _():
@@ -643,32 +665,38 @@
 
     for each in late:
         each.start()
-    for each, ticks in early:
-        for tick in range(2 * STEPS):
-            if ticks[tick] == pieces:
-                each.turn(tick)
+    open_sums = [(each, [tick for tick in range(2 * STEPS) if ticks[tick] == pieces]) for each, ticks in early]
+    open_sums += [(each, list(range(2 * STEPS))) for each in late]
 
     @pl.when(at_end)
     def _():
-        send_last_3.wait_send()
-        send_last_2.wait_recv()
-        add_block(input_sum, far)
+        @pl.loop(0, pairs)
+        def _(chunk):
+            for source in range(3):
+                inward(source, chunk).wait_send()
+            outward(chunk).wait_recv()
+            add_chunk(input_sum, from_near.at[0], chunk)
 
     @pl.when(jnp.logical_not(at_end))
     def _():
-        send_last_1.wait()
-        send_last_2.wait_send()
-        send_last_3.wait_recv()
-        add_block(input_sum, last_1)
-        add_block(input_sum, last_3)
+        @pl.loop(0, pairs)
+        def _(chunk):
+            outward(chunk).wait_send()
+            for source in range(2):
+                middle(source, chunk).wait_send()
+            middle(1, chunk).wait_recv()
+            add_chunk(input_sum, from_across.at[1], chunk)
+            inward(2, chunk).wait_recv()
+            add_chunk(input_sum, from_near.at[2], chunk)
 
     store = pltpu.make_async_copy(input_sum, input_out, out_sem)
     store.start()
     for tick in range(2 * STEPS):
         if tick < STEPS:
             small(tick).start()
-        for each in late:
-            each.turn(tick)
+        for each, ticks in open_sums:
+            if ticks:
+                each.turn(ticks.pop(0))
         if tick < STEPS:
             small(tick).wait()
             small_out[...] += small_arrived[tick]
@@ -695,15 +723,15 @@
         pltpu.VMEM((width, width), WIDE),
         pltpu.VMEM((3, *square), LOW),
     ]
-    scratch += [pltpu.VMEM(square, LOW)] * 5
+    scratch += [pltpu.VMEM((3, *square), LOW), pltpu.VMEM((2, *square), LOW)]
     scratch += [
         pltpu.VMEM((width, 3 * width), LOW),
         pltpu.VMEM((rows, 1), clips.dtype),
         pltpu.VMEM((STEPS, *small.shape), WIDE),
         pltpu.SemaphoreType.DMA((2, 2)),
         pltpu.SemaphoreType.DMA,
-        pltpu.SemaphoreType.DMA((6,)),
-        pltpu.SemaphoreType.DMA((6,)),
+        pltpu.SemaphoreType.DMA((6, pairs)),
+        pltpu.SemaphoreType.DMA((6, pairs)),
         pltpu.SemaphoreType.DMA((len(PARTS), 2 * STEPS)),
         pltpu.SemaphoreType.DMA((len(PARTS), 2 * STEPS)),
         pltpu.SemaphoreType.DMA((len(PARTS), 2)),

time: 473 us -> 444 us (0.939)
  Pallas kernels: 322 us -> 294 us
    pallas_call x1, Pallas kernels: 253 us -> 224 us  [gradient_call(): pl.pallas_call(gradient_kernel, in_specs=[anywhere] * 12 + [inside] * 4 +...]
  transfers between devices with their start and end apart: 5 -> 5, of which waited for: 3 -> 3; matrix products, arithmetic and copies ran while one was open for 2% -> 2% of each run, Pallas kernels for 11% -> 12%
where the time goes in v4:
time: 444 us; the launch traced here: 437 us
  Pallas kernels  294 us (66%)
  matrix products  48.9 us (11%)
  other arithmetic  38.1 us (9%)
  local copies, waits for them, and re-layouts  20 us (5%)
  waiting for transfers between devices  16.8 us (4%)
  starting transfers between devices  9.44 us (2%)
  between operations  9.34 us (2%)
    pallas_call x1, Pallas kernels, gradient_call(): pl.pallas_call(gradient_kernel, in_specs=[anywhere] * 12 + [inside] * 4 +...  224 us
    pallas_call x4, Pallas kernels, forward_call(): pl.pallas_call(functools.partial(forward_kernel, first, last), grid=(pair...  69.5 us
    dot_general x10, matrix products, dot(): return lax.dot_general(left, right, dims, preferred_element_type=WIDE)  48.9 us
    ppermute x5, waiting for transfers between devices, send(): return lax.ppermute(value, 'blk', pairs_of_places)  16.8 us
    unnamed x80, local copies, waits for them, and re-layouts  12.6 us
    ppermute x5, starting transfers between devices, send(): return lax.ppermute(value, 'blk', pairs_of_places)  9.44 us
  transfers between devices with their start and end apart: 5, of which 3 were waited for; matrix products, arithmetic and copies ran while one was open for 2% of the time, Pallas kernels for 12%

profile of v4, /device:TPU:0, one launch (start us, length us, event | category | flops | bytes accessed | tf_op | source)
XLA Modules:
  0.0 436.6 jit_solution(9003019501852761606)
XLA Ops:
  1.5 4.2 multiply_sine_fusion
  7.4 3.0 collective-permute-start
  24.8 2.4 convolution_convert_fusion.4.refs_3_.refs_12_
  27.2 9.3 %collective-permute-done.refs_0_.refs_9_ = bf16[768,768]{1,0:T(8,128)(2,1)} collective-permute-done((bf16[768,768]{1,0:T(8,128)(2,1)S(1)}, bf16[768,768]{1,0:T(8,128)(2,1)}, u32[]{:S(2)}, u32[]{:S(2)}) %collective-permute-start) | collective-permute-done | bytes 1179680 | tf_op jit(solution)/shard_map/ppermute | solution.py:781
  38.2 16.5 %attend.4 = (bf16[768,768]{1,0:T(8,128)(2,1)S(1)}, bf16[768,768]{1,0:T(8,128)(2,1)S(1)}, f32[768,768]{1,0:T(8,128)}, f32[6,2,768]{2,1,0:T(2,128)S(1)}, f32[6,2,768]{2,1,0:T(2,128)S(1)}) custom-call(bf16[768,768]{1,0:T(8,128)(2,1)S(1)} %multiply_convert_fusion.2.refs_0_.refs_8_, bf16[768,2304]{1,0:T(8,128)(2,1)} %refs_18_.1, bf16[768,2304]{1,0:T(8,128)(2,1)} %refs_18_.1, ...), custom_call_target="tpu_custom_call" | custom-call | flops 9059696640 | bytes 14155776 | tf_op jit(solution)/shard_map/attend/pallas_call | solution.py:179
  63.8 17.4 %attend.5 = (bf16[768,768]{1,0:T(8,128)(2,1)S(1)}, bf16[768,768]{1,0:T(8,128)(2,1)S(1)}, f32[768,768]{1,0:T(8,128)}, f32[6,2,768]{2,1,0:T(2,128)S(1)}, f32[6,2,768]{2,1,0:T(2,128)S(1)}) custom-call(bf16[768,768]{1,0:T(8,128)(2,1)} %collective-permute-done.refs_0_.refs_9_, bf16[768,2304]{1,0:T(8,128)(2,1)} %refs_18_.1, bf16[768,2304]{1,0:T(8,128)(2,1)} %refs_18_.1, ...), custom_call_target="tpu_custom_call" | custom-call | flops 9059696640 | bytes 14155776 | tf_op jit(solution)/shard_map/attend/pallas_call | solution.py:179
  83.4 5.3 %collective-permute-done.4 = bf16[768,768]{1,0:T(8,128)(2,1)S(1)} collective-permute-done((bf16[768,768]{1,0:T(8,128)(2,1)}, bf16[768,768]{1,0:T(8,128)(2,1)S(1)}, u32[]{:S(2)}, u32[]{:S(2)}) %collective-permute-start.4) | collective-permute-done | bytes 1179680 | tf_op jit(solution)/shard_map/ppermute | solution.py:781
  90.3 17.4 %attend.6 = (bf16[768,768]{1,0:T(8,128)(2,1)S(1)}, bf16[768,768]{1,0:T(8,128)(2,1)S(1)}, f32[768,768]{1,0:T(8,128)}, f32[6,2,768]{2,1,0:T(2,128)S(1)}, f32[6,2,768]{2,1,0:T(2,128)S(1)}) custom-call(bf16[768,768]{1,0:T(8,128)(2,1)S(1)} %add.84.refs_0_.refs_10_, bf16[768,2304]{1,0:T(8,128)(2,1)} %refs_18_.1, bf16[768,2304]{1,0:T(8,128)(2,1)} %refs_18_.1, ...), custom_call_target="tpu_custom_call" | custom-call | flops 9059696640 | bytes 14155776 | tf_op jit(solution)/shard_map/attend/pallas_call | solution.py:179
  109.8 2.1 collective-permute-done.2
  113.5 18.2 %attend.7 = (bf16[768,768]{1,0:T(8,128)(2,1)S(1)}, bf16[768,768]{1,0:T(8,128)(2,1)S(1)}, f32[768,768]{1,0:T(8,128)}, f32[6,2,768]{2,1,0:T(2,128)S(1)}, f32[6,2,7...) custom-call(bf16[768,768]{1,0:T(8,128)(2,1)S(1)} %add.80.refs_0_.refs_11_, bf16[768,2304]{1,0:T(8,128)(2,1)} %refs_18_.1, ...), custom_call_target="tpu_custom_call" | custom-call | flops 9059696640 | bytes 14155776 | tf_op jit(solution)/shard_map/attend/pallas_call | solution.py:179
  134.9 7.2 %multiply_convert_fusion = (bf16[768,3072]{1,0:T(8,128)(2,1)S(1)}, f32[768,3072]{1,0:T(8,128)}) fusion(f32[3072]{0:T(1024)S(1)} %copy-done.32, bf16[768,3072]{1,0:T(8,128)(2,1)S(1)} %bitcast.26, f32[768,768]{1,0:T(8,128)S(1)} %get-tuple-element.78, f32[768]{0:T(1024)S(1)} %copy-done.31, f32[768]{0:T(1024)S(1)} %add_rsqrt_fusion, ...), kind=kOutput, calls=%fused_computation.8 | convolution fusion | flops 3640393728 | bytes 21255168 | tf_op jit(solution)/shard_map/dot_general | solution.py:28
  142.1 5.3 %convolution_add_fusion.1 = f32[768,768]{1,0:T(8,128)} fusion(f32[768,768]{1,0:T(8,128)S(1)} %get-tuple-element.78, bf16[768,3072]{1,0:T(8,128)(2,1)S(1)} %get-tuple-element.79, bf16[3072,768]{1,0:T(8,128)(2,1)S(1)} %bitcast.24), kind=kOutput, calls=%fused_computation.30 | convolution fusion | flops 3624468480 | bytes 14155776 | tf_op jit(solution)/shard_map/dot_general | solution.py:28
  147.4 5.7 %convolution_convert_fusion.1.refs_19_ = bf16[3072,768]{1,0:T(8,128)(2,1)} fusion(bf16[768,3072]{1,0:T(8,128)(2,1)S(1)} %get-tuple-element.79, f32[768,768]{1,0:T(8,128)S(1)} %copy-done.27), kind=kOutput, calls=%fused_computation.11 | convolution fusion | flops 3626827776 | bytes 11796480 | tf_op jit(solution)/shard_map/dot_general | solution.py:28
  153.1 10.0 %convert_reduce_fusion = (f32[3072]{0:T(1024)S(1)}, bf16[768,3072]{1,0:T(8,128)(2,1)}) fusion(f32[768,3072]{1,0:T(8,128)} %get-tuple-element.80, f32[3072]{0:T(1024)S(1)} %copy-done.32, bf16[3072,768]{1,0:T(8,128)(2,1)S(1)} %bitcast.24, f32[768,768]{1,0:T(8,128)S(1)} %copy-done.27), kind=kOutput, calls=%fused_computation.7 | convolution fusion | flops 3655136256 | bytes 21258240 | tf_op jit(solution)/shard_map/dot_general | solution.py:28
  163.0 6.7 %multiply_reduce_fusion.1 = (f32[768]{0:T(1024)S(1)}, f32[768]{0:T(1024)S(1)}, f32[768]{0:T(1024)S(1)}, f32[768,768]{1,0:T(8,128)S(1)}) fusion(f32[768,768]{1,0:T(8,128)S(1)} %get-tuple-element.78, f32[768]{0:T(1024)S(1)} %add_rsqrt_fusion, f32[768]{0:T(1024)S(1)} %broadcast_multiply_fusion.4, f32[768]{0:T(1024)S(1)} %copy-done.31, ...), kind=kOutput, calls=%fused_computation.15 | convolution fusion | flops 3628594944 | bytes 14174208 | tf_op jit(solution)/shard_map/dot_general | solution.py:28
  169.7 6.2 %convolution_convert_fusion.refs_20_ = bf16[768,3072]{1,0:T(8,128)(2,1)} fusion(bf16[768,3072]{1,0:T(8,128)(2,1)S(1)} %copy-done.33, f32[768,768]{1,0:T(8,128)S(1)} %get-tuple-element.78, f32[768]{0:T(1024)S(1)} %copy-done.31, f32[768]{0:T(1024)S(1)} %add_rsqrt_fusion, f32[768]{0:T(1024)S(1)} %broadcast_multiply_fusion.4), kind=kOutput, calls=%fused_computation.10 | convolution fusion | flops 3628597248 | bytes 11805696 | tf_op jit(solution)/shard_map/dot_general | solution.py:28
  177.1 2.2 convolution_convert_fusion.2.refs_21_
  179.3 2.2 fusion.6.refs_13_
  182.1 2.2 convert_multiply_fusion
  185.1 224.5 %gradients.1 = (bf16[3072,768]{1,0:T(8,128)(2,1)}, bf16[768,3072]{1,0:T(8,128)(2,1)}, bf16[768,768]{1,0:T(8,128)(2,1)}, bf16[768,2304]{1,0:T(8,128)(2,1)}, f32[8,768]{1,0:T(8,128)}, /*index=5*/f32[768,768]{1,0:T(8,128)}) custom-call(bf16[768,768]{1,0:T(8,128)(2,1)} %copy-done.6, bf16[768,768]{1,0:T(8,128)(2,1)} %copy-done.8, bf16[768,768]{1,0:T(8,128)(2,1)} %copy-done.10, ...), custom_call_target="tpu_custom_call" | custom-call | tf_op jit(solution)/shard_map/gradients/pallas_call | solution.py:749
  411.7 3.2 multiply_reduce_fusion.5
  418.3 4.1 convert_element_type.73
  422.8 5.0 %convert_element_type.75 = f32[768,3072]{1,0:T(8,128)} convert(bf16[768,3072]{1,0:T(8,128)(2,1)S(1)} %copy-done.24) | non-fusion elementwise | flops 2359296 | bytes 14155776 | tf_op jit(solution)/shard_map/convert_element_type | solution.py:866
  427.9 5.5 %convert_element_type.76 = f32[3072,768]{1,0:T(8,128)} convert(bf16[3072,768]{1,0:T(8,128)(2,1)S(1)} %bitcast.22) | non-fusion elementwise | flops 2359296 | bytes 14155776 | tf_op jit(solution)/shard_map/convert_element_type | solution.py:868
  (132 shorter events, 41.6 us)
Async XLA Ops:
  0.6 131.1 %copy-start = (bf16[768,768]{1,0:T(8,128)(2,1)S(1)}, bf16[768,768]{1,0:T(8,128)(2,1)}, u32[]{:S(2)}) copy-start(bf16[768,768]{1,0:T(8,128)(2,1)} %param.17) | copy-start | bytes 3538948
  0.7 5.0 %copy-start.26 = (f32[768,768]{1,0:T(8,128)S(1)}, f32[768,768]{1,0:T(8,128)}, u32[]{:S(2)}) copy-start(f32[768,768]{1,0:T(8,128)} %param.12) | copy-start | bytes 7077892
  6.4 15.9 %copy-start.30 = (s32[3072]{0:T(1024)S(1)}, s32[3072]{0:T(1024)}, u32[]{:S(2)}) copy-start(s32[3072]{0:T(1024)} %param.14) | copy-start | bytes 36868
  7.4 30.8 %copy-start.3 = (bf16[768,768]{1,0:T(8,128)(2,1)}, bf16[768,768]{1,0:T(8,128)(2,1)S(1)}, u32[]{:S(2)}) copy-start(bf16[768,768]{1,0:T(8,128)(2,1)S(1)} %multiply_convert_fusion.2.refs_0_.refs_8_) | copy-start | bytes 3538948
  7.4 29.1 %collective-permute-start = (bf16[768,768]{1,0:T(8,128)(2,1)S(1)}, bf16[768,768]{1,0:T(8,128)(2,1)}, u32[]{:S(2)}, u32[]{:S(2)}) collective-permute-start(bf16[768,768]{1,0:T(8,128)(2,1)S(1)} %multiply_convert_fusion.2.refs_0_.refs_8_), channel_id=1, source_target_pairs={{0,1},{1,0},{2,3},{3,2},{4,5},{5,4},{6,7},{7,6},{8,9},{9,8},{10,11... | collective-permute-start | bytes 3538952 | tf_op jit(solution)/shard_map/ppermute | solution.py:781
  10.5 46.4 %collective-permute-start.3 = (bf16[768,768]{1,0:T(8,128)(2,1)S(1)}, bf16[768,768]{1,0:T(8,128)(2,1)}, u32[]{:S(2)}, u32[]{:S(2)}) collective-permute-start(bf16[768,768]{1,0:T(8,128)(2,1)S(1)} %multiply_convert_fusion.2.refs_0_.refs_8_), channel_id=1, source_target_pairs={{1,2},{2,1},{5,6},{6,5},{9,10},{10,9},{13,14},{14,13},{17,18},{18,... | collective-permute-start | bytes 3538952 | tf_op jit(solution)/shard_map/ppermute | solution.py:781
  22.5 91.0 %copy-start.17 = (s32[1,768]{1,0:T(1,128)}, s32[1,768]{1,0:T(1,128)S(1)}, u32[]{:S(2)}) copy-start(s32[1,768]{1,0:T(1,128)S(1)} %broadcast_in_dim.13.refs_5_.refs_17_) | copy-start | bytes 9220
  24.8 13.4 %copy-start.15 = (s32[768,1]{1,0:T(8,128)S(1)}, s32[768,1]{1,0:T(8,128)}, u32[]{:S(2)}) copy-start(s32[768,1]{1,0:T(8,128)} %copy.35.refs_4_) | copy-start | bytes 9220
  27.2 27.5 %copy-start.4 = (bf16[768,768]{1,0:T(8,128)(2,1)}, bf16[768,768]{1,0:T(8,128)(2,1)S(1)}, u32[]{:S(2)}) copy-start(bf16[768,768]{1,0:T(8,128)(2,1)S(1)} %convolution_convert_fusion.4.refs_3_.refs_12_) | copy-start | bytes 3538948
  36.5 23.3 %collective-permute-start.1 = (bf16[768,768]{1,0:T(8,128)(2,1)}, bf16[768,768]{1,0:T(8,128)(2,1)}, u32[]{:S(2)}, u32[]{:S(2)}) collective-permute-start(bf16[768,768]{1,0:T(8,128)(2,1)} %collective-permute-done.refs_0_.refs_9_), channel_id=1, source_target_pairs={{1,2},{2,1},{5,6},{6,5},{9,10},{10,9},{13,14},{14,13},{17,18},{18,... | collective-permute-start | bytes 3538952 | tf_op jit(solution)/shard_map/ppermute | solution.py:781
  56.8 31.9 %collective-permute-start.4 = (bf16[768,768]{1,0:T(8,128)(2,1)}, bf16[768,768]{1,0:T(8,128)(2,1)S(1)}, u32[]{:S(2)}, u32[]{:S(2)}) collective-permute-start(bf16[768,768]{1,0:T(8,128)(2,1)} %collective-permute-done.3), channel_id=1, source_target_pairs={{1,0},{2,3},{5,4},{6,7},{9,8},{10,11},{13,12},{14,15},{17,16},{18,... | collective-permute-start | bytes 3538952 | tf_op jit(solution)/shard_map/ppermute | solution.py:781
  59.8 52.1 %collective-permute-start.2 = (bf16[768,768]{1,0:T(8,128)(2,1)}, bf16[768,768]{1,0:T(8,128)(2,1)S(1)}, u32[]{:S(2)}, u32[]{:S(2)}) collective-permute-start(bf16[768,768]{1,0:T(8,128)(2,1)} %collective-permute-done.1), channel_id=1, source_target_pairs={{1,0},{2,3},{5,4},{6,7},{9,8},{10,11},{13,12},{14,15},{17,16},{18,... | collective-permute-start | bytes 3538952 | tf_op jit(solution)/shard_map/ppermute | solution.py:781
  90.3 17.4 %copy-start.1 = (bf16[768,768]{1,0:T(8,128)(2,1)}, bf16[768,768]{1,0:T(8,128)(2,1)S(1)}, u32[]{:S(2)}) copy-start(bf16[768,768]{1,0:T(8,128)(2,1)S(1)} %add.84.refs_0_.refs_10_) | copy-start | bytes 3538948
  113.5 18.2 %copy-start.2 = (bf16[768,768]{1,0:T(8,128)(2,1)}, bf16[768,768]{1,0:T(8,128)(2,1)S(1)}, u32[]{:S(2)}) copy-start(bf16[768,768]{1,0:T(8,128)(2,1)S(1)} %add.80.refs_0_.refs_11_) | copy-start | bytes 3538948
  113.5 18.2 %copy-start.19 = (f32[768,768]{1,0:T(8,128)S(1)}, f32[768,768]{1,0:T(8,128)}, u32[]{:S(2)}) copy-start(f32[768,768]{1,0:T(8,128)} %copy-done.18) | copy-start | bytes 7077892
  133.2 8.9 %slice-start.2 = ((s8[4718592]{0:T(1024)(128)(4,1)}), s8[4194304]{0:T(1024)(128)(4,1)S(1)}, s32[]{:S(2)}) async-start(s8[4718592]{0:T(1024)(128)(4,1)} %bitcast.23), calls=%async_computation.2 | async-start | bytes 8388608
  134.9 7.2 %slice-start.3 = ((s8[4718592]{0:T(1024)(128)(4,1)}), s8[524288]{0:T(1024)(128)(4,1)S(1)}, s32[]{:S(2)}) async-start(s8[4718592]{0:T(1024)(128)(4,1)} %bitcast.23), calls=%async_computation.3 | async-start | bytes 1048576
  142.1 5.3 %copy-start.27 = (f32[768,768]{1,0:T(8,128)S(1)}, f32[768,768]{1,0:T(8,128)}, u32[]{:S(2)}) copy-start(f32[768,768]{1,0:T(8,128)} %param.22) | copy-start | bytes 7077892
  163.0 6.7 %copy-start.33 = (bf16[768,3072]{1,0:T(8,128)(2,1)S(1)}, bf16[768,3072]{1,0:T(8,128)(2,1)}, u32[]{:S(2)}) copy-start(bf16[768,3072]{1,0:T(8,128)(2,1)} %get-tuple-element.83) | copy-start | bytes 14155780
  418.3 9.6 %slice-start = ((s8[4718592]{0:T(1024)(128)(4,1)}), s8[4194304]{0:T(1024)(128)(4,1)S(1)}, s32[]{:S(2)}) async-start(s8[4718592]{0:T(1024)(128)(4,1)} %bitcast.21), calls=%async_computation | async-start | bytes 8388608
  422.8 5.1 %slice-start.1 = ((s8[4718592]{0:T(1024)(128)(4,1)}), s8[524288]{0:T(1024)(128)(4,1)S(1)}, s32[]{:S(2)}) async-start(s8[4718592]{0:T(1024)(128)(4,1)} %bitcast.21), calls=%async_computation.1 | async-start | bytes 1048576
  427.9 5.5 %copy-start.20 = (f32[768,768]{1,0:T(8,128)S(1)}, f32[768,768]{1,0:T(8,128)}, u32[]{:S(2)}) copy-start(f32[768,768]{1,0:T(8,128)} %copy-done.18) | copy-start | bytes 7077892
  427.9 5.5 %copy-start.22 = (f32[768,768]{1,0:T(8,128)S(1)}, f32[768,768]{1,0:T(8,128)}, u32[]{:S(2)}) copy-start(f32[768,768]{1,0:T(8,128)} %copy-done.21) | copy-start | bytes 7077892
  427.9 6.4 %copy-start.23 = (f32[768,768]{1,0:T(8,128)S(1)}, f32[768,768]{1,0:T(8,128)}, u32[]{:S(2)}) copy-start(f32[768,768]{1,0:T(8,128)} %get-tuple-element.55) | copy-start | bytes 7077892
  (21 other events, 38.4 us)

commit v5 on v4

--- a/solution.py
+++ b/solution.py
@@ -82,112 +82,6 @@
 
 def columns_of(rows, first=0):
     return pl.BlockSpec((rows, PAIR), lambda pair: (0, pair + first))
-
-
-def forward_kernel(first, last, *refs):
-    a_ref, wk_ref, wv_ref, q_ref, key_clip, query_clip = refs[:6]
-    refs = refs[6:]
-    if not first:
-        acc_in, top_in, total_in = refs[:3]
-        refs = refs[3:]
-    k_ref, v_ref, acc_ref, top_ref, total_ref = refs[:5]
-    attn_ref = refs[5] if last else None
-    rows = q_ref.shape[0]
-    kv = dot(a_ref[...], jnp.concatenate([wk_ref[...], wv_ref[...]], axis=1), NN).astype(LOW)
-    key, value = kv[:, :PAIR], kv[:, PAIR:]
-    k_ref[...] = key
-    v_ref[...] = value
-    value_t = value.T
-    ones = jnp.ones((16, rows), LOW)
-    value_rows = [
-        jnp.concatenate([value_t[head * HEAD : (head + 1) * HEAD], ones], axis=0) for head in range(2)
-    ]
-    key_side, query_side = score_sides(key, q_ref[...])
-
-    def scores(start, head):
-        stop = start + QUERY_BLOCK
-        result = dot(key_side, query_side[head][start:stop], NT)
-        return jnp.where(key_clip[...] == query_clip[:, start:stop], result, MASKED)
-
-    def weights(start, head, result):
-        stop = start + QUERY_BLOCK
-        top = jnp.max(result, axis=0, keepdims=True)
-        if not first:
-            top = jnp.maximum(top, top_in[head : head + 1, start:stop])
-        return jnp.exp2(result - top).astype(LOW), top
-
-    def attend(start, head, expd, top):
-        stop = start + QUERY_BLOCK
-        lanes, row = slice(head * HEAD, (head + 1) * HEAD), slice(head, head + 1)
-        result = dot(value_rows[head], expd, NN)
-        acc, total = result[:HEAD], result[HEAD : HEAD + 1]
-        if not first:
-            shrink = jnp.exp2(top_in[row, start:stop] - top)
-            acc = acc_in[lanes, start:stop] * shrink + acc
-            total = total_in[row, start:stop] * shrink + total
-        if last:
-            acc = acc * (1.0 / total)
-            top = top + jnp.log(total) * LOG2E
-        acc_ref[lanes, start:stop] = acc
-        top_ref[row, start:stop] = top
-        total_ref[row, start:stop] = total
-
-    items = work_items(rows)
-    result = scores(*items[0])
-    before = None
-    for index, item in enumerate(items):
-        following = scores(*items[index + 1]) if index + 1 < len(items) else None
-        done = weights(*item, result)
-        if before is not None:
-            attend(*before)
-        before = (*item, *done)
-        result = following
-    attend(*before)
-    if last:
-        attn_ref[...] = acc_ref[...].T.astype(LOW)
-
-
-def forward_call(first, last, a_shard, w_qkv, query, key_clip, query_clip, state):
-    rows, width = query.shape
-    pairs = width // PAIR
-    across = pl.BlockSpec((PAIR, rows), lambda pair: (pair, 0))
-    line = pl.BlockSpec((None, 2, rows), lambda pair: (pair, 0, 0))
-    state_specs = [across, line, line]
-    state_shapes = [
-        jax.ShapeDtypeStruct((width, rows), WIDE),
-        jax.ShapeDtypeStruct((pairs, 2, rows), WIDE),
-        jax.ShapeDtypeStruct((pairs, 2, rows), WIDE),
-    ]
-    in_specs = [
-        whole(rows, width),
-        columns_of(width, pairs),
-        columns_of(width, 2 * pairs),
-        columns_of(rows),
-        whole(rows, 1),
-        whole(1, rows),
-    ]
-    operands = [a_shard, w_qkv, w_qkv, query, key_clip, query_clip]
-    if not first:
-        in_specs += state_specs
-        operands += list(state)
-    low_rows = jax.ShapeDtypeStruct((rows, width), LOW)
-    out_specs = [columns_of(rows), columns_of(rows), *state_specs]
-    out_shape = [low_rows, low_rows, *state_shapes]
-    if last:
-        out_specs.append(columns_of(rows))
-        out_shape.append(low_rows)
-    return pl.pallas_call(
-        functools.partial(forward_kernel, first, last),
-        grid=(pairs,),
-        in_specs=in_specs,
-        out_specs=out_specs,
-        out_shape=out_shape,
-        name="attend",
-        cost_estimate=pl.CostEstimate(
-            flops=20 * rows * rows * width, bytes_accessed=24 * rows * width, transcendentals=0
-        ),
-        compiler_params=pltpu.CompilerParams(vmem_limit_bytes=48 * 2**20),
-    )(*operands)
 
 
 def backward_pair(key, value, query, grad_t, lse, row_dots, key_clip, query_clip, add):
@@ -429,6 +323,233 @@
     pl.semaphore_wait(barrier, len(devices))
 
 
+PASS_NEAR = (2, 4, 5, 6, 6, 6)
+PASS_FAR = (10, 11, 12, 13, 15, 16)
+
+
+def attention_kernel(*refs):
+    a_in, w_ref, clips, query_clip = refs[:4]
+    a_out, k_out, v_out, q_ref, acc_ref, lse_ref, attn_ref = refs[4:11]
+    a_all, top_all, total_all, kv_slot, clip_slot = refs[11:16]
+    a_sems, kv_sems, clip_sem, line_sends, line_receives = refs[16:]
+    rows, width = q_ref.shape
+    pairs = width // PAIR
+    pieces = 4 * pairs
+    chunk_rows = rows // pairs
+    group, place = lax.axis_index("dp"), lax.axis_index("blk")
+    near = (group, place + 1 - 2 * (place % 2))
+    across = (group, 3 - place)
+    at_end = place % 3 == 0
+    at_middle = jnp.logical_not(at_end)
+
+    def line_copy(channel, chunk, source, target, device):
+        here = pl.ds(pl.multiple_of(chunk * chunk_rows, chunk_rows), chunk_rows)
+        return pltpu.make_async_remote_copy(
+            src_ref=source.at[here],
+            dst_ref=a_all.at[target, here],
+            send_sem=line_sends.at[channel, chunk],
+            recv_sem=line_receives.at[channel, chunk],
+            device_id=device,
+            device_id_type=MESH,
+        )
+
+    channels = (
+        lambda chunk: line_copy(0, chunk, a_in, 1, near),
+        lambda chunk: line_copy(1, chunk, a_in, 2, across),
+        lambda chunk: line_copy(2, chunk, a_all.at[2], 2, near),
+        lambda chunk: line_copy(3, chunk, a_all.at[1], 3, across),
+        lambda chunk: line_copy(4, chunk, a_all.at[3], 3, near),
+    )
+    load = pltpu.make_async_copy(a_in, a_all.at[0], a_sems.at[4])
+    load.start()
+    barrier = pltpu.get_barrier_semaphore()
+    for device in (near, across):
+        pl.semaphore_signal(barrier, inc=1, device_id=device, device_id_type=MESH)
+    pl.semaphore_wait(barrier, 2)
+    for chunk in range(pairs):
+        channels[0](chunk).start()
+
+    @pl.when(at_middle)
+    def _():
+        for chunk in range(pairs):
+            channels[1](chunk).start()
+
+    top_all[...] = jnp.full_like(top_all, -1.0e30)
+    total_all[...] = jnp.zeros_like(total_all)
+    acc_ref[...] = jnp.zeros_like(acc_ref)
+
+    def keep(shard):
+        return pltpu.make_async_copy(a_all.at[shard], a_out.at[shard], a_sems.at[shard])
+
+    def clip_copy(turn):
+        source = clips.at[pl.ds(pl.multiple_of(turn * rows, 8), rows)]
+        return pltpu.make_async_copy(source, clip_slot, clip_sem)
+
+    def pair_columns(pair):
+        return pl.ds(pl.multiple_of(pair * PAIR, PAIR), PAIR)
+
+    def kv_copies(turn, pair, slot):
+        return [
+            pltpu.make_async_copy(
+                kv_slot.at[slot, side], target.at[turn, :, pair_columns(pair)], kv_sems.at[slot, side]
+            )
+            for side, target in enumerate((k_out, v_out))
+        ]
+
+    load.wait()
+    keep(0).start()
+
+    @pl.loop(0, pieces)
+    def _(piece):
+        turn, pair, slot = piece // pairs, piece % pairs, piece % 2
+        for chunk, when in enumerate(PASS_NEAR):
+
+            @pl.when(jnp.logical_and(piece == when, at_middle))
+            def _():
+                channels[0](chunk).wait_recv()
+                channels[3](chunk).start()
+                channels[1](chunk).wait_recv()
+                channels[2](chunk).start()
+
+        for chunk, when in enumerate(PASS_FAR):
+
+            @pl.when(jnp.logical_and(piece == when, at_middle))
+            def _():
+                channels[3](chunk).wait_recv()
+                channels[4](chunk).start()
+
+        for shard, channel in ((1, 0), (2, 2), (3, 4)):
+
+            @pl.when(jnp.logical_and(piece == shard * pairs, at_end))
+            def _():
+                for chunk in range(pairs):
+                    channels[channel](chunk).wait_recv()
+
+            @pl.when(piece == shard * pairs)
+            def _():
+                keep(shard).start()
+
+        @pl.when(pair == 0)
+        def _():
+            clip_copy(turn).start()
+            clip_copy(turn).wait()
+
+        @pl.when(piece >= 2)
+        def _():
+            for copy in kv_copies(turn, pair, slot):
+                copy.wait()
+
+        columns = pair_columns(pair)
+
+        @pl.when(turn == 0)
+        def _():
+            q_ref[:, columns] = dot(a_all[0], w_ref[:, columns], NN).astype(LOW)
+
+        w_pair = jnp.concatenate(
+            [w_ref[:, pair_columns(pair + pairs)], w_ref[:, pair_columns(pair + 2 * pairs)]], axis=1
+        )
+        kv = dot(a_all[turn], w_pair, NN).astype(LOW)
+        key, value = kv[:, :PAIR], kv[:, PAIR:]
+        kv_slot[slot, 0] = key
+        kv_slot[slot, 1] = value
+        for copy in kv_copies(turn, pair, slot):
+            copy.start()
+        value_t = value.T
+        ones = jnp.ones((16, rows), LOW)
+        value_rows = [
+            jnp.concatenate([value_t[head * HEAD : (head + 1) * HEAD], ones], axis=0)
+            for head in range(2)
+        ]
+        key_side, query_side = score_sides(key, q_ref[:, columns])
+        key_clip = clip_slot[...]
+
+        def scores(start, head):
+            stop = start + QUERY_BLOCK
+            result = dot(key_side, query_side[head][start:stop], NT)
+            return jnp.where(key_clip == query_clip[:, start:stop], result, MASKED)
+
+        def weights(start, head, result):
+            here = slice(start, start + QUERY_BLOCK)
+            before = top_all[pair, head : head + 1, here]
+            top = jnp.maximum(before, jnp.max(result, axis=0, keepdims=True))
+            top_all[pair, head : head + 1, here] = top
+            return jnp.exp2(result - top).astype(LOW), jnp.exp2(before - top)
+
+        def attend(start, head, expd, shrink):
+            here, row = slice(start, start + QUERY_BLOCK), slice(head, head + 1)
+            lanes = pl.ds(pl.multiple_of(pair * PAIR + head * HEAD, HEAD), HEAD)
+            result = dot(value_rows[head], expd, NN)
+            acc_ref[lanes, here] = acc_ref[lanes, here] * shrink + result[:HEAD]
+            total_all[pair, row, here] = total_all[pair, row, here] * shrink + result[HEAD : HEAD + 1]
+
+        items = work_items(rows)
+        result = scores(*items[0])
+        before = None
+        for index, item in enumerate(items):
+            following = scores(*items[index + 1]) if index + 1 < len(items) else None
+            done = weights(*item, result)
+            if before is not None:
+                attend(*before)
+            before = (*item, *done)
+            result = following
+        attend(*before)
+
+        @pl.when(turn == 3)
+        def _():
+            for head in range(2):
+                lanes = pl.ds(pl.multiple_of(pair * PAIR + head * HEAD, HEAD), HEAD)
+                total = total_all[pair, head : head + 1]
+                acc_ref[lanes] = acc_ref[lanes] * (1.0 / total)
+                lse_ref[pair, head : head + 1] = top_all[pair, head : head + 1] + jnp.log(total) * LOG2E
+            attn_ref[:, columns] = acc_ref[columns].T.astype(LOW)
+
+    for slot in range(2):
+        for copy in kv_copies(3, pairs - 2 + slot, slot):
+            copy.wait()
+    for shard in range(4):
+        keep(shard).wait()
+    for chunk in range(pairs):
+        channels[0](chunk).wait_send()
+
+    @pl.when(at_middle)
+    def _():
+        for channel in channels[1:]:
+            for chunk in range(pairs):
+                channel(chunk).wait_send()
+
+
+def attention_call(a_low, w_qkv, clips, query_clip):
+    rows, width = a_low.shape
+    pairs = width // PAIR
+    anywhere = pl.BlockSpec(memory_space=pl.ANY)
+    inside = pl.BlockSpec(memory_space=pltpu.VMEM)
+    four = jax.ShapeDtypeStruct((4, rows, width), LOW)
+    square = jax.ShapeDtypeStruct((rows, width), LOW)
+    lines = jax.ShapeDtypeStruct((pairs, 2, rows), WIDE)
+    return pl.pallas_call(
+        attention_kernel,
+        in_specs=[anywhere, inside, anywhere, inside],
+        out_specs=[anywhere] * 3 + [inside] * 4,
+        out_shape=[four, four, four, square, jax.ShapeDtypeStruct((width, rows), WIDE), lines, square],
+        scratch_shapes=[
+            pltpu.VMEM((4, rows, width), LOW),
+            pltpu.VMEM((pairs, 2, rows), WIDE),
+            pltpu.VMEM((pairs, 2, rows), WIDE),
+            pltpu.VMEM((2, 2, rows, PAIR), LOW),
+            pltpu.VMEM((rows, 1), clips.dtype),
+            pltpu.SemaphoreType.DMA((5,)),
+            pltpu.SemaphoreType.DMA((2, 2)),
+            pltpu.SemaphoreType.DMA,
+            pltpu.SemaphoreType.DMA((5, pairs)),
+            pltpu.SemaphoreType.DMA((5, pairs)),
+        ],
+        name="attention",
+        compiler_params=pltpu.CompilerParams(
+            collective_id=2, has_side_effects=True, vmem_limit_bytes=48 * 2**20
+        ),
+    )(a_low, w_qkv, clips, query_clip)
+
+
 PARTS = (
     ("down", (0, 0), (1536, 384), "rrrrr", 0, (1, 3, 7, 9, 10, 12, 14, 15, 17, 18)),
     ("down", (0, 384), (1536, 384), "rrrrr", 1, (1, 3, 7, 8, 9, 11, 12, 14, 17, 18)),
@@ -447,11 +568,11 @@
 
 
 def gradient_kernel(*refs):
-    keys, values, shards = refs[:4], refs[4:8], refs[8:12]
-    q_ref, grad_ref, lse_ref, dots_ref, clips, query_clip, w_ref = refs[12:19]
-    down_in, up_in, out_in, small_in = refs[19:23]
-    down_out, up_out, out_out, qkv_out, small_out, input_out = refs[23:29]
-    refs = refs[29:]
+    keys, values, shards = refs[:3]
+    q_ref, grad_ref, lse_ref, dots_ref, clips, query_clip, w_ref = refs[3:10]
+    down_in, up_in, out_in, small_in = refs[10:14]
+    down_out, up_out, out_out, qkv_out, small_out, input_out = refs[14:20]
+    refs = refs[20:]
     kv_slot, a_slot, dq_sum, dk_sum, dv_sum, dk_all, dv_all, grad_k, grad_v, parts = refs[:10]
     from_near, from_across, qkv_term, clip_slot, small_arrived = refs[10:15]
     input_sum = dq_sum
@@ -530,16 +651,16 @@
     def kv_copies(shard, pair, slot):
         return [
             pltpu.make_async_copy(
-                source[shard].at[:, pair_columns(pair)], kv_slot.at[slot, side], kv_sems.at[slot, side]
+                source.at[shard, :, pair_columns(pair)], kv_slot.at[slot, side], kv_sems.at[slot, side]
             )
             for side, source in enumerate((keys, values))
         ]
 
     def a_copy(shard):
-        return pltpu.make_async_copy(shards[shard], a_slot, a_sem)
+        return pltpu.make_async_copy(shards.at[shard], a_slot, a_sem)
 
     def clip_copy(turn):
-        source = clips.at[pl.ds(pl.multiple_of(turn * rows, 8), rows)]
+        source = clips.at[pl.ds(pl.multiple_of((3 - turn) * rows, 8), rows)]
         return pltpu.make_async_copy(source, clip_slot, clip_sem)
 
     def of_pairs(stack):
@@ -570,21 +691,23 @@
     def _(piece):
         turn, pair, slot = piece // pairs, piece % pairs, piece % 2
 
-        def at(when, *actions, also=None):
-            @pl.when(piece == when if also is None else jnp.logical_and(piece == when, also))
+        def at(when, *actions):
+            @pl.when(piece == when)
             def _():
                 for action in actions:
                     action()
 
-        for shard in range(4):
-            following = piece + 1
-
-            @pl.when(jnp.logical_and(following // pairs == 3 - shard, following < pieces))
-            def _():
-                for copy in kv_copies(shard, following % pairs, following % 2):
-                    copy.start()
-
-            at((3 - shard) * pairs + 1, lambda: a_copy(shard).start())
+        following = piece + 1
+
+        @pl.when(following < pieces)
+        def _():
+            for copy in kv_copies(3 - following // pairs, following % pairs, following % 2):
+                copy.start()
+
+        @pl.when(pair == 1)
+        def _():
+            a_copy(3 - turn).start()
+
         for when in range(pieces):
             ends = [
                 functools.partial(each.turn, tick)
@@ -748,7 +871,7 @@
     like = lambda array: jax.ShapeDtypeStruct(array.shape, array.dtype)
     return pl.pallas_call(
         gradient_kernel,
-        in_specs=[anywhere] * 12 + [inside] * 4 + [anywhere] + [inside] * 2 + [anywhere] * 3 + [inside],
+        in_specs=[anywhere] * 3 + [inside] * 4 + [anywhere] + [inside] * 2 + [anywhere] * 3 + [inside],
         out_specs=[anywhere] * 4 + [inside, anywhere],
         out_shape=[
             like(grad_down),
@@ -764,7 +887,7 @@
             collective_id=1, has_side_effects=True, vmem_limit_bytes=62 * 2**20
         ),
     )(
-        *keys, *values, *shards, query, grad_t, lse, row_dots, clips, query_clip, w_qkv,
+        keys, values, shards, query, grad_t, lse, row_dots, clips, query_clip, w_qkv,
         grad_down, grad_up, grad_out, small,
     )
 
@@ -784,34 +907,15 @@
     normed_attn, inverse_attn = normalize(hidden)
     a_low = (normed_attn * gain_attn).astype(LOW)
 
-    near = [(0, 1), (1, 0), (2, 3), (3, 2)]
-    middle = [(1, 2), (2, 1)]
-    outward = [(1, 0), (2, 3)]
-    inward = [(0, 1), (3, 2)]
     table = jnp.array([[0, 1, 2, 3], [1, 0, 2, 3], [2, 3, 1, 0], [3, 2, 1, 0]], jnp.int32)
-    shard_1 = send(a_low, near)
-    shard_2_middle = send(a_low, middle)
-    shard_2 = shard_2_middle + send(shard_2_middle, outward)
-    shard_3_middle = send(shard_1, middle)
-    shard_3 = shard_3_middle + send(shard_3_middle, outward)
-    shards = [a_low, shard_1, shard_2, shard_3]
-
-    def clips_of(index):
-        other = lax.dynamic_index_in_dim(table[:, index], place, keepdims=False)
-        return lax.dynamic_slice_in_dim(segments, other * rows, rows)
-
-    clips = [clips_of(index)[:, None] for index in range(4)]
+    order = lax.dynamic_index_in_dim(table, place, keepdims=False)
+    clips = jnp.concatenate(
+        [lax.dynamic_slice_in_dim(segments, order[index] * rows, rows) for index in range(4)]
+    )[:, None]
     query_clip = lax.dynamic_slice_in_dim(segments, place * rows, rows)[None, :]
-
-    query = dot(a_low, w_query, NN).astype(LOW)
-    keys, values, state = [], [], None
-    for index in range(4):
-        key, value, *state = forward_call(
-            index == 0, index == 3, shards[index], w_qkv, query, clips[index], query_clip, state
-        )
-        keys.append(key)
-        values.append(value)
-    attended, lse, _, attn_low = state
+    shards, keys, values, query, attended, lse, attn_low = attention_call(
+        a_low, w_qkv, clips, query_clip
+    )
 
     resid = hidden + dot(attn_low, w_out, NN)
     normed_mlp, inverse_mlp = normalize(resid)
@@ -847,7 +951,7 @@
             d_attn_t,
             lse,
             row_dots,
-            jnp.concatenate(clips[::-1], axis=0),
+            clips,
             query_clip,
             w_qkv,
             grad_down,
@@ -880,12 +984,13 @@
             d_attn_t,
             lse,
             row_dots,
-            clips[index],
+            clips[index * rows : (index + 1) * rows],
             query_clip,
             w_qkv,
             dq,
         )
 
+    middle, outward, inward = [(1, 2), (2, 1)], [(1, 0), (2, 3)], [(0, 1), (3, 2)]
     dk_3, dv_3, dq, part_3 = back(3, None)
     far = send(part_3, inward)
     dk_2, dv_2, dq, part_2 = back(2, dq)

time: 444 us -> 426 us (0.959)
  Pallas kernels: 294 us -> 326 us
  waiting for transfers between devices: 16.8 us -> 0 us
  starting transfers between devices: 9.44 us -> 0 us
  local copies, waits for them, and re-layouts: 20 us -> 11 us
  between operations: 9.34 us -> 3.83 us
  other arithmetic: 38.1 us -> 33 us
    pallas_call x5 -> x2, Pallas kernels: 294 us -> 326 us  [the longest x1 222 us: gradient_call(): pl.pallas_call(gradient_kernel, in_specs=[anywhere] * 3 + [inside] * 4 +...]
    ppermute x5 -> x0, waiting for transfers between devices: 16.8 us -> none  [send(): return lax.ppermute(value, 'blk', pairs_of_places)]
    ppermute x5 -> x0, starting transfers between devices: 9.44 us -> none  [send(): return lax.ppermute(value, 'blk', pairs_of_places)]
    unnamed x80 -> x56, local copies, waits for them, and re-layouts: 12.6 us -> 5.13 us
    mul x3 -> x0, other arithmetic: 4.65 us -> none  [the longest x2 2.44 us: clips_of(): return lax.dynamic_slice_in_dim(segments, other * rows, rows)]
    dot_general x10 -> x9, matrix products: 48.9 us -> 47.8 us  [dot(): return lax.dot_general(left, right, dims, preferred_element_type=WIDE)]
  transfers between devices with their start and end apart: 5 -> 0, of which waited for: 3 -> 0; matrix products, arithmetic and copies ran while one was open for 2% -> 0% of each run, Pallas kernels for 12% -> 0%
where the time goes in v5:
time: 426 us; the launch traced here: 421 us
  Pallas kernels  326 us (77%)
  matrix products  47.8 us (11%)
  other arithmetic  33 us (8%)
  local copies, waits for them, and re-layouts  11 us (3%)
    pallas_call x1, Pallas kernels, gradient_call(): pl.pallas_call(gradient_kernel, in_specs=[anywhere] * 3 + [inside] * 4 +...  222 us
    pallas_call x1, Pallas kernels, attention_call(): pl.pallas_call(attention_kernel, in_specs=[anywhere, inside, anywhere, in...  103 us
    dot_general x9, matrix products, dot(): return lax.dot_general(left, right, dims, preferred_element_type=WIDE)  47.8 us

profile of v5, /device:TPU:0, one launch (start us, length us, event | category | flops | bytes accessed | tf_op | source)
XLA Modules:
  0.0 421.4 jit_solution(6989929379920132559)
XLA Ops:
  5.4 0.9 fusion.13
  6.3 1.7 copy.24.refs_2_.refs_7_
  8.0 4.2 multiply_sine_fusion
  13.6 1.2 copy-done.1
  14.8 103.4 %attention.1 = (bf16[4,768,768]{2,1,0:T(8,128)(2,1)}, bf16[4,768,768]{2,1,0:T(8,128)(2,1)}, bf16[4,768,768]{2,1,0:T(8,128)(2,1)}, bf16[768,768]{1,0:T(8,128)(2,1...) custom-call(bf16[768,768]{1,0:T(8,128)(2,1)S(1)} %multiply_convert_fusion.2.refs_0_, ...), custom_call_target="tpu_custom_call" | custom-call | tf_op jit(solution)/shard_map/attention/pallas_call | solution.py:529
  118.2 1.2 fusion.15
  119.9 1.7 slice-done.6
  121.8 7.7 %multiply_convert_fusion = (bf16[768,3072]{1,0:T(8,128)(2,1)}, f32[768,3072]{1,0:T(8,128)}) fusion(f32[3072]{0:T(1024)S(1)} %copy-done.18, bf16[768,3072]{1,0:T(8,128)(2,1)S(1)} %bitcast.29, f32[768,768]{1,0:T(8,128)S(1)} %get-tuple-element.56, f32[768]{0:T(1024)S(1)} %copy-done.17, f32[768]{0:T(1024)S(1)} %add_rsqrt_fusion, ...), kind=kOutput, calls=%fused_computation.8 | convolution fusion | flops 3640393728 | bytes 21255168 | tf_op jit(solution)/shard_map/dot_general | solution.py:28
  129.5 9.2 %convert_reduce_fusion = (f32[3072]{0:T(1024)S(1)}, bf16[768,3072]{1,0:T(8,128)(2,1)S(1)}) fusion(f32[768,3072]{1,0:T(8,128)} %get-tuple-element.58, f32[3072]{0:T(1024)S(1)} %copy-done.18, bf16[3072,768]{1,0:T(8,128)(2,1)S(1)} %bitcast.27, f32[768,768]{1,0:T(8,128)S(1)} %copy-done.12), kind=kOutput, calls=%fused_computation.7 | convolution fusion | flops 3655136256 | bytes 21258240 | tf_op jit(solution)/shard_map/dot_general | solution.py:28
  138.7 7.8 %convolution_add_fusion.1 = f32[768,768]{1,0:T(8,128)} fusion(f32[768,768]{1,0:T(8,128)S(1)} %get-tuple-element.56, bf16[768,3072]{1,0:T(8,128)(2,1)} %get-tuple-element.57, bf16[3072,768]{1,0:T(8,128)(2,1)S(1)} %bitcast.27), kind=kOutput, calls=%fused_computation.30 | convolution fusion | flops 3624468480 | bytes 14155776 | tf_op jit(solution)/shard_map/dot_general | solution.py:28
  146.4 5.8 %convolution_convert_fusion.1.refs_10_ = bf16[3072,768]{1,0:T(8,128)(2,1)} fusion(bf16[768,3072]{1,0:T(8,128)(2,1)S(1)} %copy-done.19, f32[768,768]{1,0:T(8,128)S(1)} %copy-done.12), kind=kOutput, calls=%fused_computation.11 | convolution fusion | flops 3626827776 | bytes 11796480 | tf_op jit(solution)/shard_map/dot_general | solution.py:28
  152.3 5.6 %multiply_reduce_fusion.1 = (f32[768]{0:T(1024)S(1)}, f32[768]{0:T(1024)S(1)}, f32[768]{0:T(1024)S(1)}, f32[768,768]{1,0:T(8,128)}) fusion(f32[768,768]{1,0:T(8,128)S(1)} %get-tuple-element.56, f32[768]{0:T(1024)S(1)} %add_rsqrt_fusion, f32[768]{0:T(1024)S(1)} %broadcast_multiply_fusion.4, f32[768]{0:T(1024)S(1)} %copy-done.17, ...), kind=kOutput, calls=%fused_computation.15 | convolution fusion | flops 3628594944 | bytes 14174208 | tf_op jit(solution)/shard_map/dot_general | solution.py:28
  157.9 6.2 %convolution_convert_fusion.refs_11_ = bf16[768,3072]{1,0:T(8,128)(2,1)} fusion(bf16[768,3072]{1,0:T(8,128)(2,1)S(1)} %get-tuple-element.63, f32[768,768]{1,0:T(8,128)S(1)} %get-tuple-element.56, f32[768]{0:T(1024)S(1)} %copy-done.17, f32[768]{0:T(1024)S(1)} %add_rsqrt_fusion, f32[768]{0:T(1024)S(1)} %broadcast_multiply_fusion.4), kind=kOutput, calls=%fused_computation.10 | convolution fusion | flops 3628597248 | bytes 11805696 | tf_op jit(solution)/shard_map/dot_general | solution.py:28
  164.7 3.5 multiply_add_fusion.1
  168.2 2.2 convolution_convert_fusion.2.refs_12_
  171.1 2.2 convert_multiply_fusion
  173.3 0.8 reduce_sum.105.refs_6_
  174.1 222.4 %gradients.1 = (bf16[3072,768]{1,0:T(8,128)(2,1)}, bf16[768,3072]{1,0:T(8,128)(2,1)}, bf16[768,768]{1,0:T(8,128)(2,1)}, bf16[768,2304]{1,0:T(8,128)(2,1)}, f32[8,768]{1,0:T(8,128)}, /*index=5*/f32[768,768]{1,0:T(8,128)}) custom-call(bf16[4,768,768]{2,1,0:T(8,128)(2,1)} %get-tuple-element.23.refs_0_, bf16[4,768,768]{2,1,0:T(8,128)(2,1)} %get-tuple-element.24.refs_1_, ...), custom_call_target="tpu_custom_call" | custom-call | tf_op jit(solution)/shard_map/gradients/pallas_call | solution.py:872
  396.5 3.3 multiply_reduce_fusion.5
  400.3 3.3 multiply_add_fusion
  405.4 1.6 convert_element_type.70
  407.5 4.1 convert_element_type.69
  411.6 5.0 %convert_element_type.71 = f32[768,3072]{1,0:T(8,128)} convert(bf16[768,3072]{1,0:T(8,128)(2,1)S(1)} %bitcast.24) | non-fusion elementwise | flops 2359296 | bytes 14155776 | tf_op jit(solution)/shard_map/convert_element_type | solution.py:970
  416.7 4.5 %convert_element_type.72 = f32[3072,768]{1,0:T(8,128)} convert(bf16[3072,768]{1,0:T(8,128)(2,1)S(1)} %bitcast.22) | non-fusion elementwise | flops 2359296 | bytes 14155776 | tf_op jit(solution)/shard_map/convert_element_type | solution.py:972
  (83 shorter events, 8.3 us)
Async XLA Ops:
  0.6 117.6 %copy-start = (bf16[768,768]{1,0:T(8,128)(2,1)S(1)}, bf16[768,768]{1,0:T(8,128)(2,1)}, u32[]{:S(2)}) copy-start(bf16[768,768]{1,0:T(8,128)(2,1)} %param.17) | copy-start | bytes 3538948
  6.3 7.3 %copy-start.4 = (s32[1,768]{1,0:T(1,128)}, s32[1,768]{1,0:T(1,128)S(1)}, u32[]{:S(2)}) copy-start(s32[1,768]{1,0:T(1,128)S(1)} %broadcast_in_dim.7.refs_3_.refs_8_) | copy-start | bytes 9220
  8.0 4.2 copy-start.11
  12.5 105.7 %copy-start.5 = (f32[768,768]{1,0:T(8,128)}, f32[768,768]{1,0:T(8,128)S(1)}, u32[]{:S(2)}) copy-start(f32[768,768]{1,0:T(8,128)S(1)} %get-tuple-element.43) | copy-start | bytes 7077892
  118.2 3.5 slice-start.6
  118.2 3.6 slice-start.7
  119.4 38.4 %copy-start.7 = (f32[768,768]{1,0:T(8,128)}, f32[768,768]{1,0:T(8,128)S(1)}, u32[]{:S(2)}) copy-start(f32[768,768]{1,0:T(8,128)S(1)} %get-tuple-element.56) | copy-start | bytes 7077892
  119.5 2.3 copy-start.17
  119.5 2.3 copy-start.18
  119.5 10.0 %slice-start.4 = ((s8[4718592]{0:T(1024)(128)(4,1)}), s8[4194304]{0:T(1024)(128)(4,1)S(1)}, s32[]{:S(2)}) async-start(s8[4718592]{0:T(1024)(128)(4,1)} %bitcast.26), calls=%async_computation.4 | async-start | bytes 8388608
  121.8 7.7 %copy-start.12 = (f32[768,768]{1,0:T(8,128)S(1)}, f32[768,768]{1,0:T(8,128)}, u32[]{:S(2)}) copy-start(f32[768,768]{1,0:T(8,128)} %param.22) | copy-start | bytes 7077892
  121.8 7.7 %slice-start.5 = ((s8[4718592]{0:T(1024)(128)(4,1)}), s8[524288]{0:T(1024)(128)(4,1)S(1)}, s32[]{:S(2)}) async-start(s8[4718592]{0:T(1024)(128)(4,1)} %bitcast.26), calls=%async_computation.5 | async-start | bytes 1048576
  138.6 7.8 %copy-start.19 = (bf16[768,3072]{1,0:T(8,128)(2,1)S(1)}, bf16[768,3072]{1,0:T(8,128)(2,1)}, u32[]{:S(2)}) copy-start(bf16[768,3072]{1,0:T(8,128)(2,1)} %get-tuple-element.57) | copy-start | bytes 14155780
  168.2 2.2 copy-start.8
  168.2 2.9 copy-start.13
  396.5 3.3 copy-start.6
  396.5 3.8 copy-start.9
  400.3 3.3 copy-start.16
  400.3 5.1 %copy-start.14 = (bf16[768,768]{1,0:T(8,128)(2,1)S(1)}, bf16[768,768]{1,0:T(8,128)(2,1)}, u32[]{:S(2)}) copy-start(bf16[768,768]{1,0:T(8,128)(2,1)} %get-tuple-element.32) | copy-start | bytes 3538948
  400.3 11.3 %slice-start.2 = ((s8[4718592]{0:T(1024)(128)(4,1)}), s8[524288]{0:T(1024)(128)(4,1)S(1)}, s32[]{:S(2)}) async-start(s8[4718592]{0:T(1024)(128)(4,1)} %bitcast.23), calls=%async_computation.2 | async-start | bytes 1048576
  404.8 2.7 copy-start.10
  405.4 6.2 %slice-start.3 = ((s8[4718592]{0:T(1024)(128)(4,1)}), s8[4194304]{0:T(1024)(128)(4,1)S(1)}, s32[]{:S(2)}) async-start(s8[4718592]{0:T(1024)(128)(4,1)} %bitcast.23), calls=%async_computation.3 | async-start | bytes 8388608
  407.5 9.2 %slice-start = ((s8[4718592]{0:T(1024)(128)(4,1)}), s8[4194304]{0:T(1024)(128)(4,1)S(1)}, s32[]{:S(2)}) async-start(s8[4718592]{0:T(1024)(128)(4,1)} %bitcast.21), calls=%async_computation | async-start | bytes 8388608
  411.6 5.0 %slice-start.1 = ((s8[4718592]{0:T(1024)(128)(4,1)}), s8[524288]{0:T(1024)(128)(4,1)S(1)}, s32[]{:S(2)}) async-start(s8[4718592]{0:T(1024)(128)(4,1)} %bitcast.21), calls=%async_computation.1 | async-start | bytes 1048576
  (4 other events, 5.1 us)

commit v6 on v5

--- a/solution.py
+++ b/solution.py
@@ -548,6 +548,137 @@
             collective_id=2, has_side_effects=True, vmem_limit_bytes=48 * 2**20
         ),
     )(a_low, w_qkv, clips, query_clip)
+
+
+FF_BLOCK = 512
+ROW_BLOCK = 384
+
+
+def mlp_kernel(
+    hidden_ref,
+    attn_ref,
+    attended_ref,
+    cotangent_ref,
+    w_out_ref,
+    gain_ref,
+    w_up_ref,
+    b_up_ref,
+    w_down_ref,
+    outputs_ref,
+    d_resid_ref,
+    grad_t_ref,
+    dots_ref,
+    grad_down_ref,
+    grad_up_ref,
+    grad_out_ref,
+    grad_gain_ref,
+    grad_bias_ref,
+    normed_ref,
+    inverse_ref,
+    b_ref,
+    dy_ref,
+    db_ref,
+    z_ref,
+    d_pre_ref,
+):
+    block = pl.program_id(0)
+    rows = hidden_ref.shape[0]
+
+    @pl.when(block == 0)
+    def _():
+        resid = hidden_ref[...] + dot(attn_ref[...], w_out_ref[...], NN)
+        normed, inverse = normalize(resid)
+        normed_ref[...] = normed
+        inverse_ref[...] = inverse
+        b_ref[...] = (normed * gain_ref[...]).astype(LOW)
+        dy_ref[...] = cotangent_ref[...].astype(LOW)
+        outputs_ref[...] = resid
+        db_ref[...] = jnp.zeros_like(db_ref)
+
+    bias = jnp.zeros((1, FF_BLOCK), WIDE)
+    for start in range(0, rows, ROW_BLOCK):
+        here = slice(start, start + ROW_BLOCK)
+        pre_act = dot(b_ref[here], w_up_ref[...], NN) + b_up_ref[...]
+        cumulative = 0.5 * (1.0 + lax.erf(pre_act * 0.7071067811865476))
+        density = jnp.exp(-0.5 * pre_act * pre_act) * 0.3989422804014327
+        z_ref[here] = (pre_act * cumulative).astype(LOW)
+        d_gelu = dot(dy_ref[here], w_down_ref[...], NT)
+        d_pre = (d_gelu * (cumulative + pre_act * density)).astype(LOW)
+        d_pre_ref[here] = d_pre
+        bias += jnp.sum(d_pre.astype(WIDE), axis=0, keepdims=True)
+        outputs_ref[here] += dot(z_ref[here], w_down_ref[...], NN)
+        db_ref[here] += dot(d_pre, w_up_ref[...], NT)
+    grad_bias_ref[...] = bias
+    grad_down_ref[...] = dot(z_ref[...], dy_ref[...], TN).astype(LOW)
+    grad_up_ref[...] = dot(b_ref[...], d_pre_ref[...], TN).astype(LOW)
+
+    @pl.when(block == pl.num_programs(0) - 1)
+    def _():
+        normed, db = normed_ref[...], db_ref[...]
+        grad_gain_ref[...] = jnp.sum(db * normed, axis=0, keepdims=True)
+        d_resid = cotangent_ref[...] + norm_back(db * gain_ref[...], normed, inverse_ref[...])
+        d_resid_ref[...] = d_resid
+        dr_low = d_resid.astype(LOW)
+        grad_out_ref[...] = dot(attn_ref[...], dr_low, TN).astype(LOW)
+        grad_t = dot(w_out_ref[...], dr_low, NT).astype(LOW)
+        grad_t_ref[...] = grad_t
+        product = grad_t.astype(WIDE) * attended_ref[...]
+        for pair in range(dots_ref.shape[0]):
+            for head in range(2):
+                lanes = slice(pair * PAIR + head * HEAD, pair * PAIR + (head + 1) * HEAD)
+                dots_ref[pair, head : head + 1] = jnp.sum(product[lanes], axis=0, keepdims=True)
+
+
+def mlp_call(hidden, attn_low, attended, cotangent, w_out, gain_mlp, w_up, b_up, w_down):
+    rows, width = hidden.shape
+    hidden_units = w_up.shape[1]
+    pairs = width // PAIR
+    once = lambda *shape: pl.BlockSpec(
+        shape, lambda block: (0,) * len(shape), pipeline_mode=pl.Buffered(1)
+    )
+    square, line = once(rows, width), once(1, width)
+    up = pl.BlockSpec((width, FF_BLOCK), lambda block: (0, block))
+    down = pl.BlockSpec((FF_BLOCK, width), lambda block: (block, 0))
+    bias = pl.BlockSpec((1, FF_BLOCK), lambda block: (0, block))
+    wide = jax.ShapeDtypeStruct((rows, width), WIDE)
+    return pl.pallas_call(
+        mlp_kernel,
+        grid=(hidden_units // FF_BLOCK,),
+        in_specs=[square] * 4 + [once(width, width), line, up, bias, down],
+        out_specs=[
+            whole(rows, width),
+            whole(rows, width),
+            whole(width, rows),
+            whole(pairs, 2, rows),
+            down,
+            up,
+            whole(width, width),
+            whole(1, width),
+            bias,
+        ],
+        out_shape=[
+            wide,
+            wide,
+            jax.ShapeDtypeStruct((width, rows), LOW),
+            jax.ShapeDtypeStruct((pairs, 2, rows), WIDE),
+            jax.ShapeDtypeStruct(w_down.shape, LOW),
+            jax.ShapeDtypeStruct(w_up.shape, LOW),
+            jax.ShapeDtypeStruct((width, width), LOW),
+            jax.ShapeDtypeStruct((1, width), WIDE),
+            jax.ShapeDtypeStruct((1, hidden_units), WIDE),
+        ],
+        scratch_shapes=[
+            pltpu.VMEM((rows, width), WIDE),
+            pltpu.VMEM((rows, 1), WIDE),
+            pltpu.VMEM((rows, width), LOW),
+            pltpu.VMEM((rows, width), LOW),
+            pltpu.VMEM((rows, width), WIDE),
+            pltpu.VMEM((rows, FF_BLOCK), LOW),
+            pltpu.VMEM((rows, FF_BLOCK), LOW),
+        ],
+        name="mlp",
+        compiler_params=pltpu.CompilerParams(vmem_limit_bytes=56 * 2**20),
+    )(hidden, attn_low, attended, cotangent, w_out, gain_mlp[None], w_up, b_up[None], w_down)
 
 
 PARTS = (
@@ -917,29 +1048,18 @@
         a_low, w_qkv, clips, query_clip
     )
 
-    resid = hidden + dot(attn_low, w_out, NN)
-    normed_mlp, inverse_mlp = normalize(resid)
-    b_low = (normed_mlp * gain_mlp).astype(LOW)
-    pre_act = dot(b_low, w_up, NN) + b_up
-    cumulative = 0.5 * (1.0 + lax.erf(pre_act * 0.7071067811865476))
-    density = jnp.exp(-0.5 * pre_act * pre_act) * 0.3989422804014327
-    z_low = (pre_act * cumulative).astype(LOW)
-    outputs = resid + dot(z_low, w_down, NN)
-    dy_low = cotangent.astype(LOW)
-    grad_down = dot(z_low, dy_low, TN).astype(LOW)
-    d_gelu = dot(dy_low, w_down, NT)
-    d_pre = (d_gelu * (cumulative + pre_act * density)).astype(LOW)
-    grad_up = dot(b_low, d_pre, TN).astype(LOW)
-    grad_bias_up = jnp.sum(d_pre.astype(WIDE), axis=0)
-    d_normed = dot(d_pre, w_up, NT)
-    grad_gain_mlp = jnp.sum(d_normed * normed_mlp, axis=0)
-    d_resid = cotangent + norm_back(d_normed * gain_mlp, normed_mlp, inverse_mlp)
-    dr_low = d_resid.astype(LOW)
-    grad_out = dot(attn_low, dr_low, TN).astype(LOW)
-    d_attn_t = dot(w_out, dr_low, NT).astype(LOW)
-    row_dots = jnp.sum(
-        (d_attn_t.astype(WIDE) * attended).reshape(pairs, 2, HEAD, rows), axis=2
-    )
+    (
+        outputs,
+        d_resid,
+        d_attn_t,
+        row_dots,
+        grad_down,
+        grad_up,
+        grad_out,
+        grad_gain_mlp,
+        grad_bias_up,
+    ) = mlp_call(hidden, attn_low, attended, cotangent, w_out, gain_mlp, w_up, b_up, w_down)
+    grad_gain_mlp, grad_bias_up = grad_gain_mlp[0], grad_bias_up[0]
 
     if groups == 8 and rows == width:
         small = jnp.concatenate([jnp.zeros_like(gain_attn), grad_gain_mlp, grad_bias_up])

time: 426 us -> 405 us (0.951)
  matrix products: 47.8 us -> 0 us
  Pallas kernels: 326 us -> 361 us
    dot_general x9 -> x0, matrix products: 47.8 us -> none  [dot(): return lax.dot_general(left, right, dims, preferred_element_type=WIDE)]
    pallas_call x0 -> x1, Pallas kernels: none -> 36.4 us  [mlp_call(): pl.pallas_call(mlp_kernel, grid=(hidden_units // FF_BLOCK,), in_specs=[sq...]
where the time goes in v6:
time: 405 us; the launch traced here: 404 us
  Pallas kernels  361 us (89%)
  other arithmetic  29.8 us (7%)
  local copies, waits for them, and re-layouts  10.2 us (3%)
    pallas_call x1, Pallas kernels, gradient_call(): pl.pallas_call(gradient_kernel, in_specs=[anywhere] * 3 + [inside] * 4 +...  221 us
    pallas_call x1, Pallas kernels, attention_call(): pl.pallas_call(attention_kernel, in_specs=[anywhere, inside, anywhere, in...  103 us
    pallas_call x1, Pallas kernels, mlp_call(): pl.pallas_call(mlp_kernel, grid=(hidden_units // FF_BLOCK,), in_specs=[sq...  36.4 us

profile of v6, /device:TPU:0, one launch (start us, length us, event | category | flops | bytes accessed | tf_op | source)
XLA Modules:
  0.0 404.4 jit_solution(16200431672300431989)
XLA Ops:
  0.6 0.7 constant_dynamic-slice_fusion
  1.3 0.6 fusion.2
  4.6 1.3 broadcast_in_dim.12.gain_ref
  5.8 0.7 convert_element_type.20
  6.5 0.9 fusion.1
  8.0 4.2 %multiply_sine_fusion = (f32[768,384]{1,0:T(8,128)S(1)}, f32[768,384]{1,0:T(8,128)S(1)}) fusion(f32[384]{0:T(512)S(1)} %multiply_exponential_fusion, f32[768]{0:T(1024)S(1)} %convert_element_type.20), kind=kLoop, calls=%fused_computation.8 | loop fusion | flops 294912 | bytes 2363904 | tf_op jit(solution)/shard_map/sin | solution.py:35
  13.9 103.2 %attention.1 = (bf16[4,768,768]{2,1,0:T(8,128)(2,1)}, bf16[4,768,768]{2,1,0:T(8,128)(2,1)}, bf16[4,768,768]{2,1,0:T(8,128)(2,1)}, bf16[768,768]{1,0:T(8,128)(2,1...) custom-call(bf16[768,768]{1,0:T(8,128)(2,1)S(1)} %multiply_convert_fusion.refs_0_, ...), custom_call_target="tpu_custom_call" | custom-call | tf_op jit(solution)/shard_map/attention/pallas_call | solution.py:529
  117.1 1.1 copy-done.1
  118.2 1.0 copy-done.2
  119.2 0.6 copy-done.3
  119.9 36.4 %mlp.1 = (f32[768,768]{1,0:T(8,128)}, f32[768,768]{1,0:T(8,128)}, bf16[768,768]{1,0:T(8,128)(2,1)}, f32[6,2,768]{2,1,0:T(2,128)}, bf16[3072,768]{1,0:T(8,128)(2,...) custom-call(f32[768,768]{1,0:T(8,128)} %copy-done.5, ...), custom_call_target="tpu_custom_call" | custom-call | tf_op jit(solution)/shard_map/mlp/pallas_call | solution.py:644
  156.2 0.7 reduce
  156.9 0.7 pad_maximum_fusion
  157.7 0.6 pad.4.refs_13_
  158.3 221.4 %gradients.1 = (bf16[3072,768]{1,0:T(8,128)(2,1)}, bf16[768,3072]{1,0:T(8,128)(2,1)}, bf16[768,768]{1,0:T(8,128)(2,1)}, bf16[768,2304]{1,0:T(8,128)(2,1)}, f32[8,768]{1,0:T(8,128)}, /*index=5*/f32[768,768]{1,0:T(8,128)}) custom-call(bf16[4,768,768]{2,1,0:T(8,128)(2,1)} %get-tuple-element.35.refs_0_, bf16[4,768,768]{2,1,0:T(8,128)(2,1)} %get-tuple-element.36.refs_1_, ...), custom_call_target="tpu_custom_call" | custom-call | tf_op jit(solution)/shard_map/gradients/pallas_call | solution.py:1003
  379.7 3.3 multiply_reduce_fusion.2
  383.5 3.3 multiply_add_fusion
  386.9 0.6 slice_reduce_fusion
  387.5 0.6 reshape.68
  388.1 0.6 div.19
  388.7 1.6 convert_element_type.23
  390.8 4.1 %convert_element_type.22 = f32[768,2304]{1,0:T(8,128)} convert(bf16[768,2304]{1,0:T(8,128)(2,1)S(1)} %copy-done.8) | non-fusion elementwise | flops 1769472 | bytes 10616832 | tf_op jit(solution)/shard_map/convert_element_type | solution.py:1087
  394.9 5.0 %convert_element_type.24 = f32[768,3072]{1,0:T(8,128)} convert(bf16[768,3072]{1,0:T(8,128)(2,1)S(1)} %bitcast.10) | non-fusion elementwise | flops 2359296 | bytes 14155776 | tf_op jit(solution)/shard_map/convert_element_type | solution.py:1090
  399.9 4.5 %convert_element_type.25 = f32[3072,768]{1,0:T(8,128)} convert(bf16[3072,768]{1,0:T(8,128)(2,1)S(1)} %bitcast.8) | non-fusion elementwise | flops 2359296 | bytes 14155776 | tf_op jit(solution)/shard_map/convert_element_type | solution.py:1092
  (46 shorter events, 3.2 us)
Async XLA Ops:
  7.5 6.1 %copy-start.4 = (s32[1,768]{1,0:T(1,128)}, s32[1,768]{1,0:T(1,128)S(1)}, u32[]{:S(2)}) copy-start(s32[1,768]{1,0:T(1,128)S(1)} %broadcast_in_dim.11.refs_3_.refs_8_) | copy-start | bytes 9220
  8.0 5.6 %copy-start = (s32[3072,1]{1,0:T(8,128)}, s32[3072,1]{1,0:T(8,128)S(1)}, u32[]{:S(2)}) copy-start(s32[3072,1]{1,0:T(8,128)S(1)} %copy.21.refs_2_.refs_7_) | copy-start | bytes 36868
  8.0 4.2 %copy-start.9 = (f32[768,768]{1,0:T(8,128)S(1)}, f32[768,768]{1,0:T(8,128)}, u32[]{:S(2)}) copy-start(f32[768,768]{1,0:T(8,128)} %param.12) | copy-start | bytes 7077892
  12.5 1.4 copy-start.5
  12.5 0.7 copy-start.11
  117.1 1.1 copy-start.1
  118.2 1.0 copy-start.2
  119.2 0.6 copy-start.3
  379.7 3.3 copy-start.6
  379.7 3.8 copy-start.7
  383.5 3.3 copy-start.12
  383.5 5.2 %copy-start.10 = (bf16[768,768]{1,0:T(8,128)(2,1)S(1)}, bf16[768,768]{1,0:T(8,128)(2,1)}, u32[]{:S(2)}) copy-start(bf16[768,768]{1,0:T(8,128)(2,1)} %get-tuple-element.50) | copy-start | bytes 3538948
  383.5 11.4 %slice-start.2 = ((s8[4718592]{0:T(1024)(128)(4,1)}), s8[524288]{0:T(1024)(128)(4,1)S(1)}, s32[]{:S(2)}) async-start(s8[4718592]{0:T(1024)(128)(4,1)} %bitcast.9), calls=%async_computation.2 | async-start | bytes 1048576
  388.1 2.7 copy-start.8
  388.7 6.2 %slice-start.3 = ((s8[4718592]{0:T(1024)(128)(4,1)}), s8[4194304]{0:T(1024)(128)(4,1)S(1)}, s32[]{:S(2)}) async-start(s8[4718592]{0:T(1024)(128)(4,1)} %bitcast.9), calls=%async_computation.3 | async-start | bytes 8388608
  390.8 9.2 %slice-start = ((s8[4718592]{0:T(1024)(128)(4,1)}), s8[4194304]{0:T(1024)(128)(4,1)S(1)}, s32[]{:S(2)}) async-start(s8[4718592]{0:T(1024)(128)(4,1)} %bitcast.7), calls=%async_computation | async-start | bytes 8388608
  394.9 5.0 %slice-start.1 = ((s8[4718592]{0:T(1024)(128)(4,1)}), s8[524288]{0:T(1024)(128)(4,1)S(1)}, s32[]{:S(2)}) async-start(s8[4718592]{0:T(1024)(128)(4,1)} %bitcast.7), calls=%async_computation.1 | async-start | bytes 1048576

commit v7 on v6

--- a/solution.py
+++ b/solution.py
@@ -199,7 +199,6 @@
 MESH = pl.DeviceIdType.MESH
 TURNS = ((0, 1, 2), (0, 2, 1))
 STEPS = 5
-ADD_ROWS = 48
 FORWARD = 8
 
 
@@ -234,11 +233,12 @@
 
 def add_block(total, term, row=0, column=0):
     rows, columns = term.shape
-
-    @pl.loop(0, rows // ADD_ROWS)
+    block = next(size for size in (48, 32, 16) if rows % size == 0)
+
+    @pl.loop(0, rows // block)
     def _(index):
-        here = part_of(row + index * ADD_ROWS, ADD_ROWS, column, columns)
-        there = part_of(index * ADD_ROWS, ADD_ROWS, 0, columns)
+        here = part_of(row + index * block, block, column, columns)
+        there = part_of(index * block, block, 0, columns)
         total[here] = (total[here].astype(WIDE) + term[there].astype(WIDE)).astype(total.dtype)
 
 
@@ -251,9 +251,11 @@
 
 
 class Sum:
-    def __init__(self, turn, axes, corner, shape, term, result, total, arrived, sems, local_sems):
+    def __init__(
+        self, turn, axes, corner, shape, term, result, total, arrived, sems, local_sems, begin=0, stop=STEPS
+    ):
         self.term, self.result, self.total, self.arrived = term, result, total, arrived
-        self.sems, self.local_sems = sems, local_sems
+        self.sems, self.local_sems, self.begin, self.stop = sems, local_sems, begin, stop
         self.steps = place_bits(turn)
         self.shapes = halves(shape, axes)
         self.kept, self.left = [], []
@@ -263,35 +265,38 @@
             self.left.append((row + (1 - mine) * down, rows, column + (1 - mine) * across, columns))
             row, column = row + mine * down, column + mine * across
             self.kept.append((row, rows, column, columns))
+        self.held = self.kept[max(begin - 1, 0)]
 
     def inside(self, place):
         row, rows, column, columns = place
-        return part_of(row - self.kept[0][0], rows, column - self.kept[0][2], columns)
+        return part_of(row - self.held[0], rows, column - self.held[2], columns)
 
     def load(self):
+        source = self.term if self.begin else self.term.at[part_of(*self.kept[0])]
+        return pltpu.make_async_copy(source, self.total, self.local_sems.at[0])
+
+    def store(self):
+        place = self.kept[self.stop - 1]
+        target = self.result.at[part_of(*place)] if self.stop == STEPS else self.result
         return pltpu.make_async_copy(
-            self.term.at[part_of(*self.kept[0])], self.total, self.local_sems.at[0]
-        )
-
-    def store(self):
-        return pltpu.make_async_copy(
-            self.total.at[self.inside(self.kept[-1])],
-            self.result.at[part_of(*self.kept[-1])],
-            self.local_sems.at[1],
+            self.total.at[self.inside(place)], target, self.local_sems.at[1]
         )
 
     def gather(self, step):
         place = self.left[step]
         source = self.term.at[part_of(*place)] if step == 0 else self.total.at[self.inside(place)]
-        return remote(source, self.arrived[step], self.sems, step, self.steps[step][1])
+        return remote(source, self.arrived[step - self.begin], self.sems, step, self.steps[step][1])
 
     def spread(self, step):
         here = self.result.at[part_of(*self.kept[step])]
-        return remote(here, here, self.sems, STEPS + step, self.steps[step][1])
+        source = self.total.at[self.inside(self.kept[step])] if step == STEPS - 1 else here
+        return remote(source, here, self.sems, STEPS + step, self.steps[step][1])
 
     def start(self):
         self.load().start()
-        self.gather(0).start()
+        if self.begin:
+            self.load().wait()
+        self.gather(self.begin).start()
 
     def turn(self, tick):
         if tick < STEPS:
@@ -299,24 +304,25 @@
                 self.load().wait()
             self.gather(tick).wait()
             row, _, column, _ = self.kept[tick]
-            add_block(self.total, self.arrived[tick], row - self.kept[0][0], column - self.kept[0][2])
-            if tick + 1 < STEPS:
+            add_block(
+                self.total, self.arrived[tick - self.begin], row - self.held[0], column - self.held[2]
+            )
+            if tick + 1 < self.stop:
                 self.gather(tick + 1).start()
             else:
                 self.store().start()
-                self.store().wait()
-                self.spread(STEPS - 1).start()
+                if self.stop == STEPS:
+                    self.spread(STEPS - 1).start()
         else:
             step = 2 * STEPS - 1 - tick
+            if step == STEPS - 1:
+                self.store().wait()
             self.spread(step).wait()
             if step:
                 self.spread(step - 1).start()
 
 
-def greet():
-    group, place = lax.axis_index("dp"), lax.axis_index("blk")
-    devices = [device for _, device in place_bits(0)]
-    devices.append((group, 3 - place))
+def greet(devices):
     barrier = pltpu.get_barrier_semaphore()
     for device in devices:
         pl.semaphore_signal(barrier, inc=1, device_id=device, device_id_type=MESH)
@@ -362,10 +368,7 @@
     )
     load = pltpu.make_async_copy(a_in, a_all.at[0], a_sems.at[4])
     load.start()
-    barrier = pltpu.get_barrier_semaphore()
-    for device in (near, across):
-        pl.semaphore_signal(barrier, inc=1, device_id=device, device_id_type=MESH)
-    pl.semaphore_wait(barrier, 2)
+    greet((near, across))
     for chunk in range(pairs):
         channels[0](chunk).start()
 
@@ -552,9 +555,59 @@
 
 FF_BLOCK = 512
 ROW_BLOCK = 384
+AHEAD_STEPS = (3, 3, 2, 2)
+AHEAD_TICKS = ((1, 3, 4), (2, 4, 5), (3, 5), (4, 5))
+AHEAD = len(AHEAD_STEPS)
+LAST_BLOCK = 5
+DOWN_AXES, UP_AXES = "rrrrr", "rrrrc"
+
+
+def ahead_rows(shape, axes):
+    rows = [halves(shape, axes)[steps - 1][0] for steps in AHEAD_STEPS]
+    return [(sum(rows[:block]), rows[block]) for block in range(AHEAD)]
+
+
+def ahead_scratch(width):
+    scratch = [pltpu.VMEM((2, FF_BLOCK, width), LOW), pltpu.VMEM((2, width, FF_BLOCK), LOW)]
+    for shape, axes in (((FF_BLOCK, width), DOWN_AXES), ((width, FF_BLOCK), UP_AXES)):
+        for steps in AHEAD_STEPS:
+            shapes = halves(shape, axes)[:steps]
+            scratch += [pltpu.VMEM(each, LOW) for each in (shapes[0], *shapes)]
+    scratch += [pltpu.SemaphoreType.DMA((2 * AHEAD, 2 * STEPS))] * 2
+    return scratch + [pltpu.SemaphoreType.DMA((2 * AHEAD, 2))]
+
+
+def ahead_sums(width, part_down, part_up, refs):
+    terms, refs = refs[:2], refs[2:]
+    sends, receives, locals_ = refs[-3:]
+    sums = []
+    for side, (axes, shape, parts) in enumerate(
+        ((DOWN_AXES, (FF_BLOCK, width), part_down), (UP_AXES, (width, FF_BLOCK), part_up))
+    ):
+        places = ahead_rows(shape, axes)
+        for block, steps in enumerate(AHEAD_STEPS):
+            index = side * AHEAD + block
+            own, refs = refs[: steps + 1], refs[steps + 1 :]
+            sums.append(
+                Sum(
+                    (block + side) % 2,
+                    axes,
+                    (0, 0),
+                    shape,
+                    terms[side].at[block % 2],
+                    parts.at[pl.ds(*places[block])],
+                    own[0],
+                    own[1:],
+                    (sends.at[index], receives.at[index]),
+                    locals_.at[index],
+                    stop=steps,
+                )
+            )
+    return terms, [(sums[block], sums[AHEAD + block]) for block in range(AHEAD)]
 
 
 def mlp_kernel(
+    ahead,
     hidden_ref,
     attn_ref,
     attended_ref,
@@ -573,16 +626,25 @@
     grad_out_ref,
     grad_gain_ref,
     grad_bias_ref,
-    normed_ref,
-    inverse_ref,
-    b_ref,
-    dy_ref,
-    db_ref,
-    z_ref,
-    d_pre_ref,
+    *refs,
 ):
     block = pl.program_id(0)
-    rows = hidden_ref.shape[0]
+    rows, width = hidden_ref.shape
+    if ahead:
+        parts, refs = refs[:2], refs[2:]
+    normed_ref, inverse_ref, b_ref, dy_ref, db_ref, z_ref, d_pre_ref = refs[:7]
+    if ahead:
+        terms, sums = ahead_sums(width, *parts, refs[7:])
+
+        @pl.when(block == 0)
+        def _():
+            greet([device for _, device in place_bits(0)[: max(AHEAD_STEPS)]])
+
+    def trade(chosen, tick, when):
+        @pl.when(block == when)
+        def _():
+            for each in sums[chosen]:
+                each.turn(tick)
 
     @pl.when(block == 0)
     def _():
@@ -609,8 +671,24 @@
         outputs_ref[here] += dot(z_ref[here], w_down_ref[...], NN)
         db_ref[here] += dot(d_pre, w_up_ref[...], NT)
     grad_bias_ref[...] = bias
-    grad_down_ref[...] = dot(z_ref[...], dy_ref[...], TN).astype(LOW)
-    grad_up_ref[...] = dot(b_ref[...], d_pre_ref[...], TN).astype(LOW)
+    grad_down = dot(z_ref[...], dy_ref[...], TN).astype(LOW)
+    grad_up = dot(b_ref[...], d_pre_ref[...], TN).astype(LOW)
+    grad_down_ref[...] = grad_down
+    grad_up_ref[...] = grad_up
+    if ahead:
+        for chosen, ticks in enumerate(AHEAD_TICKS):
+            for tick, when in enumerate(ticks):
+                if when < LAST_BLOCK:
+                    trade(chosen, tick, when)
+        for chosen in range(AHEAD):
+
+            @pl.when(block == chosen)
+            def _():
+                terms[0][chosen % 2] = grad_down
+                terms[1][chosen % 2] = grad_up
+                for each in sums[chosen]:
+                    each.start()
+
 
     @pl.when(block == pl.num_programs(0) - 1)
     def _():
@@ -628,8 +706,20 @@
                 lanes = slice(pair * PAIR + head * HEAD, pair * PAIR + (head + 1) * HEAD)
                 dots_ref[pair, head : head + 1] = jnp.sum(product[lanes], axis=0, keepdims=True)
 
-
-def mlp_call(hidden, attn_low, attended, cotangent, w_out, gain_mlp, w_up, b_up, w_down):
+    if ahead:
+        for chosen, ticks in enumerate(AHEAD_TICKS):
+            for tick, when in enumerate(ticks):
+                if when == LAST_BLOCK:
+                    trade(chosen, tick, when)
+
+        @pl.when(block == pl.num_programs(0) - 1)
+        def _():
+            for pair in sums:
+                for each in pair:
+                    each.store().wait()
+
+
+def mlp_call(ahead, hidden, attn_low, attended, cotangent, w_out, gain_mlp, w_up, b_up, w_down):
     rows, width = hidden.shape
     hidden_units = w_up.shape[1]
     pairs = width // PAIR
@@ -641,8 +731,16 @@
     down = pl.BlockSpec((FF_BLOCK, width), lambda block: (block, 0))
     bias = pl.BlockSpec((1, FF_BLOCK), lambda block: (0, block))
     wide = jax.ShapeDtypeStruct((rows, width), WIDE)
+    anywhere = pl.BlockSpec(memory_space=pl.ANY)
+    down_rows = sum(ahead_rows((FF_BLOCK, width), DOWN_AXES)[-1])
+    up_rows = sum(ahead_rows((width, FF_BLOCK), UP_AXES)[-1])
+    part_shapes = [
+        jax.ShapeDtypeStruct((down_rows, width), LOW),
+        jax.ShapeDtypeStruct((up_rows, FF_BLOCK), LOW),
+    ]
+    params = dict(collective_id=3, has_side_effects=True) if ahead else {}
     return pl.pallas_call(
-        mlp_kernel,
+        functools.partial(mlp_kernel, ahead),
         grid=(hidden_units // FF_BLOCK,),
         in_specs=[square] * 4 + [once(width, width), line, up, bias, down],
         out_specs=[
@@ -655,7 +753,8 @@
             whole(width, width),
             whole(1, width),
             bias,
-        ],
+        ]
+        + [anywhere] * (2 if ahead else 0),
         out_shape=[
             wide,
             wide,
@@ -666,7 +765,8 @@
             jax.ShapeDtypeStruct((width, width), LOW),
             jax.ShapeDtypeStruct((1, width), WIDE),
             jax.ShapeDtypeStruct((1, hidden_units), WIDE),
-        ],
+        ]
+        + (part_shapes if ahead else []),
         scratch_shapes=[
             pltpu.VMEM((rows, width), WIDE),
             pltpu.VMEM((rows, 1), WIDE),
@@ -675,35 +775,38 @@
             pltpu.VMEM((rows, width), WIDE),
             pltpu.VMEM((rows, FF_BLOCK), LOW),
             pltpu.VMEM((rows, FF_BLOCK), LOW),
-        ],
+        ]
+        + (ahead_scratch(width) if ahead else []),
         name="mlp",
-        compiler_params=pltpu.CompilerParams(vmem_limit_bytes=56 * 2**20),
+        compiler_params=pltpu.CompilerParams(vmem_limit_bytes=60 * 2**20, **params),
     )(hidden, attn_low, attended, cotangent, w_out, gain_mlp[None], w_up, b_up[None], w_down)
 
 
 PARTS = (
-    ("down", (0, 0), (1536, 384), "rrrrr", 0, (1, 3, 7, 9, 10, 12, 14, 15, 17, 18)),
-    ("down", (0, 384), (1536, 384), "rrrrr", 1, (1, 3, 7, 8, 9, 11, 12, 14, 17, 18)),
-    ("down", (1536, 0), (1536, 384), "rrrrr", 1, (2, 5, 10, 11, 13, 15, 17, 18, 21, 22)),
-    ("down", (1536, 384), (1536, 384), "rrrrr", 0, (2, 5, 8, 9, 11, 12, 15, 18, 20, 21)),
-    ("up", (0, 0), (768, 768), "rrrrc", 0, (2, 6, 9, 10, 12, 14, 16, 18, 23, 24)),
-    ("up", (0, 768), (768, 768), "rrrrc", 1, (3, 6, 10, 12, 14, 17, 18, 21, 23, 24)),
-    ("up", (0, 1536), (768, 768), "rrrrc", 0, (3, 7, 10, 12, 13, 16, 18, 20, 24, 24)),
-    ("up", (0, 2304), (768, 768), "rrrrc", 1, (3, 7, 11, 13, 16, 18, 19, 23, 24, 24)),
-    ("out", (0, 0), (768, 768), "rrrrc", 0, (3, 9, 10, 12, 15, 17, 18, 22, 24, 24)),
-    ("qkv", (0, 0), (768, 512), "rrrrc", 0, None),
-    ("qkv", (0, 512), (768, 512), "rrrrc", 1, None),
-    ("qkv", (0, 1024), (768, 512), "rrrrc", 0, None),
-    ("qkv", (0, 1536), (768, 768), "rrrrc", 1, None),
+    ("down", (0, 0), (512, 768), DOWN_AXES, 0, AHEAD_STEPS[0], 0, (24, 24, 24, 1, 2, 4, 5, 6, 8, 9)),
+    ("down", (512, 0), (512, 768), DOWN_AXES, 1, AHEAD_STEPS[1], 1, (24, 24, 24, 1, 2, 4, 5, 6, 8, 9)),
+    ("down", (1024, 0), (512, 768), DOWN_AXES, 0, AHEAD_STEPS[2], 2, (24, 24, 1, 2, 4, 6, 7, 9, 12, 13)),
+    ("down", (1536, 0), (512, 768), DOWN_AXES, 1, AHEAD_STEPS[3], 3, (24, 24, 1, 2, 4, 6, 8, 10, 12, 13)),
+    ("up", (0, 0), (768, 512), UP_AXES, 1, AHEAD_STEPS[0], 0, (24, 24, 24, 1, 2, 5, 6, 7, 10, 11)),
+    ("up", (0, 512), (768, 512), UP_AXES, 0, AHEAD_STEPS[1], 1, (24, 24, 24, 2, 3, 5, 6, 8, 10, 11)),
+    ("up", (0, 1024), (768, 512), UP_AXES, 1, AHEAD_STEPS[2], 2, (24, 24, 2, 3, 5, 6, 8, 11, 12, 14)),
+    ("up", (0, 1536), (768, 512), UP_AXES, 0, AHEAD_STEPS[3], 3, (24, 24, 2, 4, 5, 6, 9, 11, 12, 13)),
+    ("down", (2048, 0), (1024, 768), "rrrrr", 0, 0, None, (1, 4, 6, 8, 12, 16, 19, 21, 24, 24)),
+    ("up", (0, 2048), (768, 1024), "rrrcc", 1, 0, None, (1, 4, 6, 8, 12, 16, 20, 22, 24, 24)),
+    ("out", (0, 0), (768, 768), "rrrrc", 0, 0, None, (2, 5, 6, 9, 12, 16, 20, 22, 24, 24)),
+    ("qkv", (0, 0), (768, 512), "rrrrc", 0, 0, None, None),
+    ("qkv", (0, 512), (768, 512), "rrrrc", 1, 0, None, None),
+    ("qkv", (0, 1024), (768, 512), "rrrrc", 0, 0, None, None),
+    ("qkv", (0, 1536), (768, 768), "rrrrc", 1, 0, None, None),
 )
 
 
 def gradient_kernel(*refs):
     keys, values, shards = refs[:3]
     q_ref, grad_ref, lse_ref, dots_ref, clips, query_clip, w_ref = refs[3:10]
-    down_in, up_in, out_in, small_in = refs[10:14]
-    down_out, up_out, out_out, qkv_out, small_out, input_out = refs[14:20]
-    refs = refs[20:]
+    down_in, up_in, out_in, part_down, part_up, small_in = refs[10:16]
+    down_out, up_out, out_out, qkv_out, small_out, input_out = refs[16:22]
+    refs = refs[22:]
     kv_slot, a_slot, dq_sum, dk_sum, dv_sum, dk_all, dv_all, grad_k, grad_v, parts = refs[:10]
     from_near, from_across, qkv_term, clip_slot, small_arrived = refs[10:15]
     input_sum = dq_sum
@@ -725,28 +828,30 @@
         "qkv": (qkv_term, qkv_out),
     }
     sums = []
-    for index, (name, corner, shape, axes, turn, _) in enumerate(PARTS):
-        total, arrived = refs[0], refs[1:STEPS]
-        refs = refs[STEPS:]
-        if name == "down":
-            arrived = (qkv_term.at[:, pl.ds(index * shape[1], shape[1])], *arrived)
-        else:
-            arrived, refs = (refs[0], *arrived), refs[1:]
+    for index, (name, corner, shape, axes, turn, begin, block, _) in enumerate(PARTS):
+        steps = STEPS - begin
+        total, arrived, refs = refs[0], refs[1 : steps + 1], refs[steps + 1 :]
+        term, result = arrays[name]
+        if block is not None:
+            term = {"down": part_down, "up": part_up}[name]
+            term = term.at[pl.ds(*ahead_rows(shape, axes)[block])]
         sums.append(
             Sum(
                 turn,
                 axes,
                 corner,
                 shape,
-                *arrays[name],
+                term,
+                result,
                 total,
                 arrived,
                 (sends.at[index], receives.at[index]),
                 locals_.at[index],
+                begin=begin,
             )
         )
-    early = [(each, part[5]) for each, part in zip(sums, PARTS) if part[5] is not None]
-    late = [each for each, part in zip(sums, PARTS) if part[5] is None]
+    early = [(each, part[-1]) for each, part in zip(sums, PARTS) if part[-1] is not None]
+    late = [each for each, part in zip(sums, PARTS) if part[-1] is None]
 
     chunk_rows = rows // pairs
 
@@ -799,7 +904,7 @@
 
     for copy in kv_copies(3, 0, 0):
         copy.start()
-    greet()
+    greet([device for _, device in place_bits(0)] + [across])
     for each, _ in early:
         each.start()
     dq_sum[...] = jnp.zeros_like(dq_sum)
@@ -844,7 +949,7 @@
                 functools.partial(each.turn, tick)
                 for tick in range(2 * STEPS)
                 for each, ticks in early
-                if ticks[tick] == when
+                if ticks[tick] == when and tick >= each.begin
             ]
             if ends:
                 at(when, *ends)
@@ -919,7 +1024,10 @@
 
     for each in late:
         each.start()
-    open_sums = [(each, [tick for tick in range(2 * STEPS) if ticks[tick] == pieces]) for each, ticks in early]
+    open_sums = [
+        (each, [tick for tick in range(each.begin, 2 * STEPS) if ticks[tick] == pieces])
+        for each, ticks in early
+    ]
     open_sums += [(each, list(range(2 * STEPS))) for each in late]
 
     @pl.when(at_end)
@@ -958,7 +1066,7 @@
 
 
 def gradient_call(
-    keys, values, shards, query, grad_t, lse, row_dots, clips, query_clip, w_qkv, grad_down, grad_up, grad_out, small
+    keys, values, shards, query, grad_t, lse, row_dots, clips, query_clip, w_qkv, grad_down, grad_up, grad_out, part_down, part_up, small
 ):
     rows, width = query.shape
     pairs = width // PAIR
@@ -994,15 +1102,13 @@
         pltpu.SemaphoreType.DMA,
         pltpu.SemaphoreType.DMA,
     ]
-    for name, _, shape, axes, _, _ in PARTS:
+    for _, _, shape, axes, _, begin, _, _ in PARTS:
         shapes = halves(shape, axes)
-        scratch += [pltpu.VMEM(each, LOW) for each in (shapes[0], *shapes[1:])]
-        if name != "down":
-            scratch.append(pltpu.VMEM(shapes[0], LOW))
+        scratch += [pltpu.VMEM(each, LOW) for each in (shapes[max(begin - 1, 0)], *shapes[begin:])]
     like = lambda array: jax.ShapeDtypeStruct(array.shape, array.dtype)
     return pl.pallas_call(
         gradient_kernel,
-        in_specs=[anywhere] * 3 + [inside] * 4 + [anywhere] + [inside] * 2 + [anywhere] * 3 + [inside],
+        in_specs=[anywhere] * 3 + [inside] * 4 + [anywhere] + [inside] * 2 + [anywhere] * 5 + [inside],
         out_specs=[anywhere] * 4 + [inside, anywhere],
         out_shape=[
             like(grad_down),
@@ -1019,7 +1125,7 @@
         ),
     )(
         keys, values, shards, query, grad_t, lse, row_dots, clips, query_clip, w_qkv,
-        grad_down, grad_up, grad_out, small,
+        grad_down, grad_up, grad_out, part_down, part_up, small,
     )
 
 
@@ -1048,6 +1154,7 @@
         a_low, w_qkv, clips, query_clip
     )
 
+    quick = groups == 8 and rows == width
     (
         outputs,
         d_resid,
@@ -1058,10 +1165,11 @@
         grad_out,
         grad_gain_mlp,
         grad_bias_up,
-    ) = mlp_call(hidden, attn_low, attended, cotangent, w_out, gain_mlp, w_up, b_up, w_down)
+        *parts,
+    ) = mlp_call(quick, hidden, attn_low, attended, cotangent, w_out, gain_mlp, w_up, b_up, w_down)
     grad_gain_mlp, grad_bias_up = grad_gain_mlp[0], grad_bias_up[0]
 
-    if groups == 8 and rows == width:
+    if quick:
         small = jnp.concatenate([jnp.zeros_like(gain_attn), grad_gain_mlp, grad_bias_up])
         sum_down, sum_up, sum_out, sum_qkv, sum_small, d_normed_attn = gradient_call(
             keys,
@@ -1077,6 +1185,7 @@
             grad_down,
             grad_up,
             grad_out,
+            *parts,
             jnp.pad(small.reshape(6, width), ((0, 2), (0, 0))),
         )
         input_grad = d_resid + norm_back(d_normed_attn * gain_attn, normed_attn, inverse_attn)

time: 405 us -> 405 us (level); the launches traced: 404 us -> 397 us
  Pallas kernels: 361 us -> 352 us
    pallas_call x1, Pallas kernels: 221 us -> 203 us  [gradient_call(): pl.pallas_call(gradient_kernel, in_specs=[anywhere] * 3 + [inside] * 4 +...]
    pallas_call x1, Pallas kernels: 36.4 us -> 46 us  [mlp_call(): pl.pallas_call(functools.partial(mlp_kernel, ahead), grid=(hidden_units /...]
where the time goes in v7:
time: 405 us; the launch traced here: 397 us
  Pallas kernels  352 us (87%)
  other arithmetic  29.8 us (7%)
  local copies, waits for them, and re-layouts  11.9 us (3%)
    pallas_call x1, Pallas kernels, gradient_call(): pl.pallas_call(gradient_kernel, in_specs=[anywhere] * 3 + [inside] * 4 +...  203 us
    pallas_call x1, Pallas kernels, attention_call(): pl.pallas_call(attention_kernel, in_specs=[anywhere, inside, anywhere, in...  103 us
    pallas_call x1, Pallas kernels, mlp_call(): pl.pallas_call(functools.partial(mlp_kernel, ahead), grid=(hidden_units /...  46 us

profile of v7, /device:TPU:0, one launch (start us, length us, event | category | flops | bytes accessed | tf_op | source)
XLA Modules:
  0.0 397.4 jit_solution(14577647783302134437)
XLA Ops:
  0.6 0.7 constant_dynamic-slice_fusion
  4.6 1.3 broadcast_in_dim.12.gain_ref
  5.8 0.7 convert_element_type.20
  6.5 0.9 fusion.1
  8.0 4.2 %multiply_sine_fusion = (f32[768,384]{1,0:T(8,128)S(1)}, f32[768,384]{1,0:T(8,128)S(1)}) fusion(f32[384]{0:T(512)S(1)} %multiply_exponential_fusion, f32[768]{0:T(1024)S(1)} %convert_element_type.20), kind=kLoop, calls=%fused_computation.8 | loop fusion | flops 294912 | bytes 2363904 | tf_op jit(solution)/shard_map/sin | solution.py:35
  13.0 1.0 copy-done.5
  14.3 103.3 %attention.1 = (bf16[4,768,768]{2,1,0:T(8,128)(2,1)}, bf16[4,768,768]{2,1,0:T(8,128)(2,1)}, bf16[4,768,768]{2,1,0:T(8,128)(2,1)}, bf16[768,768]{1,0:T(8,128)(2,1...) custom-call(bf16[768,768]{1,0:T(8,128)(2,1)S(1)} %multiply_convert_fusion.refs_0_, ...), custom_call_target="tpu_custom_call" | custom-call | tf_op jit(solution)/shard_map/attention/pallas_call | solution.py:532
  117.6 1.0 copy-done.1
  118.6 1.0 copy-done.2
  119.6 0.6 copy-done.3
  120.2 46.0 %mlp.1 = (f32[768,768]{1,0:T(8,128)}, f32[768,768]{1,0:T(8,128)}, bf16[768,768]{1,0:T(8,128)(2,1)}, f32[6,2,768]{2,1,0:T(2,128)}, bf16[3072,768]{1,0:T(8,128)(2,...) custom-call(f32[768,768]{1,0:T(8,128)} %copy-done.5, ...), custom_call_target="tpu_custom_call" | custom-call | tf_op jit(solution)/shard_map/mlp/pallas_call | solution.py:742
  166.2 0.7 reduce
  167.0 0.7 pad_maximum_fusion
  167.7 0.6 pad.4.refs_15_
  168.3 202.6 %gradients.1 = (bf16[3072,768]{1,0:T(8,128)(2,1)}, bf16[768,3072]{1,0:T(8,128)(2,1)}, bf16[768,768]{1,0:T(8,128)(2,1)}, bf16[768,2304]{1,0:T(8,128)(2,1)}, f32[8,768]{1,0:T(8,128)}, /*index=5*/f32[768,768]{1,0:T(8,128)}) custom-call(bf16[4,768,768]{2,1,0:T(8,128)(2,1)} %get-tuple-element.37.refs_0_, bf16[4,768,768]{2,1,0:T(8,128)(2,1)} %get-tuple-element.38.refs_1_, ...), custom_call_target="tpu_custom_call" | custom-call | tf_op jit(solution)/shard_map/gradients/pallas_call | solution.py:1109
  370.9 3.3 multiply_reduce_fusion.2
  374.7 3.3 multiply_add_fusion
  378.0 0.6 slice_reduce_fusion
  378.6 0.6 reshape.68
  379.9 1.6 convert_element_type.23
  381.9 4.1 %convert_element_type.22 = f32[768,2304]{1,0:T(8,128)} convert(bf16[768,2304]{1,0:T(8,128)(2,1)S(1)} %copy-done.8) | non-fusion elementwise | flops 1769472 | bytes 10616832 | tf_op jit(solution)/shard_map/convert_element_type | solution.py:1196
  386.1 5.0 %convert_element_type.24 = f32[768,3072]{1,0:T(8,128)} convert(bf16[768,3072]{1,0:T(8,128)(2,1)S(1)} %bitcast.10) | non-fusion elementwise | flops 2359296 | bytes 14155776 | tf_op jit(solution)/shard_map/convert_element_type | solution.py:1199
  391.1 4.5 %convert_element_type.25 = f32[3072,768]{1,0:T(8,128)} convert(bf16[3072,768]{1,0:T(8,128)(2,1)S(1)} %bitcast.8) | non-fusion elementwise | flops 2359296 | bytes 14155776 | tf_op jit(solution)/shard_map/convert_element_type | solution.py:1201
  395.6 1.4 copy.24
  (49 shorter events, 3.9 us)
Async XLA Ops:
  7.5 6.8 %copy-start.4 = (s32[1,768]{1,0:T(1,128)}, s32[1,768]{1,0:T(1,128)S(1)}, u32[]{:S(2)}) copy-start(s32[1,768]{1,0:T(1,128)S(1)} %broadcast_in_dim.11.refs_3_.refs_8_) | copy-start | bytes 9220
  8.0 6.3 %copy-start = (s32[3072,1]{1,0:T(8,128)}, s32[3072,1]{1,0:T(8,128)S(1)}, u32[]{:S(2)}) copy-start(s32[3072,1]{1,0:T(8,128)S(1)} %copy.21.refs_2_.refs_7_) | copy-start | bytes 36868
  8.0 4.2 %copy-start.9 = (f32[768,768]{1,0:T(8,128)S(1)}, f32[768,768]{1,0:T(8,128)}, u32[]{:S(2)}) copy-start(f32[768,768]{1,0:T(8,128)} %param.12) | copy-start | bytes 7077892
  12.5 1.4 copy-start.5
  12.5 1.4 copy-start.12
  117.6 1.0 copy-start.1
  118.6 1.0 copy-start.2
  119.6 0.6 copy-start.3
  370.9 3.3 copy-start.6
  370.9 3.8 copy-start.7
  374.7 3.3 copy-start.13
  374.7 5.2 %copy-start.11 = (bf16[768,768]{1,0:T(8,128)(2,1)S(1)}, bf16[768,768]{1,0:T(8,128)(2,1)}, u32[]{:S(2)}) copy-start(bf16[768,768]{1,0:T(8,128)(2,1)} %get-tuple-element.54) | copy-start | bytes 3538948
  374.7 11.4 %slice-start.2 = ((s8[4718592]{0:T(1024)(128)(4,1)}), s8[524288]{0:T(1024)(128)(4,1)S(1)}, s32[]{:S(2)}) async-start(s8[4718592]{0:T(1024)(128)(4,1)} %bitcast.9), calls=%async_computation.2 | async-start | bytes 1048576
  379.2 2.7 copy-start.8
  379.9 6.2 %slice-start.3 = ((s8[4718592]{0:T(1024)(128)(4,1)}), s8[4194304]{0:T(1024)(128)(4,1)S(1)}, s32[]{:S(2)}) async-start(s8[4718592]{0:T(1024)(128)(4,1)} %bitcast.9), calls=%async_computation.3 | async-start | bytes 8388608
  381.9 9.2 %slice-start = ((s8[4718592]{0:T(1024)(128)(4,1)}), s8[4194304]{0:T(1024)(128)(4,1)S(1)}, s32[]{:S(2)}) async-start(s8[4718592]{0:T(1024)(128)(4,1)} %bitcast.7), calls=%async_computation | async-start | bytes 8388608
  386.1 5.0 %slice-start.1 = ((s8[4718592]{0:T(1024)(128)(4,1)}), s8[524288]{0:T(1024)(128)(4,1)S(1)}, s32[]{:S(2)}) async-start(s8[4718592]{0:T(1024)(128)(4,1)} %bitcast.7), calls=%async_computation.1 | async-start | bytes 1048576
  391.1 4.5 %copy-start.10 = (f32[768,768]{1,0:T(8,128)S(1)}, f32[768,768]{1,0:T(8,128)}, u32[]{:S(2)}) copy-start(f32[768,768]{1,0:T(8,128)} %get-tuple-element.85) | copy-start | bytes 7077892

commit v8 on v7

--- a/solution.py
+++ b/solution.py
@@ -794,10 +794,15 @@
     ("down", (2048, 0), (1024, 768), "rrrrr", 0, 0, None, (1, 4, 6, 8, 12, 16, 19, 21, 24, 24)),
     ("up", (0, 2048), (768, 1024), "rrrcc", 1, 0, None, (1, 4, 6, 8, 12, 16, 20, 22, 24, 24)),
     ("out", (0, 0), (768, 768), "rrrrc", 0, 0, None, (2, 5, 6, 9, 12, 16, 20, 22, 24, 24)),
-    ("qkv", (0, 0), (768, 512), "rrrrc", 0, 0, None, None),
-    ("qkv", (0, 512), (768, 512), "rrrrc", 1, 0, None, None),
-    ("qkv", (0, 1024), (768, 512), "rrrrc", 0, 0, None, None),
-    ("qkv", (0, 1536), (768, 768), "rrrrc", 1, 0, None, None),
+    ("qkv", (0, 0), (768, 256), "rrrrc", 0, 0, None, None),
+    ("qkv", (0, 256), (768, 256), "rrrrc", 1, 0, None, None),
+    ("qkv", (0, 512), (768, 256), "rrrrc", 0, 0, None, None),
+    ("qkv", (0, 768), (768, 256), "rrrrc", 1, 0, None, None),
+    ("qkv", (0, 1024), (768, 256), "rrrrc", 0, 0, None, None),
+    ("qkv", (0, 1280), (768, 256), "rrrrc", 1, 0, None, None),
+    ("qkv", (0, 1536), (768, 256), "rrrrc", 0, 0, None, None),
+    ("qkv", (0, 1792), (768, 256), "rrrrc", 1, 0, None, None),
+    ("qkv", (0, 2048), (768, 256), "rrrrc", 0, 0, None, None),
 )
 
 

time: 405 us -> 403 us (level)
  no operation moved by 1% of the time
where the time goes in v8:
time: 403 us; the launch traced here: 395 us
  Pallas kernels  350 us (87%)
  other arithmetic  29.8 us (7%)
  local copies, waits for them, and re-layouts  11.9 us (3%)
    pallas_call x1, Pallas kernels, gradient_call(): pl.pallas_call(gradient_kernel, in_specs=[anywhere] * 3 + [inside] * 4 +...  200 us
    pallas_call x1, Pallas kernels, attention_call(): pl.pallas_call(attention_kernel, in_specs=[anywhere, inside, anywhere, in...  103 us
    pallas_call x1, Pallas kernels, mlp_call(): pl.pallas_call(functools.partial(mlp_kernel, ahead), grid=(hidden_units /...  46 us

profile of v8, /device:TPU:0, one launch (start us, length us, event | category | flops | bytes accessed | tf_op | source)
XLA Modules:
  0.0 395.1 jit_solution(16396418805247405505)
XLA Ops:
  0.6 0.7 constant_dynamic-slice_fusion
  4.6 1.3 broadcast_in_dim.12.gain_ref
  5.8 0.7 convert_element_type.20
  6.5 0.9 fusion.1
  8.0 4.2 %multiply_sine_fusion = (f32[768,384]{1,0:T(8,128)S(1)}, f32[768,384]{1,0:T(8,128)S(1)}) fusion(f32[384]{0:T(512)S(1)} %multiply_exponential_fusion, f32[768]{0:T(1024)S(1)} %convert_element_type.20), kind=kLoop, calls=%fused_computation.8 | loop fusion | flops 294912 | bytes 2363904 | tf_op jit(solution)/shard_map/sin | solution.py:35
  13.0 1.0 copy-done.5
  14.3 103.3 %attention.1 = (bf16[4,768,768]{2,1,0:T(8,128)(2,1)}, bf16[4,768,768]{2,1,0:T(8,128)(2,1)}, bf16[4,768,768]{2,1,0:T(8,128)(2,1)}, bf16[768,768]{1,0:T(8,128)(2,1...) custom-call(bf16[768,768]{1,0:T(8,128)(2,1)S(1)} %multiply_convert_fusion.refs_0_, ...), custom_call_target="tpu_custom_call" | custom-call | tf_op jit(solution)/shard_map/attention/pallas_call | solution.py:532
  117.6 1.0 copy-done.1
  118.6 1.0 copy-done.2
  119.6 0.6 copy-done.3
  120.2 46.0 %mlp.1 = (f32[768,768]{1,0:T(8,128)}, f32[768,768]{1,0:T(8,128)}, bf16[768,768]{1,0:T(8,128)(2,1)}, f32[6,2,768]{2,1,0:T(2,128)}, bf16[3072,768]{1,0:T(8,128)(2,...) custom-call(f32[768,768]{1,0:T(8,128)} %copy-done.5, ...), custom_call_target="tpu_custom_call" | custom-call | tf_op jit(solution)/shard_map/mlp/pallas_call | solution.py:742
  166.2 0.7 reduce
  167.0 0.7 pad_maximum_fusion
  167.7 0.6 pad.4.refs_15_
  168.3 200.3 %gradients.1 = (bf16[3072,768]{1,0:T(8,128)(2,1)}, bf16[768,3072]{1,0:T(8,128)(2,1)}, bf16[768,768]{1,0:T(8,128)(2,1)}, bf16[768,2304]{1,0:T(8,128)(2,1)}, f32[8,768]{1,0:T(8,128)}, /*index=5*/f32[768,768]{1,0:T(8,128)}) custom-call(bf16[4,768,768]{2,1,0:T(8,128)(2,1)} %get-tuple-element.37.refs_0_, bf16[4,768,768]{2,1,0:T(8,128)(2,1)} %get-tuple-element.38.refs_1_, ...), custom_call_target="tpu_custom_call" | custom-call | tf_op jit(solution)/shard_map/gradients/pallas_call | solution.py:1114
  368.6 3.3 multiply_reduce_fusion.2
  372.4 3.3 multiply_add_fusion
  375.7 0.6 slice_reduce_fusion
  376.3 0.6 reshape.68
  377.5 1.6 convert_element_type.23
  379.6 4.1 %convert_element_type.22 = f32[768,2304]{1,0:T(8,128)} convert(bf16[768,2304]{1,0:T(8,128)(2,1)S(1)} %copy-done.8) | non-fusion elementwise | flops 1769472 | bytes 10616832 | tf_op jit(solution)/shard_map/convert_element_type | solution.py:1201
  383.7 5.0 %convert_element_type.24 = f32[768,3072]{1,0:T(8,128)} convert(bf16[768,3072]{1,0:T(8,128)(2,1)S(1)} %bitcast.10) | non-fusion elementwise | flops 2359296 | bytes 14155776 | tf_op jit(solution)/shard_map/convert_element_type | solution.py:1204
  388.8 4.5 %convert_element_type.25 = f32[3072,768]{1,0:T(8,128)} convert(bf16[3072,768]{1,0:T(8,128)(2,1)S(1)} %bitcast.8) | non-fusion elementwise | flops 2359296 | bytes 14155776 | tf_op jit(solution)/shard_map/convert_element_type | solution.py:1206
  393.3 1.4 copy.24
  (49 shorter events, 3.9 us)
Async XLA Ops:
  7.5 6.8 %copy-start.4 = (s32[1,768]{1,0:T(1,128)}, s32[1,768]{1,0:T(1,128)S(1)}, u32[]{:S(2)}) copy-start(s32[1,768]{1,0:T(1,128)S(1)} %broadcast_in_dim.11.refs_3_.refs_8_) | copy-start | bytes 9220
  8.0 6.3 %copy-start = (s32[3072,1]{1,0:T(8,128)}, s32[3072,1]{1,0:T(8,128)S(1)}, u32[]{:S(2)}) copy-start(s32[3072,1]{1,0:T(8,128)S(1)} %copy.21.refs_2_.refs_7_) | copy-start | bytes 36868
  8.0 4.2 %copy-start.9 = (f32[768,768]{1,0:T(8,128)S(1)}, f32[768,768]{1,0:T(8,128)}, u32[]{:S(2)}) copy-start(f32[768,768]{1,0:T(8,128)} %param.12) | copy-start | bytes 7077892
  12.5 1.4 copy-start.5
  12.5 1.4 copy-start.12
  117.6 1.0 copy-start.1
  118.6 1.0 copy-start.2
  119.6 0.6 copy-start.3
  368.6 3.3 copy-start.6
  368.6 3.8 copy-start.7
  372.4 3.3 copy-start.13
  372.4 5.2 %copy-start.11 = (bf16[768,768]{1,0:T(8,128)(2,1)S(1)}, bf16[768,768]{1,0:T(8,128)(2,1)}, u32[]{:S(2)}) copy-start(bf16[768,768]{1,0:T(8,128)(2,1)} %get-tuple-element.54) | copy-start | bytes 3538948
  372.4 11.4 %slice-start.2 = ((s8[4718592]{0:T(1024)(128)(4,1)}), s8[524288]{0:T(1024)(128)(4,1)S(1)}, s32[]{:S(2)}) async-start(s8[4718592]{0:T(1024)(128)(4,1)} %bitcast.9), calls=%async_computation.2 | async-start | bytes 1048576
  376.9 2.7 copy-start.8
  377.5 6.2 %slice-start.3 = ((s8[4718592]{0:T(1024)(128)(4,1)}), s8[4194304]{0:T(1024)(128)(4,1)S(1)}, s32[]{:S(2)}) async-start(s8[4718592]{0:T(1024)(128)(4,1)} %bitcast.9), calls=%async_computation.3 | async-start | bytes 8388608
  379.6 9.2 %slice-start = ((s8[4718592]{0:T(1024)(128)(4,1)}), s8[4194304]{0:T(1024)(128)(4,1)S(1)}, s32[]{:S(2)}) async-start(s8[4718592]{0:T(1024)(128)(4,1)} %bitcast.7), calls=%async_computation | async-start | bytes 8388608
  383.7 5.0 %slice-start.1 = ((s8[4718592]{0:T(1024)(128)(4,1)}), s8[524288]{0:T(1024)(128)(4,1)S(1)}, s32[]{:S(2)}) async-start(s8[4718592]{0:T(1024)(128)(4,1)} %bitcast.7), calls=%async_computation.1 | async-start | bytes 1048576
  388.8 4.5 %copy-start.10 = (f32[768,768]{1,0:T(8,128)S(1)}, f32[768,768]{1,0:T(8,128)}, u32[]{:S(2)}) copy-start(f32[768,768]{1,0:T(8,128)} %get-tuple-element.85) | copy-start | bytes 7077892

commit v9 on v8

--- a/solution.py
+++ b/solution.py
@@ -790,10 +790,10 @@
     ("up", (0, 0), (768, 512), UP_AXES, 1, AHEAD_STEPS[0], 0, (24, 24, 24, 1, 2, 5, 6, 7, 10, 11)),
     ("up", (0, 512), (768, 512), UP_AXES, 0, AHEAD_STEPS[1], 1, (24, 24, 24, 2, 3, 5, 6, 8, 10, 11)),
     ("up", (0, 1024), (768, 512), UP_AXES, 1, AHEAD_STEPS[2], 2, (24, 24, 2, 3, 5, 6, 8, 11, 12, 14)),
-    ("up", (0, 1536), (768, 512), UP_AXES, 0, AHEAD_STEPS[3], 3, (24, 24, 2, 4, 5, 6, 9, 11, 12, 13)),
-    ("down", (2048, 0), (1024, 768), "rrrrr", 0, 0, None, (1, 4, 6, 8, 12, 16, 19, 21, 24, 24)),
-    ("up", (0, 2048), (768, 1024), "rrrcc", 1, 0, None, (1, 4, 6, 8, 12, 16, 20, 22, 24, 24)),
-    ("out", (0, 0), (768, 768), "rrrrc", 0, 0, None, (2, 5, 6, 9, 12, 16, 20, 22, 24, 24)),
+    ("up", (0, 1536), (768, 512), UP_AXES, 0, AHEAD_STEPS[3], 3, (24, 24, 2, 4, 5, 6, 9, 10, 12, 13)),
+    ("down", (2048, 0), (1024, 768), "rrrrr", 0, 0, None, (1, 4, 6, 8, 9, 11, 12, 14, 17, 18)),
+    ("up", (0, 2048), (768, 1024), "rrrcc", 1, 0, None, (1, 4, 6, 8, 10, 12, 13, 15, 18, 19)),
+    ("out", (0, 0), (768, 768), "rrrrc", 0, 0, None, (2, 5, 6, 9, 10, 12, 14, 16, 18, 20)),
     ("qkv", (0, 0), (768, 256), "rrrrc", 0, 0, None, None),
     ("qkv", (0, 256), (768, 256), "rrrrc", 1, 0, None, None),
     ("qkv", (0, 512), (768, 256), "rrrrc", 0, 0, None, None),

time: 403 us -> 404 us (level)
  no operation moved by 1% of the time
where the time goes in v9:
time: 404 us; the launch traced here: 396 us
  Pallas kernels  350 us (87%)
  other arithmetic  29.8 us (7%)
  local copies, waits for them, and re-layouts  11.9 us (3%)
    pallas_call x1, Pallas kernels, gradient_call(): pl.pallas_call(gradient_kernel, in_specs=[anywhere] * 3 + [inside] * 4 +...  201 us
    pallas_call x1, Pallas kernels, attention_call(): pl.pallas_call(attention_kernel, in_specs=[anywhere, inside, anywhere, in...  103 us
    pallas_call x1, Pallas kernels, mlp_call(): pl.pallas_call(functools.partial(mlp_kernel, ahead), grid=(hidden_units /...  46 us

profile of v9, /device:TPU:0, one launch (start us, length us, event | category | flops | bytes accessed | tf_op | source)
XLA Modules:
  0.0 396.0 jit_solution(15263502369468111388)
XLA Ops:
  0.6 0.7 constant_dynamic-slice_fusion
  4.6 1.3 broadcast_in_dim.12.gain_ref
  5.8 0.7 convert_element_type.20
  6.5 0.9 fusion.1
  8.0 4.2 %multiply_sine_fusion = (f32[768,384]{1,0:T(8,128)S(1)}, f32[768,384]{1,0:T(8,128)S(1)}) fusion(f32[384]{0:T(512)S(1)} %multiply_exponential_fusion, f32[768]{0:T(1024)S(1)} %convert_element_type.20), kind=kLoop, calls=%fused_computation.8 | loop fusion | flops 294912 | bytes 2363904 | tf_op jit(solution)/shard_map/sin | solution.py:35
  13.0 1.0 copy-done.5
  14.3 103.3 %attention.1 = (bf16[4,768,768]{2,1,0:T(8,128)(2,1)}, bf16[4,768,768]{2,1,0:T(8,128)(2,1)}, bf16[4,768,768]{2,1,0:T(8,128)(2,1)}, bf16[768,768]{1,0:T(8,128)(2,1...) custom-call(bf16[768,768]{1,0:T(8,128)(2,1)S(1)} %multiply_convert_fusion.refs_0_, ...), custom_call_target="tpu_custom_call" | custom-call | tf_op jit(solution)/shard_map/attention/pallas_call | solution.py:532
  117.6 1.0 copy-done.1
  118.6 1.0 copy-done.2
  119.6 0.6 copy-done.3
  120.2 46.0 %mlp.1 = (f32[768,768]{1,0:T(8,128)}, f32[768,768]{1,0:T(8,128)}, bf16[768,768]{1,0:T(8,128)(2,1)}, f32[6,2,768]{2,1,0:T(2,128)}, bf16[3072,768]{1,0:T(8,128)(2,...) custom-call(f32[768,768]{1,0:T(8,128)} %copy-done.5, ...), custom_call_target="tpu_custom_call" | custom-call | tf_op jit(solution)/shard_map/mlp/pallas_call | solution.py:742
  166.2 0.7 reduce
  167.0 0.7 pad_maximum_fusion
  167.7 0.6 pad.4.refs_15_
  168.3 201.2 %gradients.1 = (bf16[3072,768]{1,0:T(8,128)(2,1)}, bf16[768,3072]{1,0:T(8,128)(2,1)}, bf16[768,768]{1,0:T(8,128)(2,1)}, bf16[768,2304]{1,0:T(8,128)(2,1)}, f32[8,768]{1,0:T(8,128)}, /*index=5*/f32[768,768]{1,0:T(8,128)}) custom-call(bf16[4,768,768]{2,1,0:T(8,128)(2,1)} %get-tuple-element.37.refs_0_, bf16[4,768,768]{2,1,0:T(8,128)(2,1)} %get-tuple-element.38.refs_1_, ...), custom_call_target="tpu_custom_call" | custom-call | tf_op jit(solution)/shard_map/gradients/pallas_call | solution.py:1114
  369.5 3.3 multiply_reduce_fusion.2
  373.3 3.3 multiply_add_fusion
  376.6 0.6 slice_reduce_fusion
  377.2 0.6 reshape.68
  378.4 1.6 convert_element_type.23
  380.5 4.1 %convert_element_type.22 = f32[768,2304]{1,0:T(8,128)} convert(bf16[768,2304]{1,0:T(8,128)(2,1)S(1)} %copy-done.8) | non-fusion elementwise | flops 1769472 | bytes 10616832 | tf_op jit(solution)/shard_map/convert_element_type | solution.py:1201
  384.6 5.0 %convert_element_type.24 = f32[768,3072]{1,0:T(8,128)} convert(bf16[768,3072]{1,0:T(8,128)(2,1)S(1)} %bitcast.10) | non-fusion elementwise | flops 2359296 | bytes 14155776 | tf_op jit(solution)/shard_map/convert_element_type | solution.py:1204
  389.7 4.5 %convert_element_type.25 = f32[3072,768]{1,0:T(8,128)} convert(bf16[3072,768]{1,0:T(8,128)(2,1)S(1)} %bitcast.8) | non-fusion elementwise | flops 2359296 | bytes 14155776 | tf_op jit(solution)/shard_map/convert_element_type | solution.py:1206
  394.2 1.4 copy.24
  (49 shorter events, 3.9 us)
Async XLA Ops:
  7.5 6.8 %copy-start.4 = (s32[1,768]{1,0:T(1,128)}, s32[1,768]{1,0:T(1,128)S(1)}, u32[]{:S(2)}) copy-start(s32[1,768]{1,0:T(1,128)S(1)} %broadcast_in_dim.11.refs_3_.refs_8_) | copy-start | bytes 9220
  8.0 6.3 %copy-start = (s32[3072,1]{1,0:T(8,128)}, s32[3072,1]{1,0:T(8,128)S(1)}, u32[]{:S(2)}) copy-start(s32[3072,1]{1,0:T(8,128)S(1)} %copy.21.refs_2_.refs_7_) | copy-start | bytes 36868
  8.0 4.2 %copy-start.9 = (f32[768,768]{1,0:T(8,128)S(1)}, f32[768,768]{1,0:T(8,128)}, u32[]{:S(2)}) copy-start(f32[768,768]{1,0:T(8,128)} %param.12) | copy-start | bytes 7077892
  12.5 1.4 copy-start.5
  12.5 1.4 copy-start.12
  117.6 1.0 copy-start.1
  118.6 1.0 copy-start.2
  119.6 0.6 copy-start.3
  369.5 3.3 copy-start.6
  369.5 3.8 copy-start.7
  373.3 3.3 copy-start.13
  373.3 5.2 %copy-start.11 = (bf16[768,768]{1,0:T(8,128)(2,1)S(1)}, bf16[768,768]{1,0:T(8,128)(2,1)}, u32[]{:S(2)}) copy-start(bf16[768,768]{1,0:T(8,128)(2,1)} %get-tuple-element.54) | copy-start | bytes 3538948
  373.3 11.4 %slice-start.2 = ((s8[4718592]{0:T(1024)(128)(4,1)}), s8[524288]{0:T(1024)(128)(4,1)S(1)}, s32[]{:S(2)}) async-start(s8[4718592]{0:T(1024)(128)(4,1)} %bitcast.9), calls=%async_computation.2 | async-start | bytes 1048576
  377.8 2.7 copy-start.8
  378.4 6.2 %slice-start.3 = ((s8[4718592]{0:T(1024)(128)(4,1)}), s8[4194304]{0:T(1024)(128)(4,1)S(1)}, s32[]{:S(2)}) async-start(s8[4718592]{0:T(1024)(128)(4,1)} %bitcast.9), calls=%async_computation.3 | async-start | bytes 8388608
  380.5 9.2 %slice-start = ((s8[4718592]{0:T(1024)(128)(4,1)}), s8[4194304]{0:T(1024)(128)(4,1)S(1)}, s32[]{:S(2)}) async-start(s8[4718592]{0:T(1024)(128)(4,1)} %bitcast.7), calls=%async_computation | async-start | bytes 8388608
  384.6 5.0 %slice-start.1 = ((s8[4718592]{0:T(1024)(128)(4,1)}), s8[524288]{0:T(1024)(128)(4,1)S(1)}, s32[]{:S(2)}) async-start(s8[4718592]{0:T(1024)(128)(4,1)} %bitcast.7), calls=%async_computation.1 | async-start | bytes 1048576
  389.7 4.5 %copy-start.10 = (f32[768,768]{1,0:T(8,128)S(1)}, f32[768,768]{1,0:T(8,128)}, u32[]{:S(2)}) copy-start(f32[768,768]{1,0:T(8,128)} %get-tuple-element.85) | copy-start | bytes 7077892
